TPU v7x, 32 devices: a whole 2x2x4 slice. The times are simulated.
32 devices in a mesh: grp: 2 (over x), chol: 16 (over z, y, core).
Axes of the slice: x: 2, y: 2, z: 4, core: 2. Of those that a mesh axis runs over, the one named last changes fastest.
Arguments:
- chol_full: bfloat16 [128, 1024, 1024], P(None, 'chol'), may hold values from -0.015625 to 0.015625
- chol_half: bfloat16 [128, 1024, 256], P(None, 'chol'), may hold values from -0.046875 to 0.046875
- green: bfloat16 [128, 1024, 256], P('grp', 'chol'), parts along dimension 0, may hold values from -6 to 6
- gauss: float32 [128, 128], P('grp'), parts along dimension 0, may hold values from -5 to 5
- orbitals: bfloat16 [128, 1024, 256], P(('grp', 'chol')), parts along dimension 0, may hold values from -6 to 6
Outputs:
- new_orbitals: bfloat16 [128, 1024, 256], P(('grp', 'chol')), parts along dimension 0
- log_factor: float32 [128], P(('grp', 'chol')), parts along dimension 0
There are 2 independent parts, one for each index of `grp`. A program takes and returns all parts, laid end to end along the dimension named above; an argument that names none is the same for every part. Nothing has to cross between parts.
All inputs are finite; a program needn't handle non-finite values.
Results may differ from a plain program's by a relative error of at most 0.0032.
Values may be sent and summed in bfloat16 or wider, within the bound.
No kernel may reach another device: no remote copies, remote signals or barrier semaphores. Data moves between devices by JAX's collectives and lax.ppermute only.
A program may use at most 128 MiB of HBM per device.

v0:
```python
import jax
import jax.numpy as jnp
from jax import lax
from jax.sharding import PartitionSpec as P


def shift_terms(vbias, gauss_rows):
    xbar = jnp.clip(-0.3 * vbias, -1.0, 1.0)
    log_terms = jnp.sum(gauss_rows * xbar - 0.5 * xbar * xbar, axis=1)
    fields = (gauss_rows - xbar).astype(jnp.bfloat16)
    return (fields, log_terms)


def on_device(chol_full, chol_half, green, gauss, orbitals):
    walkers = green.shape[0]
    local_rows = green.shape[1]
    owned = orbitals.shape[0]
    vectors = chol_half.shape[0]
    partial_value = lax.dot_general(
        green.reshape(walkers, -1),
        chol_half.reshape(vectors, -1),
        (((1,), (1,)), ((), ())),
        preferred_element_type=jnp.float32,
    )
    first = lax.axis_index("chol") * owned
    vbias = lax.psum(partial_value, "chol")
    fields, log_terms = shift_terms(vbias, gauss)
    log_factor = lax.dynamic_slice_in_dim(log_terms, first, owned, 0)
    width = chol_full.shape[2]
    potential = jnp.dot(
        fields, chol_full.reshape(vectors, local_rows * width), preferred_element_type=jnp.float32
    )
    potential = (potential * 0.3).astype(jnp.bfloat16).reshape(walkers, local_rows, width)
    whole = lax.all_to_all(potential, "chol", split_axis=0, concat_axis=1, tiled=True)
    moved = jnp.einsum("wpq,wqk->wpk", whole, orbitals, preferred_element_type=jnp.float32)
    new_orbitals = (orbitals.astype(jnp.float32) + moved).astype(jnp.bfloat16)
    return (new_orbitals, log_factor)


def solution(mesh):
    placed = (
        P(None, "chol", None),
        P(None, "chol", None),
        P("grp", "chol", None),
        P("grp", None),
        P(("grp", "chol"), None, None),
    )
    return jax.shard_map(
        on_device,
        mesh=mesh,
        in_specs=placed,
        out_specs=(P(("grp", "chol"), None, None), P(("grp", "chol"))),
        check_vma=False,
    )
```

profile of v0, /device:TPU:15, one launch (start us, length us, event | category | flops | bytes accessed | tf_op | source)
XLA Modules:
  0.0 314.3 jit_solution(14263485968305415056)
XLA Ops:
  0.6 0.0 copy-start.1
  0.6 0.0 copy-start.2
  0.6 18.8 %copy.10 = bf16[16,8,64,1024]{3,1,2,0:T(8,128)(2,1)} copy(bf16[16,8,64,1024]{3,2,1,0:T(8,128)(2,1)} %bitcast.16) | data formatting | bytes 33554432
  19.5 0.0 copy-done.1
  19.5 0.0 copy-done.2
  19.5 0.0 copy-start
  19.5 6.7 %fusion.4 = f32[64,128]{1,0:T(8,128)S(1)} fusion(bf16[128,64,256]{2,1,0:T(8,128)(2,1)S(1)} %copy-done.1, bf16[64,64,256]{2,1,0:T(8,128)(2,1)S(1)} %copy-done.2), kind=kOutput, calls=%fused_computation.6 | convolution fusion | flops 268435456 | bytes 6324224 | tf_op jit(solution)/shard_map/dot_general | solution.py:19
  26.2 44.7 %psum.7 = f32[64,128]{1,0:T(8,128)S(1)} all-reduce(f32[64,128]{1,0:T(8,128)S(1)} %fusion.4), channel_id=1, replica_groups=mesh['grp'=2,'chol'=16] {'chol'}, use_global_device_ids=true, to_apply=%region_0.0 | all-reduce | flops 8192 | bytes 65536 | tf_op jit(solution)/shard_map/psum | solution.py:26
  70.8 0.0 copy-done
  70.8 11.8 %fusion = bf16[64,65536]{1,0:T(8,128)(2,1)} fusion(bf16[128,65536]{1,0:T(8,128)(2,1)} %bitcast.13, f32[64,128]{1,0:T(8,128)S(1)} %copy-done, f32[64,128]{1,0:T(8,128)S(1)} %psum.7), kind=kOutput, calls=%fused_computation.1 | convolution fusion | flops 1082163200 | bytes 25231360 | tf_op jit(solution)/shard_map/dot_general | solution.py:30
  82.6 11.6 %copy.11 = bf16[8,8,64,1024]{3,2,1,0:T(8,128)(2,1)} copy(bf16[8,8,64,1024]{3,1,2,0:T(8,128)(2,1)} %bitcast.14) | data formatting | bytes 16777216
  94.2 22.1 %all-to-all-start = ((bf16[64,64,1024]{2,1,0:T(8,128)(2,1)}), bf16[64,64,1024]{2,1,0:T(8,128)(2,1)}, u32[]{:S(2)}, u32[]{:S(2)}) async-start(bf16[64,64,1024]{2,1,0:T(8,128)(2,1)} %bitcast.15), calls=%async_computation | async-start | bytes 16777216 | tf_op jit(solution)/shard_map/all_to_all | solution.py:34
  116.3 0.1 fusion.10
  116.4 0.6 dynamic_slice.3
  117.0 181.7 %all-to-all-done = bf16[64,64,1024]{2,1,0:T(8,128)(2,1)} async-done(((bf16[64,64,1024]{2,1,0:T(8,128)(2,1)}), bf16[64,64,1024]{2,1,0:T(8,128)(2,1)}, u32[]{:S(2)}, u32[]{:S(2)}) %all-to-all-start) | async-done | bytes 8388640 | tf_op jit(solution)/shard_map/all_to_all | solution.py:34
  298.6 0.0 copy-start.3
  298.6 8.5 %copy.9 = bf16[16,4,64,1024]{3,2,0,1:T(8,128)(2,1)} copy(bf16[16,4,64,1024]{3,2,1,0:T(8,128)(2,1)} %bitcast.1) | data formatting | bytes 16777216 | tf_op jit(solution)/shard_map/all_to_all | solution.py:34
  307.2 0.0 copy-done.3
  307.2 7.1 %add_convert_fusion = bf16[4,1024,256]{2,1,0:T(8,128)(2,1)} fusion(bf16[4,1024,256]{2,1,0:T(8,128)(2,1)S(1)} %copy-done.3, bf16[4,1024,1024]{2,1,0:T(8,128)(2,1)} %bitcast.17), kind=kOutput, calls=%fused_computation.4 | convolution fusion | flops 2150629376 | bytes 12582912 | tf_op jit(solution)/shard_map/wpq,wqk->wpk/dot_general | solution.py:35
Async XLA Ops:
  0.6 18.8 %copy-start.1 = (bf16[128,64,256]{2,1,0:T(8,128)(2,1)S(1)}, bf16[128,64,256]{2,1,0:T(8,128)(2,1)}, u32[]{:S(2)}) copy-start(bf16[128,64,256]{2,1,0:T(8,128)(2,1)} %param.6) | copy-start | bytes 12582916
  0.6 18.8 %copy-start.2 = (bf16[64,64,256]{2,1,0:T(8,128)(2,1)S(1)}, bf16[64,64,256]{2,1,0:T(8,128)(2,1)}, u32[]{:S(2)}) copy-start(bf16[64,64,256]{2,1,0:T(8,128)(2,1)} %param.7) | copy-start | bytes 6291460
  19.5 51.4 %copy-start = (f32[64,128]{1,0:T(8,128)S(1)}, f32[64,128]{1,0:T(8,128)}, u32[]{:S(2)}) copy-start(f32[64,128]{1,0:T(8,128)} %param.8) | copy-start | bytes 98308
  94.2 204.4 %all-to-all-start = ((bf16[64,64,1024]{2,1,0:T(8,128)(2,1)}), bf16[64,64,1024]{2,1,0:T(8,128)(2,1)}, u32[]{:S(2)}, u32[]{:S(2)}) async-start(bf16[64,64,1024]{2,1,0:T(8,128)(2,1)} %bitcast.15), calls=%async_computation | async-start | bytes 16777216 | tf_op jit(solution)/shard_map/all_to_all | solution.py:34
  298.6 8.5 %copy-start.3 = (bf16[4,1024,256]{2,1,0:T(8,128)(2,1)S(1)}, bf16[4,1024,256]{2,1,0:T(8,128)(2,1)}, u32[]{:S(2)}) copy-start(bf16[4,1024,256]{2,1,0:T(8,128)(2,1)} %param.9) | copy-start | bytes 6291460
where the time goes:
time: 315 us; the launch traced here: 314 us
  waiting for transfers between devices  182 us (58%)
  blocking collectives  44.7 us (14%)
  local copies, waits for them, and re-layouts  39.6 us (13%)
  matrix products  25.5 us (8%)
  starting transfers between devices  22.1 us (7%)
    all_to_all x1, waiting for transfers between devices, on_device(): lax.all_to_all(potential, 'chol', split_axis=0, concat_axis=1, tiled=True)  182 us
    psum x1, blocking collectives, on_device(): vbias = lax.psum(partial_value, 'chol')  44.7 us
    unnamed x10, local copies, waits for them, and re-layouts  30.4 us
    all_to_all x1, starting transfers between devices, on_device(): lax.all_to_all(potential, 'chol', split_axis=0, concat_axis=1, tiled=True)  22.1 us
    dot_general x1, matrix products, on_device(): jnp.dot(fields, chol_full.reshape(vectors, local_rows * width), preferred...  11.8 us
    all_to_all x1, local copies, waits for them, and re-layouts, on_device(): lax.all_to_all(potential, 'chol', split_axis=0, concat_axis=1, tiled=True)  8.54 us
    dot_general x1, matrix products, on_device(): jnp.einsum('wpq,wqk->wpk', whole, orbitals, preferred_element_type=jnp.fl...  7.1 us
    dot_general x1, matrix products, on_device(): lax.dot_general(green.reshape(walkers, -1), chol_half.reshape(vectors, -1...  6.68 us
  transfers between devices with their start and end apart: 1, of which 1 were waited for; matrix products, arithmetic and copies ran while one was open for 0% of the time, Pallas kernels for 0%

commit v1 on v0

v1 whole, which is shorter than its diff:
```python
import functools

import jax
import jax.numpy as jnp
from jax import lax
from jax.experimental import pallas as pl
from jax.experimental.pallas import tpu as pltpu
from jax.sharding import PartitionSpec as P

PLANES = 4
TILE = 16
VMEM = 40 * 1024 * 1024


def shift_terms(vbias, gauss_rows):
    xbar = jnp.clip(-0.3 * vbias, -1.0, 1.0)
    log_terms = jnp.sum(gauss_rows * xbar - 0.5 * xbar * xbar, axis=1)
    fields = (gauss_rows - xbar).astype(jnp.bfloat16)
    return (fields, log_terms)


def butterfly_sum(value, size):
    step = 1
    while step < size:
        if 2 * step < size:
            one, two, three = (
                lax.ppermute(value, "chol", [(i, i ^ (k * step)) for i in range(size)]) for k in (1, 2, 3)
            )
            value = (value + one) + (two + three)
            step *= 4
        else:
            value = value + lax.ppermute(value, "chol", [(i, i ^ step) for i in range(size)])
            step *= 2
    return value


def potential_kernel(lanes, owned, fields_ref, chol_ref, *rest):
    outs, spread = rest[:lanes], rest[lanes]
    vectors, tile, width = chol_ref.shape

    @pl.when(pl.program_id(0) == 0)
    def _():
        shape = (vectors, vectors * tile)
        pick = lax.broadcasted_iota(jnp.int32, shape, 1) // tile == lax.broadcasted_iota(jnp.int32, shape, 0)
        wide = jnp.dot(fields_ref[...], pick.astype(jnp.bfloat16), preferred_element_type=jnp.float32)
        shape = (tile, vectors * tile)
        mine = lax.broadcasted_iota(jnp.int32, shape, 1) % tile == lax.broadcasted_iota(jnp.int32, shape, 0)
        for w in range(lanes * owned):
            rows = jnp.where(mine, jnp.broadcast_to(wide[w : w + 1], shape), 0.0)
            spread[w * tile : (w + 1) * tile, :] = rows.astype(jnp.bfloat16)

    total = jnp.dot(
        spread[...], chol_ref[...].reshape(vectors * tile, width), preferred_element_type=jnp.float32
    )
    value = (total * 0.3).astype(jnp.bfloat16).reshape(lanes, owned, tile, width)
    for k in range(lanes):
        outs[k][...] = value[k]


def potential_rows(fields, chol_full, lanes):
    vectors, rows, width = chol_full.shape
    walkers = fields.shape[0]
    owned = walkers // lanes
    return pl.pallas_call(
        functools.partial(potential_kernel, lanes, owned),
        grid=(rows // TILE,),
        in_specs=[
            pl.BlockSpec((walkers, vectors), lambda b: (0, 0)),
            pl.BlockSpec((vectors, TILE, width), lambda b: (0, b, 0)),
        ],
        out_specs=[pl.BlockSpec((owned, TILE, width), lambda b: (0, b, 0))] * lanes,
        out_shape=[jax.ShapeDtypeStruct((owned, rows, width), jnp.bfloat16)] * lanes,
        scratch_shapes=[pltpu.VMEM((walkers * TILE, vectors * TILE), jnp.bfloat16)],
        compiler_params=pltpu.CompilerParams(vmem_limit_bytes=VMEM),
        cost_estimate=pl.CostEstimate(
            flops=2 * walkers * TILE * vectors * rows * width,
            bytes_accessed=2 * (vectors + walkers) * rows * width,
            transcendentals=0,
        ),
    )(fields, chol_full)


def moved_kernel(lanes, choices, scalars, *refs):
    pieces, orbs, out = refs[:lanes], refs[lanes : lanes + choices], refs[lanes + choices]
    rows = pieces[0].shape[1]

    def orbital_rows(index):
        if choices == 1:
            return orbs[0][index]
        return jnp.where(scalars[0] == 0, orbs[0][index], orbs[1][index])

    left = jnp.concatenate([piece[0] for piece in pieces], axis=0)
    moved = jnp.dot(left, orbital_rows(0), preferred_element_type=jnp.float32)
    for k in range(lanes):
        lane = lax.rem(scalars[2] + (lanes - k), lanes)
        old = orbital_rows((0, pl.ds(pl.multiple_of((scalars[1] + lane) * rows, rows), rows)))
        new = old.astype(jnp.float32) + moved[k * rows : (k + 1) * rows]
        out[0, pl.ds(pl.multiple_of(lane * rows, rows), rows), :] = new.astype(jnp.bfloat16)


def moved_rows(pieces, orbs, scalars):
    lanes, choices = len(pieces), len(orbs)
    walkers, rows, width = pieces[0].shape
    occupied = orbs[0].shape[2]
    return pl.pallas_call(
        functools.partial(moved_kernel, lanes, choices),
        grid_spec=pltpu.PrefetchScalarGridSpec(
            num_scalar_prefetch=1,
            grid=(walkers,),
            in_specs=[pl.BlockSpec((1, rows, width), lambda w, s: (w, 0, 0))] * lanes
            + [pl.BlockSpec((1, width, occupied), lambda w, s: (w, 0, 0))] * choices,
            out_specs=pl.BlockSpec((1, lanes * rows, occupied), lambda w, s: (w, 0, 0)),
        ),
        out_shape=jax.ShapeDtypeStruct((walkers, lanes * rows, occupied), jnp.bfloat16),
        compiler_params=pltpu.CompilerParams(vmem_limit_bytes=VMEM),
        cost_estimate=pl.CostEstimate(
            flops=2 * walkers * lanes * rows * width * occupied,
            bytes_accessed=2 * walkers * (lanes * rows * (width + occupied) + choices * width * occupied),
            transcendentals=0,
        ),
    )(scalars, *pieces, *orbs)


def join_kernel(scalars, *refs):
    own, beside, sent, cross, mirror, out = refs
    rows = own.shape[1]

    def put(value, k):
        out[0, pl.ds(pl.multiple_of((scalars[1] ^ k) * rows, rows), rows), :] = value

    put(own[0], 0)
    put(jnp.where(scalars[0] == 0, beside[0], sent[0]), 1)
    put(cross[0], 2)
    put(mirror[0], 3)


def join_rows(scalars, blocks):
    walkers, rows, occupied = blocks[0].shape
    return pl.pallas_call(
        join_kernel,
        grid_spec=pltpu.PrefetchScalarGridSpec(
            num_scalar_prefetch=1,
            grid=(walkers,),
            in_specs=[pl.BlockSpec((1, rows, occupied), lambda w, s: (w, 0, 0))] * len(blocks),
            out_specs=pl.BlockSpec((1, PLANES * rows, occupied), lambda w, s: (w, 0, 0)),
        ),
        out_shape=jax.ShapeDtypeStruct((walkers, PLANES * rows, occupied), jnp.bfloat16),
        compiler_params=pltpu.CompilerParams(vmem_limit_bytes=VMEM),
    )(scalars, *blocks)


def on_device(size, chol_full, chol_half, green, gauss, orbitals):
    walkers = green.shape[0]
    owned = orbitals.shape[0]
    vectors = chol_half.shape[0]
    lanes = size // PLANES
    me = lax.axis_index("chol")
    plane, lane = me // lanes, me % lanes
    inner = ((plane == 1) | (plane == 2)).astype(jnp.int32)

    def along(targets):
        return [(a * lanes + k, b * lanes + k) for a, b in targets for k in range(lanes)]

    inward = along([(0, 1), (3, 2)])
    outward = along([(1, 0), (2, 3)])
    middle = along([(1, 2), (2, 1)])

    def send(arrays, targets):
        return [lax.ppermute(a, "chol", targets) for a in arrays]

    parts = 2
    share = owned // parts
    own = [orbitals[i * share : (i + 1) * share] for i in range(parts)]
    beside = send(own, inward)
    facing = send(own, middle)
    far = send(beside, middle)
    out_facing = send(facing, outward)
    out_far = send(far, outward)

    partial_value = lax.dot_general(
        green.reshape(walkers, -1),
        chol_half.reshape(vectors, -1),
        (((1,), (1,)), ((), ())),
        preferred_element_type=jnp.float32,
    )
    vbias = butterfly_sum(partial_value, size)
    fields, log_terms = shift_terms(vbias, gauss)
    log_factor = lax.dynamic_slice_in_dim(log_terms, me * owned, owned, 0)

    fields = fields.reshape(PLANES, lanes * owned, vectors)

    def pieces_of(slot):
        rows = lax.dynamic_index_in_dim(fields, plane ^ slot, 0, keepdims=False)
        rows = jnp.concatenate([rows, rows], axis=0)
        rows = lax.dynamic_slice_in_dim(rows, lane * owned, lanes * owned, 0)
        made = potential_rows(rows, chol_full, lanes)
        return [made[0]] + [
            lax.ppermute(
                made[k], "chol", [(p * lanes + j, p * lanes + (j + k) % lanes) for p in range(PLANES) for j in range(lanes)]
            )
            for k in range(1, lanes)
        ]

    pieces = {slot: pieces_of(slot) for slot in (1, 3, 2, 0)}
    sent = send(pieces[1], inward)

    def scalars(which, rows_of):
        return jnp.stack([which, rows_of * lanes, lane]).astype(jnp.int32)

    def halves(blocks, i):
        return [b[i * share : (i + 1) * share] for b in blocks]

    new = []
    for i in range(parts):
        mirror = moved_rows(halves(pieces[3], i), [out_far[i], facing[i]], scalars(inner, plane))
        cross = moved_rows(halves(pieces[2], i), [out_facing[i], far[i]], scalars(inner, plane))
        next_to = moved_rows(halves(pieces[1], i), [beside[i]], scalars(inner, plane))
        mirror = lax.ppermute(mirror, "chol", along([(0, 3), (3, 0), (1, 2), (2, 1)]))
        cross = lax.ppermute(cross, "chol", along([(0, 2), (2, 0), (1, 3), (3, 1)]))
        next_to = lax.ppermute(next_to, "chol", outward)
        home = moved_rows(halves(pieces[0], i), [own[i]], scalars(inner, plane))
        landed = moved_rows(halves(sent, i), [own[i]], scalars(inner, plane ^ 1))
        new.append(join_rows(jnp.stack([inner, plane]).astype(jnp.int32), [home, next_to, landed, cross, mirror]))
    return (jnp.concatenate(new, axis=0), log_factor)


def solution(mesh):
    placed = (
        P(None, "chol", None),
        P(None, "chol", None),
        P("grp", "chol", None),
        P("grp", None),
        P(("grp", "chol"), None, None),
    )
    return jax.shard_map(
        functools.partial(on_device, mesh.shape["chol"]),
        mesh=mesh,
        in_specs=placed,
        out_specs=(P(("grp", "chol"), None, None), P(("grp", "chol"))),
        check_vma=False,
    )
```

time: 315 us -> 277 us (0.88)
  Pallas kernels: 0 us -> 48.7 us
  blocking collectives: 44.7 us -> 0 us
  local copies, waits for them, and re-layouts: 39.6 us -> 3.01 us
  starting transfers between devices: 22.1 us -> 55.7 us
  waiting for transfers between devices: 182 us -> 155 us
  matrix products: 25.5 us -> 9.51 us
    all_to_all x1 -> x0, waiting for transfers between devices: 182 us -> none  [on_device(): lax.all_to_all(potential, 'chol', split_axis=0, concat_axis=1, tiled=True)]
    ppermute x0 -> x38, waiting for transfers between devices: none -> 155 us  [the longest x14 81.8 us: send(): return [lax.ppermute(a, 'chol', targets) for a in arrays]]
    ppermute x0 -> x38, starting transfers between devices: none -> 55.7 us  [the longest x14 27.8 us: send(): return [lax.ppermute(a, 'chol', targets) for a in arrays]]
    pallas_call x0 -> x16, Pallas kernels: none -> 48.7 us  [the longest x4 35.4 us: potential_rows(): pl.pallas_call(functools.partial(potential_kernel, lanes, owned), grid=(r...]
    psum x1 -> x0, blocking collectives: 44.7 us -> none  [on_device(): vbias = lax.psum(partial_value, 'chol')]
    unnamed x10 -> x2, local copies, waits for them, and re-layouts: 30.4 us -> 0.01 us
    all_to_all x1 -> x0, starting transfers between devices: 22.1 us -> none  [on_device(): lax.all_to_all(potential, 'chol', split_axis=0, concat_axis=1, tiled=True)]
    dot_general x2 -> x0, matrix products: 18.9 us -> none  [the longest x1 11.8 us: on_device(): jnp.dot(fields, chol_full.reshape(vectors, local_rows * width), preferred...]
  transfers between devices with their start and end apart: 1 -> 38, of which waited for: 1 -> 18; matrix products, arithmetic and copies ran while one was open for 0% -> 1% of each run, Pallas kernels for 0% -> 14%
where the time goes in v1:
time: 277 us; the launch traced here: 275 us
  waiting for transfers between devices  155 us (56%)
  starting transfers between devices  55.7 us (20%)
  Pallas kernels  48.7 us (18%)
  matrix products  9.51 us (3%)
  local copies, waits for them, and re-layouts  3.01 us (1%)
    ppermute x14, waiting for transfers between devices, send(): return [lax.ppermute(a, 'chol', targets) for a in arrays]  81.8 us
    ppermute x12, waiting for transfers between devices, pieces_of(): lax.ppermute(made[k], 'chol', [(p * lanes + j, p * lanes + (j + k) % lane...  44.1 us
    pallas_call x4, Pallas kernels, potential_rows(): pl.pallas_call(functools.partial(potential_kernel, lanes, owned), grid=(r...  35.4 us
    ppermute x14, starting transfers between devices, send(): return [lax.ppermute(a, 'chol', targets) for a in arrays]  27.8 us
    ppermute x2, waiting for transfers between devices, on_device(): lax.ppermute(mirror, 'chol', along([(0, 3), (3, 0), (1, 2), (2, 1)]))  25.6 us
    pallas_call x10, Pallas kernels, moved_rows(): pl.pallas_call(functools.partial(moved_kernel, lanes, choices), grid_spec...  12 us
    ppermute x12, starting transfers between devices, pieces_of(): lax.ppermute(made[k], 'chol', [(p * lanes + j, p * lanes + (j + k) % lane...  11.7 us
    dot_general x1, matrix products, on_device(): lax.dot_general(green.reshape(walkers, -1), chol_half.reshape(vectors, -1...  9.51 us
  transfers between devices with their start and end apart: 38, of which 18 were waited for; matrix products, arithmetic and copies ran while one was open for 1% of the time, Pallas kernels for 14%

profile of v1, /device:TPU:15, one launch (start us, length us, event | category | flops | bytes accessed | tf_op | source)
XLA Modules:
  0.0 275.3 jit_solution(7956307393109152583)
XLA Ops:
  0.6 9.5 %fusion.3 = f32[64,128]{1,0:T(8,128)S(1)} fusion(bf16[128,64,256]{2,1,0:T(8,128)(2,1)} %param.6, bf16[64,64,256]{2,1,0:T(8,128)(2,1)} %param.7), kind=kOutput, calls=%fused_computation.4 | convolution fusion | flops 268435456 | bytes 6324224 | tf_op jit(solution)/shard_map/dot_general | solution.py:180
  10.4 2.1 collective-permute-start.2
  12.5 1.7 fusion.14
  14.8 2.4 collective-permute-start.4
  20.3 8.8 %shard_map.68 = (bf16[4,64,1024]{2,1,0:T(8,128)(2,1)S(1)}, bf16[4,64,1024]{2,1,0:T(8,128)(2,1)S(1)}, bf16[4,64,1024]{2,1,0:T(8,128)(2,1)S(1)}, bf16[4,64,1024]{2,1,0:T(8,128)(2,1)S(1)}) custom-call(bf16[16,128]{1,0:T(8,128)(2,1)S(1)} %get-tuple-element.85.fields_ref, bf16[128,64,1024]{2,1,0:T(8,128)(2,1)} %chol_ref.7), custom_call_target="tpu_custom_call" | custom-call | flops 4294967296 | bytes 18874368 | tf_op jit(solution)/shard_map/pallas_call | solution.py:64
  29.2 2.6 collective-permute-start.6
  32.3 8.8 %shard_map.70 = (bf16[4,64,1024]{2,1,0:T(8,128)(2,1)S(1)}, bf16[4,64,1024]{2,1,0:T(8,128)(2,1)S(1)}, bf16[4,64,1024]{2,1,0:T(8,128)(2,1)S(1)}, bf16[4,64,1024]{2,1,0:T(8,128)(2,1)S(1)}) custom-call(bf16[16,128]{1,0:T(8,128)(2,1)S(1)} %get-tuple-element.84.fields_ref, bf16[128,64,1024]{2,1,0:T(8,128)(2,1)} %chol_ref.7), custom_call_target="tpu_custom_call" | custom-call | flops 4294967296 | bytes 18874368 | tf_op jit(solution)/shard_map/pallas_call | solution.py:64
  41.2 2.0 collective-permute-start.9
  43.2 8.8 %shard_map.73 = (bf16[4,64,1024]{2,1,0:T(8,128)(2,1)S(1)}, bf16[4,64,1024]{2,1,0:T(8,128)(2,1)S(1)}, bf16[4,64,1024]{2,1,0:T(8,128)(2,1)S(1)}, bf16[4,64,1024]{2,1,0:T(8,128)(2,1)S(1)}) custom-call(bf16[16,128]{1,0:T(8,128)(2,1)S(1)} %get-tuple-element.83.fields_ref, bf16[128,64,1024]{2,1,0:T(8,128)(2,1)} %chol_ref.7), custom_call_target="tpu_custom_call" | custom-call | flops 4294967296 | bytes 18874368 | tf_op jit(solution)/shard_map/pallas_call | solution.py:64
  52.0 8.8 %shard_map.75 = (bf16[4,64,1024]{2,1,0:T(8,128)(2,1)S(1)}, bf16[4,64,1024]{2,1,0:T(8,128)(2,1)S(1)}, bf16[4,64,1024]{2,1,0:T(8,128)(2,1)S(1)}, bf16[4,64,1024]{2,1,0:T(8,128)(2,1)S(1)}) custom-call(bf16[16,128]{1,0:T(8,128)(2,1)S(1)} %get-tuple-element.82.fields_ref, bf16[128,64,1024]{2,1,0:T(8,128)(2,1)} %chol_ref.7), custom_call_target="tpu_custom_call" | custom-call | flops 4294967296 | bytes 18874368 | tf_op jit(solution)/shard_map/pallas_call | solution.py:64
  64.0 1.7 collective-permute-start.18
  66.2 8.6 %collective-permute-done.10 = bf16[4,64,1024]{2,1,0:T(8,128)(2,1)S(1)} collective-permute-done((bf16[4,64,1024]{2,1,0:T(8,128)(2,1)S(1)}, bf16[4,64,1024]{2,1,0:T(8,128)(2,1)S(1)}, u32[]{:S(2)}, u32[]{:S(2)}) %collective-permute-start.10) | collective-permute-done | bytes 524320 | tf_op jit(solution)/shard_map/ppermute | solution.py:198
  76.1 10.2 %collective-permute-done.11 = bf16[4,64,1024]{2,1,0:T(8,128)(2,1)S(1)} collective-permute-done((bf16[4,64,1024]{2,1,0:T(8,128)(2,1)S(1)}, bf16[4,64,1024]{2,1,0:T(8,128)(2,1)S(1)}, u32[]{:S(2)}, u32[]{:S(2)}) %collective-permute-start.11) | collective-permute-done | bytes 524320 | tf_op jit(solution)/shard_map/ppermute | solution.py:198
  87.7 1.8 collective-permute-start.25
  89.5 7.8 %collective-permute-done.19 = bf16[4,64,1024]{2,1,0:T(8,128)(2,1)S(1)} collective-permute-done((bf16[4,64,1024]{2,1,0:T(8,128)(2,1)S(1)}, bf16[4,64,1024]{2,1,0:T(8,128)(2,1)S(1)}, u32[]{:S(2)}, u32[]{:S(2)}) %collective-permute-start.19) | collective-permute-done | bytes 524320 | tf_op jit(solution)/shard_map/ppermute | solution.py:198
  98.4 10.4 %collective-permute-done.20 = bf16[4,64,1024]{2,1,0:T(8,128)(2,1)S(1)} collective-permute-done((bf16[4,64,1024]{2,1,0:T(8,128)(2,1)S(1)}, bf16[4,64,1024]{2,1,0:T(8,128)(2,1)S(1)}, u32[]{:S(2)}, u32[]{:S(2)}) %collective-permute-start.20) | collective-permute-done | bytes 524320 | tf_op jit(solution)/shard_map/ppermute | solution.py:198
  108.7 3.5 %collective-permute-start.32 = (bf16[2,1024,256]{2,1,0:T(8,128)(2,1)S(1)}, bf16[2,1024,256]{2,1,0:T(8,128)(2,1)S(1)}, u32[]{:S(2)}, u32[]{:S(2)}) collective-permute-start(bf16[2,1024,256]{2,1,0:T(8,128)(2,1)S(1)} %get-tuple-element.37.refs_4_), channel_id=1, source_target_pairs={{4,8},{5,9},{6,10},{7,11},{8,4},{9,5},{10,6},{11,7},{20,24},{21,25... | collective-permute-start | bytes 3145736 | tf_op jit(solution)/shard_map/ppermute | solution.py:169
  112.3 1.9 collective-permute-start.21
  114.3 5.5 %collective-permute-done.26 = bf16[4,64,1024]{2,1,0:T(8,128)(2,1)S(1)} collective-permute-done((bf16[4,64,1024]{2,1,0:T(8,128)(2,1)S(1)}, bf16[4,64,1024]{2,1,0:T(8,128)(2,1)S(1)}, u32[]{:S(2)}, u32[]{:S(2)}) %collective-permute-start.26) | collective-permute-done | bytes 524320 | tf_op jit(solution)/shard_map/ppermute | solution.py:198
  120.3 3.5 %collective-permute-start.34 = (bf16[2,1024,256]{2,1,0:T(8,128)(2,1)S(1)}, bf16[2,1024,256]{2,1,0:T(8,128)(2,1)S(1)}, u32[]{:S(2)}, u32[]{:S(2)}) collective-permute-start(bf16[2,1024,256]{2,1,0:T(8,128)(2,1)S(1)} %collective-permute-done.30.refs_4_), channel_id=1, source_target_pairs={{4,8},{5,9},{6,10},{7,11},{8,4},{9,5},{10,6},{11,7},{20,24},{21,25... | collective-permute-start | bytes 3145736 | tf_op jit(solution)/shard_map/ppermute | solution.py:169
  123.8 3.0 %collective-permute-start.23 = (bf16[2,1024,256]{2,1,0:T(8,128)(2,1)S(1)}, bf16[2,1024,256]{2,1,0:T(8,128)(2,1)S(1)}, u32[]{:S(2)}, u32[]{:S(2)}) collective-permute-start(bf16[2,1024,256]{2,1,0:T(8,128)(2,1)S(1)} %collective-permute-done.12.refs_4_), channel_id=1, source_target_pairs={{4,8},{5,9},{6,10},{7,11},{8,4},{9,5},{10,6},{11,7},{20,24},{21,25... | collective-permute-start | bytes 3145736 | tf_op jit(solution)/shard_map/ppermute | solution.py:169
  127.0 1.7 collective-permute-done.27
  131.2 4.8 %collective-permute-done.32.refs_5_ = bf16[2,1024,256]{2,1,0:T(8,128)(2,1)S(1)} collective-permute-done((bf16[2,1024,256]{2,1,0:T(8,128)(2,1)S(1)}, bf16[2,1024,256]{2,1,0:T(8,128)(2,1)S(1)}, u32[]{:S(2)}, u32[]{:S(2)}) %collective-permute-start.32) | collective-permute-done | bytes 1048608 | tf_op jit(solution)/shard_map/ppermute | solution.py:169
  138.6 19.9 %collective-permute-done.21.refs_5_ = bf16[2,1024,256]{2,1,0:T(8,128)(2,1)S(1)} collective-permute-done((bf16[2,1024,256]{2,1,0:T(8,128)(2,1)S(1)}, bf16[2,1024,256]{2,1,0:T(8,128)(2,1)S(1)}, u32[]{:S(2)}, u32[]{:S(2)}) %collective-permute-start.21) | collective-permute-done | bytes 1048608 | tf_op jit(solution)/shard_map/ppermute | solution.py:169
  159.8 4.1 %collective-permute-start.22 = (bf16[2,1024,256]{2,1,0:T(8,128)(2,1)S(1)}, bf16[2,1024,256]{2,1,0:T(8,128)(2,1)S(1)}, u32[]{:S(2)}, u32[]{:S(2)}) collective-permute-start(bf16[2,1024,256]{2,1,0:T(8,128)(2,1)S(1)} %collective-permute-done.21.refs_5_), channel_id=1, source_target_pairs={{4,0},{5,1},{6,2},{7,3},{8,12},{9,13},{10,14},{11,15},{20,16},{21,... | collective-permute-start | bytes 3145736 | tf_op jit(solution)/shard_map/ppermute | solution.py:169
  163.9 17.1 %collective-permute-done.34.refs_5_ = bf16[2,1024,256]{2,1,0:T(8,128)(2,1)S(1)} collective-permute-done((bf16[2,1024,256]{2,1,0:T(8,128)(2,1)S(1)}, bf16[2,1024,256]{2,1,0:T(8,128)(2,1)S(1)}, u32[]{:S(2)}, u32[]{:S(2)}) %collective-permute-start.34) | collective-permute-done | bytes 1048608 | tf_op jit(solution)/shard_map/ppermute | solution.py:169
  182.3 19.5 %collective-permute-done.23.refs_5_ = bf16[2,1024,256]{2,1,0:T(8,128)(2,1)S(1)} collective-permute-done((bf16[2,1024,256]{2,1,0:T(8,128)(2,1)S(1)}, bf16[2,1024,256]{2,1,0:T(8,128)(2,1)S(1)}, u32[]{:S(2)}, u32[]{:S(2)}) %collective-permute-start.23) | collective-permute-done | bytes 1048608 | tf_op jit(solution)/shard_map/ppermute | solution.py:169
  207.0 4.0 %collective-permute-start.31 = (bf16[2,256,256]{2,1,0:T(8,128)(2,1)S(1)}, bf16[2,256,256]{2,1,0:T(8,128)(2,1)S(1)}, u32[]{:S(2)}, u32[]{:S(2)}) collective-permute-start(bf16[2,256,256]{2,1,0:T(8,128)(2,1)S(1)} %shard_map.79), channel_id=1, source_target_pairs={{4,0},{5,1},{6,2},{7,3},{8,12},{9,13},{10,14},{11,15},{20,16},{21,... | collective-permute-start | bytes 786440 | tf_op jit(solution)/shard_map/ppermute | solution.py:220
  216.8 20.6 %collective-permute-done.28.refs_4_ = bf16[2,1024,256]{2,1,0:T(8,128)(2,1)S(1)} collective-permute-done((bf16[2,1024,256]{2,1,0:T(8,128)(2,1)S(1)}, bf16[2,1024,256]{2,1,0:T(8,128)(2,1)S(1)}, u32[]{:S(2)}, u32[]{:S(2)}) %collective-permute-start.28) | collective-permute-done | bytes 1048608 | tf_op jit(solution)/shard_map/ppermute | solution.py:169
  237.4 3.3 %collective-permute-start.24 = (bf16[2,256,256]{2,1,0:T(8,128)(2,1)S(1)}, bf16[2,256,256]{2,1,0:T(8,128)(2,1)S(1)}, u32[]{:S(2)}, u32[]{:S(2)}) collective-permute-start(bf16[2,256,256]{2,1,0:T(8,128)(2,1)S(1)} %shard_map.74), channel_id=1, source_target_pairs={{0,8},{1,9},{2,10},{3,11},{8,0},{9,1},{10,2},{11,3},{4,12},{5,13},... | collective-permute-start | bytes 786440 | tf_op jit(solution)/shard_map/ppermute | solution.py:219
  246.8 21.7 %collective-permute-done.37.refs_4_ = bf16[2,256,256]{2,1,0:T(8,128)(2,1)S(1)} collective-permute-done((bf16[2,256,256]{2,1,0:T(8,128)(2,1)S(1)}, bf16[2,256,256]{2,1,0:T(8,128)(2,1)S(1)}, u32[]{:S(2)}, u32[]{:S(2)}) %collective-permute-start.37) | collective-permute-done | bytes 262176 | tf_op jit(solution)/shard_map/ppermute | solution.py:218
  269.2 3.9 %collective-permute-done.29.refs_4_ = bf16[2,256,256]{2,1,0:T(8,128)(2,1)S(1)} collective-permute-done((bf16[2,256,256]{2,1,0:T(8,128)(2,1)S(1)}, bf16[2,256,256]{2,1,0:T(8,128)(2,1)S(1)}, u32[]{:S(2)}, u32[]{:S(2)}) %collective-permute-start.29) | collective-permute-done | bytes 262176 | tf_op jit(solution)/shard_map/ppermute | solution.py:218
  (95 shorter events, 40.0 us)
Async XLA Ops:
  29.2 32.7 %collective-permute-start.6 = (bf16[4,64,1024]{2,1,0:T(8,128)(2,1)S(1)}, bf16[4,64,1024]{2,1,0:T(8,128)(2,1)S(1)}, u32[]{:S(2)}, u32[]{:S(2)}) collective-permute-start(bf16[4,64,1024]{2,1,0:T(8,128)(2,1)S(1)} %get-tuple-element.19), channel_id=1, source_target_pairs={{0,1},{1,2},{2,3},{3,0},{4,5},{5,6},{6,7},{7,4},{8,9},{9,10},{10,1... | collective-permute-start | bytes 1572872 | tf_op jit(solution)/shard_map/ppermute | solution.py:198
  31.8 30.2 %collective-permute-start.7 = (bf16[4,64,1024]{2,1,0:T(8,128)(2,1)S(1)}, bf16[4,64,1024]{2,1,0:T(8,128)(2,1)S(1)}, u32[]{:S(2)}, u32[]{:S(2)}) collective-permute-start(bf16[4,64,1024]{2,1,0:T(8,128)(2,1)S(1)} %get-tuple-element.20), channel_id=1, source_target_pairs={{0,2},{1,3},{2,0},{3,1},{4,6},{5,7},{6,4},{7,5},{8,10},{9,11},{10,... | collective-permute-start | bytes 1572872 | tf_op jit(solution)/shard_map/ppermute | solution.py:198
  32.3 31.6 %collective-permute-start.8 = (bf16[4,64,1024]{2,1,0:T(8,128)(2,1)S(1)}, bf16[4,64,1024]{2,1,0:T(8,128)(2,1)S(1)}, u32[]{:S(2)}, u32[]{:S(2)}) collective-permute-start(bf16[4,64,1024]{2,1,0:T(8,128)(2,1)S(1)} %get-tuple-element.21), channel_id=1, source_target_pairs={{0,3},{1,0},{2,1},{3,2},{4,7},{5,4},{6,5},{7,6},{8,11},{9,8},{10,9... | collective-permute-start | bytes 1572872 | tf_op jit(solution)/shard_map/ppermute | solution.py:198
  41.2 24.5 %collective-permute-start.9 = (bf16[4,64,1024]{2,1,0:T(8,128)(2,1)S(1)}, bf16[4,64,1024]{2,1,0:T(8,128)(2,1)S(1)}, u32[]{:S(2)}, u32[]{:S(2)}) collective-permute-start(bf16[4,64,1024]{2,1,0:T(8,128)(2,1)S(1)} %get-tuple-element.23), channel_id=1, source_target_pairs={{0,1},{1,2},{2,3},{3,0},{4,5},{5,6},{6,7},{7,4},{8,9},{9,10},{10,1... | collective-permute-start | bytes 1572872 | tf_op jit(solution)/shard_map/ppermute | solution.py:198
  60.9 13.9 %collective-permute-start.10 = (bf16[4,64,1024]{2,1,0:T(8,128)(2,1)S(1)}, bf16[4,64,1024]{2,1,0:T(8,128)(2,1)S(1)}, u32[]{:S(2)}, u32[]{:S(2)}) collective-permute-start(bf16[4,64,1024]{2,1,0:T(8,128)(2,1)S(1)} %get-tuple-element.24), channel_id=1, source_target_pairs={{0,2},{1,3},{2,0},{3,1},{4,6},{5,7},{6,4},{7,5},{8,10},{9,11},{10,... | collective-permute-start | bytes 1572872 | tf_op jit(solution)/shard_map/ppermute | solution.py:198
  62.0 24.3 %collective-permute-start.11 = (bf16[4,64,1024]{2,1,0:T(8,128)(2,1)S(1)}, bf16[4,64,1024]{2,1,0:T(8,128)(2,1)S(1)}, u32[]{:S(2)}, u32[]{:S(2)}) collective-permute-start(bf16[4,64,1024]{2,1,0:T(8,128)(2,1)S(1)} %get-tuple-element.25), channel_id=1, source_target_pairs={{0,3},{1,0},{2,1},{3,2},{4,7},{5,4},{6,5},{7,6},{8,11},{9,8},{10,9... | collective-permute-start | bytes 1572872 | tf_op jit(solution)/shard_map/ppermute | solution.py:198
  62.0 25.6 %collective-permute-start.14 = (bf16[4,64,1024]{2,1,0:T(8,128)(2,1)S(1)}, bf16[4,64,1024]{2,1,0:T(8,128)(2,1)S(1)}, u32[]{:S(2)}, u32[]{:S(2)}) collective-permute-start(bf16[4,64,1024]{2,1,0:T(8,128)(2,1)S(1)} %get-tuple-element.22), channel_id=1, source_target_pairs={{0,4},{1,5},{2,6},{3,7},{12,8},{13,9},{14,10},{15,11},{16,20},{17,... | collective-permute-start | bytes 1572872 | tf_op jit(solution)/shard_map/ppermute | solution.py:169
  64.0 23.8 %collective-permute-start.18 = (bf16[4,64,1024]{2,1,0:T(8,128)(2,1)S(1)}, bf16[4,64,1024]{2,1,0:T(8,128)(2,1)S(1)}, u32[]{:S(2)}, u32[]{:S(2)}) collective-permute-start(bf16[4,64,1024]{2,1,0:T(8,128)(2,1)S(1)} %get-tuple-element.27), channel_id=1, source_target_pairs={{0,1},{1,2},{2,3},{3,0},{4,5},{5,6},{6,7},{7,4},{8,9},{9,10},{10,1... | collective-permute-start | bytes 1572872 | tf_op jit(solution)/shard_map/ppermute | solution.py:198
  65.7 31.6 %collective-permute-start.19 = (bf16[4,64,1024]{2,1,0:T(8,128)(2,1)S(1)}, bf16[4,64,1024]{2,1,0:T(8,128)(2,1)S(1)}, u32[]{:S(2)}, u32[]{:S(2)}) collective-permute-start(bf16[4,64,1024]{2,1,0:T(8,128)(2,1)S(1)} %get-tuple-element.28), channel_id=1, source_target_pairs={{0,2},{1,3},{2,0},{3,1},{4,6},{5,7},{6,4},{7,5},{8,10},{9,11},{10,... | collective-permute-start | bytes 1572872 | tf_op jit(solution)/shard_map/ppermute | solution.py:198
  74.8 45.4 %collective-permute-start.30 = (bf16[2,1024,256]{2,1,0:T(8,128)(2,1)S(1)}, bf16[2,1024,256]{2,1,0:T(8,128)(2,1)S(1)}, u32[]{:S(2)}, u32[]{:S(2)}) collective-permute-start(bf16[2,1024,256]{2,1,0:T(8,128)(2,1)S(1)} %get-tuple-element.37.refs_4_), channel_id=1, source_target_pairs={{0,4},{1,5},{2,6},{3,7},{12,8},{13,9},{14,10},{15,11},{16,20},{17,... | collective-permute-start | bytes 3145736 | tf_op jit(solution)/shard_map/ppermute | solution.py:169
  86.3 37.5 %collective-permute-start.12 = (bf16[2,1024,256]{2,1,0:T(8,128)(2,1)S(1)}, bf16[2,1024,256]{2,1,0:T(8,128)(2,1)S(1)}, u32[]{:S(2)}, u32[]{:S(2)}) collective-permute-start(bf16[2,1024,256]{2,1,0:T(8,128)(2,1)S(1)} %get-tuple-element.36.refs_4_), channel_id=1, source_target_pairs={{0,4},{1,5},{2,6},{3,7},{12,8},{13,9},{14,10},{15,11},{16,20},{17,... | collective-permute-start | bytes 3145736 | tf_op jit(solution)/shard_map/ppermute | solution.py:169
  87.6 21.1 %collective-permute-start.20 = (bf16[4,64,1024]{2,1,0:T(8,128)(2,1)S(1)}, bf16[4,64,1024]{2,1,0:T(8,128)(2,1)S(1)}, u32[]{:S(2)}, u32[]{:S(2)}) collective-permute-start(bf16[4,64,1024]{2,1,0:T(8,128)(2,1)S(1)} %get-tuple-element.29), channel_id=1, source_target_pairs={{0,3},{1,0},{2,1},{3,2},{4,7},{5,4},{6,5},{7,6},{8,11},{9,8},{10,9... | collective-permute-start | bytes 1572872 | tf_op jit(solution)/shard_map/ppermute | solution.py:198
  87.7 24.6 %collective-permute-start.25 = (bf16[4,64,1024]{2,1,0:T(8,128)(2,1)S(1)}, bf16[4,64,1024]{2,1,0:T(8,128)(2,1)S(1)}, u32[]{:S(2)}, u32[]{:S(2)}) collective-permute-start(bf16[4,64,1024]{2,1,0:T(8,128)(2,1)S(1)} %get-tuple-element.31), channel_id=1, source_target_pairs={{0,1},{1,2},{2,3},{3,0},{4,5},{5,6},{6,7},{7,4},{8,9},{9,10},{10,1... | collective-permute-start | bytes 1572872 | tf_op jit(solution)/shard_map/ppermute | solution.py:198
  97.3 22.5 %collective-permute-start.26 = (bf16[4,64,1024]{2,1,0:T(8,128)(2,1)S(1)}, bf16[4,64,1024]{2,1,0:T(8,128)(2,1)S(1)}, u32[]{:S(2)}, u32[]{:S(2)}) collective-permute-start(bf16[4,64,1024]{2,1,0:T(8,128)(2,1)S(1)} %get-tuple-element.32), channel_id=1, source_target_pairs={{0,2},{1,3},{2,0},{3,1},{4,6},{5,7},{6,4},{7,5},{8,10},{9,11},{10,... | collective-permute-start | bytes 1572872 | tf_op jit(solution)/shard_map/ppermute | solution.py:198
  108.7 27.3 %collective-permute-start.32 = (bf16[2,1024,256]{2,1,0:T(8,128)(2,1)S(1)}, bf16[2,1024,256]{2,1,0:T(8,128)(2,1)S(1)}, u32[]{:S(2)}, u32[]{:S(2)}) collective-permute-start(bf16[2,1024,256]{2,1,0:T(8,128)(2,1)S(1)} %get-tuple-element.37.refs_4_), channel_id=1, source_target_pairs={{4,8},{5,9},{6,10},{7,11},{8,4},{9,5},{10,6},{11,7},{20,24},{21,25... | collective-permute-start | bytes 3145736 | tf_op jit(solution)/shard_map/ppermute | solution.py:169
  112.3 46.2 %collective-permute-start.21 = (bf16[2,1024,256]{2,1,0:T(8,128)(2,1)S(1)}, bf16[2,1024,256]{2,1,0:T(8,128)(2,1)S(1)}, u32[]{:S(2)}, u32[]{:S(2)}) collective-permute-start(bf16[2,1024,256]{2,1,0:T(8,128)(2,1)S(1)} %get-tuple-element.36.refs_4_), channel_id=1, source_target_pairs={{4,8},{5,9},{6,10},{7,11},{8,4},{9,5},{10,6},{11,7},{20,24},{21,25... | collective-permute-start | bytes 3145736 | tf_op jit(solution)/shard_map/ppermute | solution.py:169
  119.8 8.9 %collective-permute-start.27 = (bf16[4,64,1024]{2,1,0:T(8,128)(2,1)S(1)}, bf16[4,64,1024]{2,1,0:T(8,128)(2,1)S(1)}, u32[]{:S(2)}, u32[]{:S(2)}) collective-permute-start(bf16[4,64,1024]{2,1,0:T(8,128)(2,1)S(1)} %get-tuple-element.33), channel_id=1, source_target_pairs={{0,3},{1,0},{2,1},{3,2},{4,7},{5,4},{6,5},{7,6},{8,11},{9,8},{10,9... | collective-permute-start | bytes 1572872 | tf_op jit(solution)/shard_map/ppermute | solution.py:198
  120.3 60.7 %collective-permute-start.34 = (bf16[2,1024,256]{2,1,0:T(8,128)(2,1)S(1)}, bf16[2,1024,256]{2,1,0:T(8,128)(2,1)S(1)}, u32[]{:S(2)}, u32[]{:S(2)}) collective-permute-start(bf16[2,1024,256]{2,1,0:T(8,128)(2,1)S(1)} %collective-permute-done.30.refs_4_), channel_id=1, source_target_pairs={{4,8},{5,9},{6,10},{7,11},{8,4},{9,5},{10,6},{11,7},{20,24},{21,25... | collective-permute-start | bytes 3145736 | tf_op jit(solution)/shard_map/ppermute | solution.py:169
  123.8 78.0 %collective-permute-start.23 = (bf16[2,1024,256]{2,1,0:T(8,128)(2,1)S(1)}, bf16[2,1024,256]{2,1,0:T(8,128)(2,1)S(1)}, u32[]{:S(2)}, u32[]{:S(2)}) collective-permute-start(bf16[2,1024,256]{2,1,0:T(8,128)(2,1)S(1)} %collective-permute-done.12.refs_4_), channel_id=1, source_target_pairs={{4,8},{5,9},{6,10},{7,11},{8,4},{9,5},{10,6},{11,7},{20,24},{21,25... | collective-permute-start | bytes 3145736 | tf_op jit(solution)/shard_map/ppermute | solution.py:169
  128.7 31.1 %collective-permute-start.15 = (bf16[4,64,1024]{2,1,0:T(8,128)(2,1)S(1)}, bf16[4,64,1024]{2,1,0:T(8,128)(2,1)S(1)}, u32[]{:S(2)}, u32[]{:S(2)}) collective-permute-start(bf16[4,64,1024]{2,1,0:T(8,128)(2,1)S(1)} %collective-permute-done.9), channel_id=1, source_target_pairs={{0,4},{1,5},{2,6},{3,7},{12,8},{13,9},{14,10},{15,11},{16,20},{17,... | collective-permute-start | bytes 1572872 | tf_op jit(solution)/shard_map/ppermute | solution.py:169
  136.0 71.0 %collective-permute-start.33 = (bf16[2,1024,256]{2,1,0:T(8,128)(2,1)S(1)}, bf16[2,1024,256]{2,1,0:T(8,128)(2,1)S(1)}, u32[]{:S(2)}, u32[]{:S(2)}) collective-permute-start(bf16[2,1024,256]{2,1,0:T(8,128)(2,1)S(1)} %collective-permute-done.32.refs_5_), channel_id=1, source_target_pairs={{4,0},{5,1},{6,2},{7,3},{8,12},{9,13},{10,14},{11,15},{20,16},{21,... | collective-permute-start | bytes 3145736 | tf_op jit(solution)/shard_map/ppermute | solution.py:169
  158.5 47.2 %collective-permute-start.16 = (bf16[4,64,1024]{2,1,0:T(8,128)(2,1)S(1)}, bf16[4,64,1024]{2,1,0:T(8,128)(2,1)S(1)}, u32[]{:S(2)}, u32[]{:S(2)}) collective-permute-start(bf16[4,64,1024]{2,1,0:T(8,128)(2,1)S(1)} %collective-permute-done.10), channel_id=1, source_target_pairs={{0,4},{1,5},{2,6},{3,7},{12,8},{13,9},{14,10},{15,11},{16,20},{17,... | collective-permute-start | bytes 1572872 | tf_op jit(solution)/shard_map/ppermute | solution.py:169
  159.8 52.5 %collective-permute-start.22 = (bf16[2,1024,256]{2,1,0:T(8,128)(2,1)S(1)}, bf16[2,1024,256]{2,1,0:T(8,128)(2,1)S(1)}, u32[]{:S(2)}, u32[]{:S(2)}) collective-permute-start(bf16[2,1024,256]{2,1,0:T(8,128)(2,1)S(1)} %collective-permute-done.21.refs_5_), channel_id=1, source_target_pairs={{4,0},{5,1},{6,2},{7,3},{8,12},{9,13},{10,14},{11,15},{20,16},{21,... | collective-permute-start | bytes 3145736 | tf_op jit(solution)/shard_map/ppermute | solution.py:169
  181.0 33.9 %collective-permute-start.36 = (bf16[2,1024,256]{2,1,0:T(8,128)(2,1)S(1)}, bf16[2,1024,256]{2,1,0:T(8,128)(2,1)S(1)}, u32[]{:S(2)}, u32[]{:S(2)}) collective-permute-start(bf16[2,1024,256]{2,1,0:T(8,128)(2,1)S(1)} %collective-permute-done.34.refs_5_), channel_id=1, source_target_pairs={{4,0},{5,1},{6,2},{7,3},{8,12},{9,13},{10,14},{11,15},{20,16},{21,... | collective-permute-start | bytes 3145736 | tf_op jit(solution)/shard_map/ppermute | solution.py:169
  201.8 35.6 %collective-permute-start.28 = (bf16[2,1024,256]{2,1,0:T(8,128)(2,1)S(1)}, bf16[2,1024,256]{2,1,0:T(8,128)(2,1)S(1)}, u32[]{:S(2)}, u32[]{:S(2)}) collective-permute-start(bf16[2,1024,256]{2,1,0:T(8,128)(2,1)S(1)} %collective-permute-done.23.refs_5_), channel_id=1, source_target_pairs={{4,0},{5,1},{6,2},{7,3},{8,12},{9,13},{10,14},{11,15},{20,16},{21,... | collective-permute-start | bytes 3145736 | tf_op jit(solution)/shard_map/ppermute | solution.py:169
  205.6 36.2 %collective-permute-start.17 = (bf16[4,64,1024]{2,1,0:T(8,128)(2,1)S(1)}, bf16[4,64,1024]{2,1,0:T(8,128)(2,1)S(1)}, u32[]{:S(2)}, u32[]{:S(2)}) collective-permute-start(bf16[4,64,1024]{2,1,0:T(8,128)(2,1)S(1)} %collective-permute-done.11), channel_id=1, source_target_pairs={{0,4},{1,5},{2,6},{3,7},{12,8},{13,9},{14,10},{15,11},{16,20},{17,... | collective-permute-start | bytes 1572872 | tf_op jit(solution)/shard_map/ppermute | solution.py:169
  207.0 36.6 %collective-permute-start.31 = (bf16[2,256,256]{2,1,0:T(8,128)(2,1)S(1)}, bf16[2,256,256]{2,1,0:T(8,128)(2,1)S(1)}, u32[]{:S(2)}, u32[]{:S(2)}) collective-permute-start(bf16[2,256,256]{2,1,0:T(8,128)(2,1)S(1)} %shard_map.79), channel_id=1, source_target_pairs={{4,0},{5,1},{6,2},{7,3},{8,12},{9,13},{10,14},{11,15},{20,16},{21,... | collective-permute-start | bytes 786440 | tf_op jit(solution)/shard_map/ppermute | solution.py:220
  212.3 56.9 %collective-permute-start.13 = (bf16[2,256,256]{2,1,0:T(8,128)(2,1)S(1)}, bf16[2,256,256]{2,1,0:T(8,128)(2,1)S(1)}, u32[]{:S(2)}, u32[]{:S(2)}) collective-permute-start(bf16[2,256,256]{2,1,0:T(8,128)(2,1)S(1)} %shard_map.71), channel_id=1, source_target_pairs={{4,0},{5,1},{6,2},{7,3},{8,12},{9,13},{10,14},{11,15},{20,16},{21,... | collective-permute-start | bytes 786440 | tf_op jit(solution)/shard_map/ppermute | solution.py:220
  214.8 32.0 %collective-permute-start.35 = (bf16[2,256,256]{2,1,0:T(8,128)(2,1)S(1)}, bf16[2,256,256]{2,1,0:T(8,128)(2,1)S(1)}, u32[]{:S(2)}, u32[]{:S(2)}) collective-permute-start(bf16[2,256,256]{2,1,0:T(8,128)(2,1)S(1)} %shard_map.81), channel_id=1, source_target_pairs={{0,8},{1,9},{2,10},{3,11},{8,0},{9,1},{10,2},{11,3},{4,12},{5,13},... | collective-permute-start | bytes 786440 | tf_op jit(solution)/shard_map/ppermute | solution.py:219
  237.4 31.8 %collective-permute-start.24 = (bf16[2,256,256]{2,1,0:T(8,128)(2,1)S(1)}, bf16[2,256,256]{2,1,0:T(8,128)(2,1)S(1)}, u32[]{:S(2)}, u32[]{:S(2)}) collective-permute-start(bf16[2,256,256]{2,1,0:T(8,128)(2,1)S(1)} %shard_map.74), channel_id=1, source_target_pairs={{0,8},{1,9},{2,10},{3,11},{8,0},{9,1},{10,2},{11,3},{4,12},{5,13},... | collective-permute-start | bytes 786440 | tf_op jit(solution)/shard_map/ppermute | solution.py:219
  241.9 26.6 %collective-permute-start.37 = (bf16[2,256,256]{2,1,0:T(8,128)(2,1)S(1)}, bf16[2,256,256]{2,1,0:T(8,128)(2,1)S(1)}, u32[]{:S(2)}, u32[]{:S(2)}) collective-permute-start(bf16[2,256,256]{2,1,0:T(8,128)(2,1)S(1)} %shard_map.82), channel_id=1, source_target_pairs={{0,12},{1,13},{2,14},{3,15},{12,0},{13,1},{14,2},{15,3},{4,8},{5,9... | collective-permute-start | bytes 786440 | tf_op jit(solution)/shard_map/ppermute | solution.py:218
  243.6 29.5 %collective-permute-start.29 = (bf16[2,256,256]{2,1,0:T(8,128)(2,1)S(1)}, bf16[2,256,256]{2,1,0:T(8,128)(2,1)S(1)}, u32[]{:S(2)}, u32[]{:S(2)}) collective-permute-start(bf16[2,256,256]{2,1,0:T(8,128)(2,1)S(1)} %shard_map.76), channel_id=1, source_target_pairs={{0,12},{1,13},{2,14},{3,15},{12,0},{13,1},{14,2},{15,3},{4,8},{5,9... | collective-permute-start | bytes 786440 | tf_op jit(solution)/shard_map/ppermute | solution.py:218
  (7 other events, 27.9 us)

commit v2 on v1

v2 whole, which is shorter than its diff:
```python
import functools

import jax
import jax.numpy as jnp
from jax import lax
from jax.experimental import pallas as pl
from jax.experimental.pallas import tpu as pltpu
from jax.sharding import PartitionSpec as P

PLANES = 4
TILE = 16
VMEM = 60 * 1024 * 1024


def shift_terms(vbias, gauss_rows):
    xbar = jnp.clip(-0.3 * vbias, -1.0, 1.0)
    log_terms = jnp.sum(gauss_rows * xbar - 0.5 * xbar * xbar, axis=1)
    fields = (gauss_rows - xbar).astype(jnp.bfloat16)
    return (fields, log_terms)


def butterfly_sum(value, size):
    step = 1
    while step < size:
        if 2 * step < size:
            one, two, three = (
                lax.ppermute(value, "chol", [(i, i ^ (k * step)) for i in range(size)]) for k in (1, 2, 3)
            )
            value = (value + one) + (two + three)
            step *= 4
        else:
            value = value + lax.ppermute(value, "chol", [(i, i ^ step) for i in range(size)])
            step *= 2
    return value


def potential_kernel(fields_ref, chol_ref, *rest):
    out, spread = rest[-2:]
    vectors, tile, width = chol_ref.shape
    walkers = fields_ref.shape[0]

    @pl.when(pl.program_id(0) == 0)
    def _():
        shape = (vectors, vectors * tile)
        pick = lax.broadcasted_iota(jnp.int32, shape, 1) // tile == lax.broadcasted_iota(jnp.int32, shape, 0)
        wide = jnp.dot(fields_ref[...], pick.astype(jnp.bfloat16), preferred_element_type=jnp.float32)
        shape = (tile, vectors * tile)
        mine = lax.broadcasted_iota(jnp.int32, shape, 1) % tile == lax.broadcasted_iota(jnp.int32, shape, 0)
        for w in range(walkers):
            rows = jnp.where(mine, jnp.broadcast_to(wide[w : w + 1], shape), 0.0)
            spread[w * tile : (w + 1) * tile, :] = rows.astype(jnp.bfloat16)

    total = jnp.dot(
        spread[...], chol_ref[...].reshape(vectors * tile, width), preferred_element_type=jnp.float32
    )
    out[...] = (total * 0.3).astype(jnp.bfloat16).reshape(walkers, tile, width)


def potential_rows(fields, chol_full, after):
    vectors, rows, width = chol_full.shape
    walkers = fields.shape[0]
    return pl.pallas_call(
        potential_kernel,
        grid=(rows // TILE,),
        in_specs=[
            pl.BlockSpec((walkers, vectors), lambda b: (0, 0)),
            pl.BlockSpec((vectors, TILE, width), lambda b: (0, b, 0)),
        ]
        + [pl.BlockSpec(memory_space=pl.ANY)] * len(after),
        out_specs=pl.BlockSpec((walkers, TILE, width), lambda b: (0, b, 0)),
        out_shape=jax.ShapeDtypeStruct((walkers, rows, width), jnp.bfloat16),
        scratch_shapes=[pltpu.VMEM((walkers * TILE, vectors * TILE), jnp.bfloat16)],
        compiler_params=pltpu.CompilerParams(vmem_limit_bytes=VMEM),
        cost_estimate=pl.CostEstimate(flops=60_000_000_000, bytes_accessed=1, transcendentals=0),
    )(fields, chol_full, *after)


def copy_kernel(source, *rest):
    rest[-1][...] = source[...]


def some_walkers(orbitals, first, walkers, after):
    _, width, occupied = orbitals.shape
    return pl.pallas_call(
        copy_kernel,
        grid=(walkers,),
        in_specs=[pl.BlockSpec((1, width, occupied), lambda w: (w + first, 0, 0))]
        + [pl.BlockSpec(memory_space=pl.ANY)] * len(after),
        out_specs=pl.BlockSpec((1, width, occupied), lambda w: (w, 0, 0)),
        out_shape=jax.ShapeDtypeStruct((walkers, width, occupied), orbitals.dtype),
        compiler_params=pltpu.CompilerParams(vmem_limit_bytes=VMEM),
        cost_estimate=pl.CostEstimate(flops=1, bytes_accessed=1, transcendentals=0),
    )(orbitals, *after)


def moved_kernel(choices, scalars, pieces, *refs):
    orbs, out = refs[:choices], refs[-1]
    rows = out.shape[1]

    def orbital_rows(index):
        if choices == 1:
            return orbs[0][index]
        return jnp.where(scalars[0] == 0, orbs[0][index], orbs[1][index])

    left = pieces[...].reshape(rows, pieces.shape[3])
    moved = jnp.dot(left, orbital_rows(0), preferred_element_type=jnp.float32)
    old = orbital_rows((0, pl.ds(pl.multiple_of(scalars[1] * rows, rows), rows)))
    out[0] = (old.astype(jnp.float32) + moved).astype(jnp.bfloat16)


def moved_rows(pieces, orbs, scalars, first, after=()):
    choices = len(orbs)
    lanes, _, rows, width = pieces.shape
    walkers, _, occupied = orbs[0].shape
    return pl.pallas_call(
        functools.partial(moved_kernel, choices),
        grid_spec=pltpu.PrefetchScalarGridSpec(
            num_scalar_prefetch=1,
            grid=(walkers,),
            in_specs=[pl.BlockSpec((lanes, 1, rows, width), lambda w, s: (0, w + first, 0, 0))]
            + [pl.BlockSpec((1, width, occupied), lambda w, s: (w, 0, 0))] * choices
            + [pl.BlockSpec(memory_space=pl.ANY)] * len(after),
            out_specs=pl.BlockSpec((1, lanes * rows, occupied), lambda w, s: (w, 0, 0)),
        ),
        out_shape=jax.ShapeDtypeStruct((walkers, lanes * rows, occupied), jnp.bfloat16),
        compiler_params=pltpu.CompilerParams(vmem_limit_bytes=VMEM),
        cost_estimate=pl.CostEstimate(flops=15_000_000_000, bytes_accessed=1, transcendentals=0),
    )(scalars, pieces, *orbs, *after)


def join_kernel(scalars, *refs):
    own, beside, sent, cross, mirror, out = refs
    rows = own.shape[1]

    def put(value, k):
        out[0, pl.ds(pl.multiple_of((scalars[1] ^ k) * rows, rows), rows), :] = value

    put(own[0], 0)
    put(jnp.where(scalars[0] == 0, beside[0], sent[0]), 1)
    put(cross[0], 2)
    put(mirror[0], 3)


def join_rows(scalars, blocks):
    walkers, rows, occupied = blocks[0].shape
    return pl.pallas_call(
        join_kernel,
        grid_spec=pltpu.PrefetchScalarGridSpec(
            num_scalar_prefetch=1,
            grid=(walkers,),
            in_specs=[pl.BlockSpec((1, rows, occupied), lambda w, s: (w, 0, 0))] * len(blocks),
            out_specs=pl.BlockSpec((1, PLANES * rows, occupied), lambda w, s: (w, 0, 0)),
        ),
        out_shape=jax.ShapeDtypeStruct((walkers, PLANES * rows, occupied), jnp.bfloat16),
        compiler_params=pltpu.CompilerParams(vmem_limit_bytes=VMEM),
    )(scalars, *blocks)


def on_device(size, chol_full, chol_half, green, gauss, orbitals):
    walkers = green.shape[0]
    owned = orbitals.shape[0]
    vectors = chol_half.shape[0]
    lanes = size // PLANES
    me = lax.axis_index("chol")
    plane, lane = me // lanes, me % lanes
    inner = ((plane == 1) | (plane == 2)).astype(jnp.int32)

    def along(targets):
        return [(a * lanes + k, b * lanes + k) for a, b in targets for k in range(lanes)]

    inward = along([(0, 1), (3, 2)])
    outward = along([(1, 0), (2, 3)])
    middle = along([(1, 2), (2, 1)])

    def send(arrays, targets):
        return [lax.ppermute(a, "chol", targets) for a in arrays]

    parts = 2
    share = owned // parts

    def forward(mine):
        beside, facing = send([mine], inward), send([mine], middle)
        far, out_facing = send(beside, middle), send(facing, outward)
        return mine, beside[0], facing[0], far[0], out_facing[0], send(far, outward)[0]

    halves = [forward(some_walkers(orbitals, 0, share, []))]

    partial_value = lax.dot_general(
        green.reshape(walkers, -1),
        chol_half.reshape(vectors, -1),
        (((1,), (1,)), ((), ())),
        preferred_element_type=jnp.float32,
    )
    vbias = butterfly_sum(partial_value, size)
    fields, log_terms = shift_terms(vbias, gauss)
    log_factor = lax.dynamic_slice_in_dim(log_terms, me * owned, owned, 0)
    fields = fields.reshape(PLANES, lanes * owned, vectors)
    rows, width = chol_full.shape[1:]
    groups = [[p * lanes + k for k in range(lanes)] for p in range(PLANES)]

    def made_for(slot, after):
        return potential_rows(lax.dynamic_index_in_dim(fields, plane ^ slot, 0, keepdims=False), chol_full, after)

    def exchange(made):
        return lax.all_to_all(made, "chol", 0, 0, axis_index_groups=groups, tiled=True).reshape(lanes, owned, rows, width)

    def scalars(rows_of):
        return jnp.stack([inner, rows_of]).astype(jnp.int32)

    def moved(pieces, choices, rows_of, i, after=()):
        return moved_rows(pieces, choices, scalars(rows_of), i * share, after)

    first, second = range(parts)
    made = made_for(1, [halves[0][1], halves[0][2]])
    halves.append(forward(some_walkers(orbitals, share, share, [made])))
    own, beside, facing, far, out_facing, out_far = zip(*halves)
    pieces = exchange(made)
    (sent,) = send([pieces], inward)
    next_to = [moved(pieces, [beside[i]], plane, i) for i in range(parts)]
    pieces = exchange(made_for(3, [far[first], out_facing[first]]))
    mirror = [moved(pieces, [out_far[i], facing[i]], plane, i) for i in range(parts)]
    pieces = exchange(made_for(2, [facing[second], beside[second], out_far[first]]))
    cross = [moved(pieces, [out_facing[i], far[i]], plane, i, [out_far[second]]) for i in range(parts)]
    pieces = exchange(made_for(0, [far[second], out_facing[second], *next_to, mirror[first]]))
    mirror = send(mirror, along([(0, 3), (3, 0), (1, 2), (2, 1)]))
    cross = send(cross, along([(0, 2), (2, 0), (1, 3), (3, 1)]))
    next_to = send(next_to, outward)
    new = []
    for i in range(parts):
        home = moved(pieces, [own[i]], plane, i)
        landed = moved(sent, [own[i]], plane ^ 1, i)
        new.append(join_rows(scalars(plane), [home, next_to[i], landed, cross[i], mirror[i]]))
    return (jnp.concatenate(new, axis=0), log_factor)


def solution(mesh):
    placed = (
        P(None, "chol", None),
        P(None, "chol", None),
        P("grp", "chol", None),
        P("grp", None),
        P(("grp", "chol"), None, None),
    )
    return jax.shard_map(
        functools.partial(on_device, mesh.shape["chol"]),
        mesh=mesh,
        in_specs=placed,
        out_specs=(P(("grp", "chol"), None, None), P(("grp", "chol"))),
        check_vma=False,
    )
```

time: 277 us -> 231 us (0.83)
  the two profiles are of different devices: /device:TPU:15 before, /device:TPU:0 now
where the time goes in v2:
time: 231 us; the launch traced here: 230 us
  Pallas kernels  83 us (36%)
  waiting for transfers between devices  62.4 us (27%)
  starting transfers between devices  62.1 us (27%)
  matrix products  8.87 us (4%)
  local copies, waits for them, and re-layouts  8.29 us (4%)
  other arithmetic  4.1 us (2%)
    ppermute x17, waiting for transfers between devices, send(): return [lax.ppermute(a, 'chol', targets) for a in arrays]  40.7 us
    pallas_call x4, Pallas kernels, potential_rows(): pl.pallas_call(potential_kernel, grid=(rows // TILE,), in_specs=[pl.Block...  39.8 us
    ppermute x17, starting transfers between devices, send(): return [lax.ppermute(a, 'chol', targets) for a in arrays]  39.6 us
    pallas_call x10, Pallas kernels, moved_rows(): pl.pallas_call(functools.partial(moved_kernel, choices), grid_spec=pltpu....  33.1 us
    all_to_all x4, starting transfers between devices, exchange(): lax.all_to_all(made, 'chol', 0, 0, axis_index_groups=groups, tiled=True)  16.1 us
    all_to_all x4, waiting for transfers between devices, exchange(): lax.all_to_all(made, 'chol', 0, 0, axis_index_groups=groups, tiled=True)  12.3 us
    ppermute x6, waiting for transfers between devices, butterfly_sum(): lax.ppermute(value, 'chol', [(i, i ^ k * step) for i in range(size)])  9.28 us
    dot_general x1, matrix products, on_device(): lax.dot_general(green.reshape(walkers, -1), chol_half.reshape(vectors, -1...  8.87 us
  transfers between devices with their start and end apart: 27, of which 8 were waited for; matrix products, arithmetic and copies ran while one was open for 5% of the time, Pallas kernels for 34%

profile of v2, /device:TPU:0, one launch (start us, length us, event | category | flops | bytes accessed | tf_op | source)
XLA Modules:
  0.0 229.6 jit_solution(14466073087714131320)
XLA Ops:
  3.7 8.7 %collective-permute-start.6 = (bf16[2,1024,256]{2,1,0:T(8,128)(2,1)}, bf16[2,1024,256]{2,1,0:T(8,128)(2,1)}, u32[]{:S(2)}, u32[]{:S(2)}) collective-permute-start(bf16[2,1024,256]{2,1,0:T(8,128)(2,1)} %shard_map.68.refs_0_), channel_id=1, source_target_pairs={{0,4},{1,5},{2,6},{3,7},{12,8},{13,9},{14,10},{15,11},{16,20},{17,... | collective-permute-start | bytes 3145736 | tf_op jit(solution)/shard_map/ppermute | solution.py:176
  12.4 8.9 %fusion.3 = f32[64,128]{1,0:T(8,128)S(1)} fusion(bf16[128,64,256]{2,1,0:T(8,128)(2,1)} %param.6, bf16[64,64,256]{2,1,0:T(8,128)(2,1)S(1)} %copy-done.7), kind=kOutput, calls=%fused_computation.4 | convolution fusion | flops 268435456 | bytes 6324224 | tf_op jit(solution)/shard_map/dot_general | solution.py:188
  27.2 3.0 %collective-permute-start.3 = (f32[64,128]{1,0:T(8,128)S(1)}, f32[64,128]{1,0:T(8,128)S(1)}, u32[]{:S(2)}, u32[]{:S(2)}) collective-permute-start(f32[64,128]{1,0:T(8,128)S(1)} %add_add_fusion), channel_id=1, source_target_pairs={{0,4},{1,5},{2,6},{3,7},{4,0},{5,1},{6,2},{7,3},{8,12},{9,13},{10,... | collective-permute-start | bytes 98312 | tf_op jit(solution)/shard_map/ppermute | solution.py:27
  30.2 6.7 %collective-permute-done.5 = f32[64,128]{1,0:T(8,128)S(1)} collective-permute-done((f32[64,128]{1,0:T(8,128)S(1)}, f32[64,128]{1,0:T(8,128)S(1)}, u32[]{:S(2)}, u32[]{:S(2)}) %collective-permute-start.5) | collective-permute-done | bytes 32800 | tf_op jit(solution)/shard_map/ppermute | solution.py:27
  40.4 9.9 %shard_map.69.rest_0_ = bf16[16,64,1024]{2,1,0:T(8,128)(2,1)} custom-call(bf16[16,128]{1,0:T(8,128)(2,1)} %get-tuple-element.6.fields_ref, bf16[128,64,1024]{2,1,0:T(8,128)(2,1)} %chol_ref.7, bf16[2,1024,256]{2,1,0:T(8,128)(2,1)} %collective-permute-done.6.rest_0_.refs_0_, bf16[2,1024,256]{2,1,0:T(8,128)(2,1)} %copy-done.8), custom_call_target="tpu_custom_call" | custom-call | flops 60000002048 | bytes 1 | tf_op jit(solution)/shard_map/pallas_call | solution.py:62
  54.1 5.9 %collective-permute-start.8 = (bf16[2,1024,256]{2,1,0:T(8,128)(2,1)}, bf16[2,1024,256]{2,1,0:T(8,128)(2,1)S(1)}, u32[]{:S(2)}, u32[]{:S(2)}) collective-permute-start(bf16[2,1024,256]{2,1,0:T(8,128)(2,1)} %shard_map.70.refs_0_), channel_id=1, source_target_pairs={{0,4},{1,5},{2,6},{3,7},{12,8},{13,9},{14,10},{15,11},{16,20},{17,... | collective-permute-start | bytes 3145736 | tf_op jit(solution)/shard_map/ppermute | solution.py:176
  63.2 4.5 %all-to-all-start = ((bf16[16,64,1024]{2,1,0:T(8,128)(2,1)}), bf16[16,64,1024]{2,1,0:T(8,128)(2,1)}, u32[]{:S(2)}, u32[]{:S(2)}) async-start(bf16[16,64,1024]{2,1,0:T(8,128)(2,1)} %shard_map.69.rest_0_), calls=%async_computation | async-start | bytes 4194304 | tf_op jit(solution)/shard_map/all_to_all | solution.py:205
  70.3 10.8 %collective-permute-done.8.refs_0_.rest_1_ = bf16[2,1024,256]{2,1,0:T(8,128)(2,1)S(1)} collective-permute-done((bf16[2,1024,256]{2,1,0:T(8,128)(2,1)}, bf16[2,1024,256]{2,1,0:T(8,128)(2,1)S(1)}, u32[]{:S(2)}, u32[]{:S(2)}) %collective-permute-start.8) | collective-permute-done | bytes 1048608 | tf_op jit(solution)/shard_map/ppermute | solution.py:176
  82.7 5.3 %collective-permute-done.13.rest_1_.refs_0_ = bf16[2,1024,256]{2,1,0:T(8,128)(2,1)S(1)} collective-permute-done((bf16[2,1024,256]{2,1,0:T(8,128)(2,1)S(1)}, bf16[2,1024,256]{2,1,0:T(8,128)(2,1)S(1)}, u32[]{:S(2)}, u32[]{:S(2)}) %collective-permute-start.13) | collective-permute-done | bytes 1048608 | tf_op jit(solution)/shard_map/ppermute | solution.py:176
  89.0 10.0 %shard_map.73 = bf16[16,64,1024]{2,1,0:T(8,128)(2,1)} custom-call(bf16[16,128]{1,0:T(8,128)(2,1)} %get-tuple-element.5.fields_ref, bf16[128,64,1024]{2,1,0:T(8,128)(2,1)} %chol_ref.7, bf16[2,1024,256]{2,1,0:T(8,128)(2,1)} %collective-permute-done.12.rest_0_.refs_1_, bf16[2,1024,256]{2,1,0:T(8,128)(2,1)} %copy-done.10), custom_call_target="tpu_custom_call" | custom-call | flops 60000002048 | bytes 1 | tf_op jit(solution)/shard_map/pallas_call | solution.py:62
  99.0 3.6 %all-to-all-start.1 = ((bf16[16,64,1024]{2,1,0:T(8,128)(2,1)}), bf16[16,64,1024]{2,1,0:T(8,128)(2,1)S(1)}, u32[]{:S(2)}, u32[]{:S(2)}) async-start(bf16[16,64,1024]{2,1,0:T(8,128)(2,1)} %shard_map.73), calls=%async_computation.1 | async-start | bytes 4194304 | tf_op jit(solution)/shard_map/all_to_all | solution.py:205
  102.6 7.4 %collective-permute-start.16 = (bf16[4,4,64,1024]{3,2,1,0:T(8,128)(2,1)}, bf16[4,4,64,1024]{3,2,1,0:T(8,128)(2,1)}, u32[]{:S(2)}, u32[]{:S(2)}) collective-permute-start(bf16[4,4,64,1024]{3,2,1,0:T(8,128)(2,1)} %bitcast.6.pieces), channel_id=1, source_target_pairs={{0,4},{1,5},{2,6},{3,7},{12,8},{13,9},{14,10},{15,11},{16,20},{17,... | collective-permute-start | bytes 6291464 | tf_op jit(solution)/shard_map/ppermute | solution.py:176
  110.0 3.1 %shard_map.71.rest_2_ = bf16[2,256,256]{2,1,0:T(8,128)(2,1)} custom-call(s32[2]{0:T(128)} %pad_add_fusion.scalars, bf16[4,4,64,1024]{3,2,1,0:T(8,128)(2,1)} %bitcast.6.pieces, bf16[2,1024,256]{2,1,0:T(8,128)(2,1)} %collective-permute-done.6.rest_0_.refs_0_), custom_call_target="tpu_custom_call" | custom-call | flops 15000000512 | bytes 1 | tf_op jit(solution)/shard_map/pallas_call | solution.py:115
  114.6 3.2 %shard_map.72.rest_3_ = bf16[2,256,256]{2,1,0:T(8,128)(2,1)} custom-call(s32[2]{0:T(128)} %pad_add_fusion.scalars, bf16[4,4,64,1024]{3,2,1,0:T(8,128)(2,1)} %bitcast.6.pieces, bf16[2,1024,256]{2,1,0:T(8,128)(2,1)} %copy-done.11), custom_call_target="tpu_custom_call" | custom-call | flops 15000000512 | bytes 1 | tf_op jit(solution)/shard_map/pallas_call | solution.py:115
  120.4 10.0 %shard_map.78 = bf16[16,64,1024]{2,1,0:T(8,128)(2,1)} custom-call(bf16[16,128]{1,0:T(8,128)(2,1)} %get-tuple-element.4.fields_ref, bf16[128,64,1024]{2,1,0:T(8,128)(2,1)} %chol_ref.7, bf16[2,1024,256]{2,1,0:T(8,128)(2,1)} %collective-permute-done.10.rest_0_.refs_1_, bf16[2,1024,256]{2,1,0:T(8,128)(2,1)} %copy-done.11, ...), custom_call_target="tpu_custom_call" | custom-call | flops 60000002048 | bytes 1 | tf_op jit(solution)/shard_map/pallas_call | solution.py:62
  131.7 4.4 %all-to-all-start.3 = ((bf16[16,64,1024]{2,1,0:T(8,128)(2,1)}), bf16[16,64,1024]{2,1,0:T(8,128)(2,1)}, u32[]{:S(2)}, u32[]{:S(2)}) async-start(bf16[16,64,1024]{2,1,0:T(8,128)(2,1)} %shard_map.78), calls=%async_computation.3 | async-start | bytes 4194304 | tf_op jit(solution)/shard_map/all_to_all | solution.py:205
  136.1 3.5 %shard_map.74.rest_4_ = bf16[2,256,256]{2,1,0:T(8,128)(2,1)} custom-call(s32[2]{0:T(128)} %pad_add_fusion.scalars, bf16[4,4,64,1024]{3,2,1,0:T(8,128)(2,1)} %bitcast.18, bf16[2,1024,256]{2,1,0:T(8,128)(2,1)} %collective-permute-done.14.refs_0_.rest_2_, bf16[2,1024,256]{2,1,0:T(8,128)(2,1)} %copy-done.8), custom_call_target="tpu_custom_call" | custom-call | flops 15000000512 | bytes 1 | tf_op jit(solution)/shard_map/pallas_call | solution.py:115
  142.1 10.0 %shard_map.75 = bf16[16,64,1024]{2,1,0:T(8,128)(2,1)} custom-call(bf16[16,128]{1,0:T(8,128)(2,1)} %get-tuple-element.7.fields_ref, bf16[128,64,1024]{2,1,0:T(8,128)(2,1)} %chol_ref.7, bf16[2,1024,256]{2,1,0:T(8,128)(2,1)} %collective-permute-done.9.rest_0_.refs_1_, bf16[2,1024,256]{2,1,0:T(8,128)(2,1)} %collective-permute-done.11.rest_1_.refs_0_, ...), custom_call_target="tpu_custom_call" | custom-call | flops 60000002048 | bytes 1 | tf_op jit(solution)/shard_map/pallas_call | solution.py:62
  152.0 17.1 %collective-permute-done.17.refs_2_.refs_0_ = bf16[2,1024,256]{2,1,0:T(8,128)(2,1)S(1)} collective-permute-done((bf16[2,1024,256]{2,1,0:T(8,128)(2,1)}, bf16[2,1024,256]{2,1,0:T(8,128)(2,1)S(1)}, u32[]{:S(2)}, u32[]{:S(2)}) %collective-permute-start.17) | collective-permute-done | bytes 1048608 | tf_op jit(solution)/shard_map/ppermute | solution.py:176
  170.2 3.5 %shard_map.84 = bf16[2,256,256]{2,1,0:T(8,128)(2,1)} custom-call(s32[2]{0:T(128)} %pad_add_fusion.scalars, bf16[4,4,64,1024]{3,2,1,0:T(8,128)(2,1)} %bitcast.19, bf16[2,1024,256]{2,1,0:T(8,128)(2,1)} %copy-done.12, bf16[2,1024,256]{2,1,0:T(8,128)(2,1)} %collective-permute-done.10.rest_0_.refs_1_), custom_call_target="tpu_custom_call" | custom-call | flops 15000000512 | bytes 1 | tf_op jit(solution)/shard_map/pallas_call | solution.py:115
  175.0 3.6 %all-to-all-start.2 = ((bf16[16,64,1024]{2,1,0:T(8,128)(2,1)}), bf16[16,64,1024]{2,1,0:T(8,128)(2,1)S(1)}, u32[]{:S(2)}, u32[]{:S(2)}) async-start(bf16[16,64,1024]{2,1,0:T(8,128)(2,1)} %shard_map.75), calls=%async_computation.2 | async-start | bytes 4194304 | tf_op jit(solution)/shard_map/all_to_all | solution.py:205
  178.7 3.5 %shard_map.83 = bf16[2,256,256]{2,1,0:T(8,128)(2,1)} custom-call(s32[2]{0:T(128)} %pad_add_fusion.scalars, bf16[4,4,64,1024]{3,2,1,0:T(8,128)(2,1)} %bitcast.12.pieces, bf16[2,1024,256]{2,1,0:T(8,128)(2,1)} %collective-permute-done.11.rest_1_.refs_0_, bf16[2,1024,256]{2,1,0:T(8,128)(2,1)} %collective-permute-done.9.rest_0_.refs_1_, ...), custom_call_target="tpu_custom_call" | custom-call | flops 15000000512 | bytes 1 | tf_op jit(solution)/shard_map/pallas_call | solution.py:115
  182.2 3.5 %shard_map.79 = bf16[2,256,256]{2,1,0:T(8,128)(2,1)} custom-call(s32[2]{0:T(128)} %pad_add_fusion.scalars, bf16[4,4,64,1024]{3,2,1,0:T(8,128)(2,1)} %bitcast.12.pieces, bf16[2,1024,256]{2,1,0:T(8,128)(2,1)} %copy-done.10, bf16[2,1024,256]{2,1,0:T(8,128)(2,1)} %collective-permute-done.12.rest_0_.refs_1_, bf16[2,1024,256]{2,1,0:T(8,128)(2,1)} %copy-done.12), custom_call_target="tpu_custom_call" | custom-call | flops 15000000512 | bytes 1 | tf_op jit(solution)/shard_map/pallas_call | solution.py:115
  185.7 3.2 %shard_map.82.refs_2_ = bf16[2,256,256]{2,1,0:T(8,128)(2,1)} custom-call(s32[2]{0:T(128)} %pad_add_fusion.1.scalars, bf16[4,4,64,1024]{3,2,1,0:T(8,128)(2,1)} %collective-permute-done.16.pieces, bf16[2,1024,256]{2,1,0:T(8,128)(2,1)} %shard_map.70.refs_0_), custom_call_target="tpu_custom_call" | custom-call | flops 15000000512 | bytes 1 | tf_op jit(solution)/shard_map/pallas_call | solution.py:115
  188.8 3.2 %shard_map.77.refs_2_ = bf16[2,256,256]{2,1,0:T(8,128)(2,1)} custom-call(s32[2]{0:T(128)} %pad_add_fusion.1.scalars, bf16[4,4,64,1024]{3,2,1,0:T(8,128)(2,1)} %collective-permute-done.16.pieces, bf16[2,1024,256]{2,1,0:T(8,128)(2,1)} %shard_map.68.refs_0_), custom_call_target="tpu_custom_call" | custom-call | flops 15000000512 | bytes 1 | tf_op jit(solution)/shard_map/pallas_call | solution.py:115
  192.0 12.3 %all-to-all-done.2 = bf16[16,64,1024]{2,1,0:T(8,128)(2,1)S(1)} async-done(((bf16[16,64,1024]{2,1,0:T(8,128)(2,1)}), bf16[16,64,1024]{2,1,0:T(8,128)(2,1)S(1)}, u32[]{:S(2)}, u32[]{:S(2)}) %all-to-all-start.2) | async-done | bytes 2097184 | tf_op jit(solution)/shard_map/all_to_all | solution.py:205
  205.6 3.3 %shard_map.81.refs_0_ = bf16[2,256,256]{2,1,0:T(8,128)(2,1)} custom-call(s32[2]{0:T(128)} %pad_add_fusion.scalars, bf16[4,4,64,1024]{3,2,1,0:T(8,128)(2,1)} %bitcast.20, bf16[2,1024,256]{2,1,0:T(8,128)(2,1)} %shard_map.70.refs_0_), custom_call_target="tpu_custom_call" | custom-call | flops 15000000512 | bytes 1 | tf_op jit(solution)/shard_map/pallas_call | solution.py:115
  209.0 3.2 %shard_map.76.refs_0_ = bf16[2,256,256]{2,1,0:T(8,128)(2,1)} custom-call(s32[2]{0:T(128)} %pad_add_fusion.scalars, bf16[4,4,64,1024]{3,2,1,0:T(8,128)(2,1)} %bitcast.21, bf16[2,1024,256]{2,1,0:T(8,128)(2,1)} %shard_map.68.refs_0_), custom_call_target="tpu_custom_call" | custom-call | flops 15000000512 | bytes 1 | tf_op jit(solution)/shard_map/pallas_call | solution.py:115
  212.9 2.9 %shard_map.80 = bf16[2,1024,256]{2,1,0:T(8,128)(2,1)} custom-call(s32[2]{0:T(128)} %pad_add_fusion.scalars, bf16[2,256,256]{2,1,0:T(8,128)(2,1)} %shard_map.76.refs_0_, bf16[2,256,256]{2,1,0:T(8,128)(2,1)} %collective-permute-done.15.refs_1_, bf16[2,256,256]{2,1,0:T(8,128)(2,1)} %shard_map.77.refs_2_, bf16[2,256,256]{2,1,0:T(8,128)(2,1)} %copy-done.5, ...), custom_call_target="tpu_custom_call" | custom-call | tf_op jit(solution)/shard_map/pallas_call | solution.py:146
  215.8 7.4 %collective-permute-done.21.refs_3_ = bf16[2,256,256]{2,1,0:T(8,128)(2,1)S(1)} collective-permute-done((bf16[2,256,256]{2,1,0:T(8,128)(2,1)S(1)}, bf16[2,256,256]{2,1,0:T(8,128)(2,1)S(1)}, u32[]{:S(2)}, u32[]{:S(2)}) %collective-permute-start.21) | collective-permute-done | bytes 262176 | tf_op jit(solution)/shard_map/ppermute | solution.py:176
  223.9 2.9 %shard_map.85 = bf16[2,1024,256]{2,1,0:T(8,128)(2,1)} custom-call(s32[2]{0:T(128)} %pad_add_fusion.scalars, bf16[2,256,256]{2,1,0:T(8,128)(2,1)} %shard_map.81.refs_0_, bf16[2,256,256]{2,1,0:T(8,128)(2,1)} %collective-permute-done.20.refs_1_, bf16[2,256,256]{2,1,0:T(8,128)(2,1)} %shard_map.82.refs_2_, bf16[2,256,256]{2,1,0:T(8,128)(2,1)} %copy-done.4, ...), custom_call_target="tpu_custom_call" | custom-call | tf_op jit(solution)/shard_map/pallas_call | solution.py:146
  226.8 2.7 %pad_maximum_fusion = bf16[4,1024,256]{2,1,0:T(8,128)(2,1)} fusion(bf16[2,1024,256]{2,1,0:T(8,128)(2,1)} %shard_map.85, bf16[2,1024,256]{2,1,0:T(8,128)(2,1)S(1)} %copy-done), kind=kLoop, calls=%fused_computation.2 | loop fusion | flops 1048576 | bytes 4194304 | tf_op jit(solution)/shard_map/concatenate | solution.py:233
  (77 shorter events, 37.5 us)
Async XLA Ops:
  0.6 11.8 %copy-start.7 = (bf16[64,64,256]{2,1,0:T(8,128)(2,1)S(1)}, bf16[64,64,256]{2,1,0:T(8,128)(2,1)}, u32[]{:S(2)}) copy-start(bf16[64,64,256]{2,1,0:T(8,128)(2,1)} %param.7) | copy-start | bytes 6291460
  2.8 34.1 %copy-start.6 = (f32[64,128]{1,0:T(8,128)S(1)}, f32[64,128]{1,0:T(8,128)}, u32[]{:S(2)}) copy-start(f32[64,128]{1,0:T(8,128)} %param.8) | copy-start | bytes 98308
  2.9 36.5 %collective-permute-start.7 = (bf16[2,1024,256]{2,1,0:T(8,128)(2,1)}, bf16[2,1024,256]{2,1,0:T(8,128)(2,1)S(1)}, u32[]{:S(2)}, u32[]{:S(2)}) collective-permute-start(bf16[2,1024,256]{2,1,0:T(8,128)(2,1)} %shard_map.68.refs_0_), channel_id=1, source_target_pairs={{4,8},{5,9},{6,10},{7,11},{8,4},{9,5},{10,6},{11,7},{20,24},{21,25... | collective-permute-start | bytes 3145736 | tf_op jit(solution)/shard_map/ppermute | solution.py:176
  3.7 34.0 %collective-permute-start.6 = (bf16[2,1024,256]{2,1,0:T(8,128)(2,1)}, bf16[2,1024,256]{2,1,0:T(8,128)(2,1)}, u32[]{:S(2)}, u32[]{:S(2)}) collective-permute-start(bf16[2,1024,256]{2,1,0:T(8,128)(2,1)} %shard_map.68.refs_0_), channel_id=1, source_target_pairs={{0,4},{1,5},{2,6},{3,7},{12,8},{13,9},{14,10},{15,11},{16,20},{17,... | collective-permute-start | bytes 3145736 | tf_op jit(solution)/shard_map/ppermute | solution.py:176
  21.3 3.7 %collective-permute-start.2 = (f32[64,128]{1,0:T(8,128)S(1)}, f32[64,128]{1,0:T(8,128)S(1)}, u32[]{:S(2)}, u32[]{:S(2)}) collective-permute-start(f32[64,128]{1,0:T(8,128)S(1)} %fusion.3), channel_id=1, source_target_pairs={{0,3},{1,2},{2,1},{3,0},{4,7},{5,6},{6,5},{7,4},{8,11},{9,10},{10,... | collective-permute-start | bytes 98312 | tf_op jit(solution)/shard_map/ppermute | solution.py:27
  21.7 4.0 %collective-permute-start.1 = (f32[64,128]{1,0:T(8,128)S(1)}, f32[64,128]{1,0:T(8,128)S(1)}, u32[]{:S(2)}, u32[]{:S(2)}) collective-permute-start(f32[64,128]{1,0:T(8,128)S(1)} %fusion.3), channel_id=1, source_target_pairs={{0,2},{1,3},{2,0},{3,1},{4,6},{5,7},{6,4},{7,5},{8,10},{9,11},{10,... | collective-permute-start | bytes 98312 | tf_op jit(solution)/shard_map/ppermute | solution.py:27
  22.9 2.8 %collective-permute-start = (f32[64,128]{1,0:T(8,128)S(1)}, f32[64,128]{1,0:T(8,128)S(1)}, u32[]{:S(2)}, u32[]{:S(2)}) collective-permute-start(f32[64,128]{1,0:T(8,128)S(1)} %fusion.3), channel_id=1, source_target_pairs={{0,1},{1,0},{2,3},{3,2},{4,5},{5,4},{6,7},{7,6},{8,9},{9,8},{10,11... | collective-permute-start | bytes 98312 | tf_op jit(solution)/shard_map/ppermute | solution.py:27
  25.7 11.2 %collective-permute-start.5 = (f32[64,128]{1,0:T(8,128)S(1)}, f32[64,128]{1,0:T(8,128)S(1)}, u32[]{:S(2)}, u32[]{:S(2)}) collective-permute-start(f32[64,128]{1,0:T(8,128)S(1)} %add_add_fusion), channel_id=1, source_target_pairs={{0,12},{1,13},{2,14},{3,15},{4,8},{5,9},{6,10},{7,11},{8,4},{9,5},... | collective-permute-start | bytes 98312 | tf_op jit(solution)/shard_map/ppermute | solution.py:27
  27.2 9.8 %collective-permute-start.4 = (f32[64,128]{1,0:T(8,128)S(1)}, f32[64,128]{1,0:T(8,128)S(1)}, u32[]{:S(2)}, u32[]{:S(2)}) collective-permute-start(f32[64,128]{1,0:T(8,128)S(1)} %add_add_fusion), channel_id=1, source_target_pairs={{0,8},{1,9},{2,10},{3,11},{4,12},{5,13},{6,14},{7,15},{8,0},{9,1},... | collective-permute-start | bytes 98312 | tf_op jit(solution)/shard_map/ppermute | solution.py:27
  27.2 9.8 %collective-permute-start.3 = (f32[64,128]{1,0:T(8,128)S(1)}, f32[64,128]{1,0:T(8,128)S(1)}, u32[]{:S(2)}, u32[]{:S(2)}) collective-permute-start(f32[64,128]{1,0:T(8,128)S(1)} %add_add_fusion), channel_id=1, source_target_pairs={{0,4},{1,5},{2,6},{3,7},{4,0},{5,1},{6,2},{7,3},{8,12},{9,13},{10,... | collective-permute-start | bytes 98312 | tf_op jit(solution)/shard_map/ppermute | solution.py:27
  37.7 29.9 %collective-permute-start.12 = (bf16[2,1024,256]{2,1,0:T(8,128)(2,1)}, bf16[2,1024,256]{2,1,0:T(8,128)(2,1)}, u32[]{:S(2)}, u32[]{:S(2)}) collective-permute-start(bf16[2,1024,256]{2,1,0:T(8,128)(2,1)} %collective-permute-done.6.rest_0_.refs_0_), channel_id=1, source_target_pairs={{4,8},{5,9},{6,10},{7,11},{8,4},{9,5},{10,6},{11,7},{20,24},{21,25... | collective-permute-start | bytes 3145736 | tf_op jit(solution)/shard_map/ppermute | solution.py:176
  50.3 9.8 %copy-start.9 = (bf16[2,1024,256]{2,1,0:T(8,128)(2,1)S(1)}, bf16[2,1024,256]{2,1,0:T(8,128)(2,1)}, u32[]{:S(2)}) copy-start(bf16[2,1024,256]{2,1,0:T(8,128)(2,1)} %copy-done.8) | copy-start | bytes 3145732
  52.5 16.5 %collective-permute-start.10 = (bf16[2,1024,256]{2,1,0:T(8,128)(2,1)}, bf16[2,1024,256]{2,1,0:T(8,128)(2,1)}, u32[]{:S(2)}, u32[]{:S(2)}) collective-permute-start(bf16[2,1024,256]{2,1,0:T(8,128)(2,1)} %shard_map.70.refs_0_), channel_id=1, source_target_pairs={{4,8},{5,9},{6,10},{7,11},{8,4},{9,5},{10,6},{11,7},{20,24},{21,25... | collective-permute-start | bytes 3145736 | tf_op jit(solution)/shard_map/ppermute | solution.py:176
  54.1 26.9 %collective-permute-start.8 = (bf16[2,1024,256]{2,1,0:T(8,128)(2,1)}, bf16[2,1024,256]{2,1,0:T(8,128)(2,1)S(1)}, u32[]{:S(2)}, u32[]{:S(2)}) collective-permute-start(bf16[2,1024,256]{2,1,0:T(8,128)(2,1)} %shard_map.70.refs_0_), channel_id=1, source_target_pairs={{0,4},{1,5},{2,6},{3,7},{12,8},{13,9},{14,10},{15,11},{16,20},{17,... | collective-permute-start | bytes 3145736 | tf_op jit(solution)/shard_map/ppermute | solution.py:176
  60.0 28.0 %collective-permute-start.13 = (bf16[2,1024,256]{2,1,0:T(8,128)(2,1)S(1)}, bf16[2,1024,256]{2,1,0:T(8,128)(2,1)S(1)}, u32[]{:S(2)}, u32[]{:S(2)}) collective-permute-start(bf16[2,1024,256]{2,1,0:T(8,128)(2,1)S(1)} %copy-done.9), channel_id=1, source_target_pairs={{4,0},{5,1},{6,2},{7,3},{8,12},{9,13},{10,14},{11,15},{20,16},{21,... | collective-permute-start | bytes 3145736 | tf_op jit(solution)/shard_map/ppermute | solution.py:176
  63.2 35.8 %all-to-all-start = ((bf16[16,64,1024]{2,1,0:T(8,128)(2,1)}), bf16[16,64,1024]{2,1,0:T(8,128)(2,1)}, u32[]{:S(2)}, u32[]{:S(2)}) async-start(bf16[16,64,1024]{2,1,0:T(8,128)(2,1)} %shard_map.69.rest_0_), calls=%async_computation | async-start | bytes 4194304 | tf_op jit(solution)/shard_map/all_to_all | solution.py:205
  67.6 50.1 %collective-permute-start.14 = (bf16[2,1024,256]{2,1,0:T(8,128)(2,1)}, bf16[2,1024,256]{2,1,0:T(8,128)(2,1)}, u32[]{:S(2)}, u32[]{:S(2)}) collective-permute-start(bf16[2,1024,256]{2,1,0:T(8,128)(2,1)} %collective-permute-done.12.rest_0_.refs_1_), channel_id=1, source_target_pairs={{4,0},{5,1},{6,2},{7,3},{8,12},{9,13},{10,14},{11,15},{20,16},{21,... | collective-permute-start | bytes 3145736 | tf_op jit(solution)/shard_map/ppermute | solution.py:176
  69.0 70.6 %collective-permute-start.11 = (bf16[2,1024,256]{2,1,0:T(8,128)(2,1)}, bf16[2,1024,256]{2,1,0:T(8,128)(2,1)}, u32[]{:S(2)}, u32[]{:S(2)}) collective-permute-start(bf16[2,1024,256]{2,1,0:T(8,128)(2,1)} %collective-permute-done.10.rest_0_.refs_1_), channel_id=1, source_target_pairs={{4,0},{5,1},{6,2},{7,3},{8,12},{9,13},{10,14},{11,15},{20,16},{21,... | collective-permute-start | bytes 3145736 | tf_op jit(solution)/shard_map/ppermute | solution.py:176
  81.0 17.9 %copy-start.11 = (bf16[2,1024,256]{2,1,0:T(8,128)(2,1)}, bf16[2,1024,256]{2,1,0:T(8,128)(2,1)S(1)}, u32[]{:S(2)}) copy-start(bf16[2,1024,256]{2,1,0:T(8,128)(2,1)S(1)} %collective-permute-done.8.refs_0_.rest_1_) | copy-start | bytes 3145732
  81.0 38.0 %collective-permute-start.9 = (bf16[2,1024,256]{2,1,0:T(8,128)(2,1)S(1)}, bf16[2,1024,256]{2,1,0:T(8,128)(2,1)}, u32[]{:S(2)}, u32[]{:S(2)}) collective-permute-start(bf16[2,1024,256]{2,1,0:T(8,128)(2,1)S(1)} %collective-permute-done.8.refs_0_.rest_1_), channel_id=1, source_target_pairs={{4,8},{5,9},{6,10},{7,11},{8,4},{9,5},{10,6},{11,7},{20,24},{21,25... | collective-permute-start | bytes 3145736 | tf_op jit(solution)/shard_map/ppermute | solution.py:176
  99.0 31.4 %all-to-all-start.1 = ((bf16[16,64,1024]{2,1,0:T(8,128)(2,1)}), bf16[16,64,1024]{2,1,0:T(8,128)(2,1)S(1)}, u32[]{:S(2)}, u32[]{:S(2)}) async-start(bf16[16,64,1024]{2,1,0:T(8,128)(2,1)} %shard_map.73), calls=%async_computation.1 | async-start | bytes 4194304 | tf_op jit(solution)/shard_map/all_to_all | solution.py:205
  102.6 83.1 %collective-permute-start.16 = (bf16[4,4,64,1024]{3,2,1,0:T(8,128)(2,1)}, bf16[4,4,64,1024]{3,2,1,0:T(8,128)(2,1)}, u32[]{:S(2)}, u32[]{:S(2)}) collective-permute-start(bf16[4,4,64,1024]{3,2,1,0:T(8,128)(2,1)} %bitcast.6.pieces), channel_id=1, source_target_pairs={{0,4},{1,5},{2,6},{3,7},{12,8},{13,9},{14,10},{15,11},{16,20},{17,... | collective-permute-start | bytes 6291464 | tf_op jit(solution)/shard_map/ppermute | solution.py:176
  113.1 95.8 %collective-permute-start.15 = (bf16[2,256,256]{2,1,0:T(8,128)(2,1)}, bf16[2,256,256]{2,1,0:T(8,128)(2,1)}, u32[]{:S(2)}, u32[]{:S(2)}) collective-permute-start(bf16[2,256,256]{2,1,0:T(8,128)(2,1)} %shard_map.71.rest_2_), channel_id=1, source_target_pairs={{4,0},{5,1},{6,2},{7,3},{8,12},{9,13},{10,14},{11,15},{20,16},{21,... | collective-permute-start | bytes 786440 | tf_op jit(solution)/shard_map/ppermute | solution.py:176
  117.8 98.0 %collective-permute-start.20 = (bf16[2,256,256]{2,1,0:T(8,128)(2,1)}, bf16[2,256,256]{2,1,0:T(8,128)(2,1)}, u32[]{:S(2)}, u32[]{:S(2)}) collective-permute-start(bf16[2,256,256]{2,1,0:T(8,128)(2,1)} %shard_map.72.rest_3_), channel_id=1, source_target_pairs={{4,0},{5,1},{6,2},{7,3},{8,12},{9,13},{10,14},{11,15},{20,16},{21,... | collective-permute-start | bytes 786440 | tf_op jit(solution)/shard_map/ppermute | solution.py:176
  119.1 50.1 %collective-permute-start.17 = (bf16[2,1024,256]{2,1,0:T(8,128)(2,1)}, bf16[2,1024,256]{2,1,0:T(8,128)(2,1)S(1)}, u32[]{:S(2)}, u32[]{:S(2)}) collective-permute-start(bf16[2,1024,256]{2,1,0:T(8,128)(2,1)} %collective-permute-done.9.rest_0_.refs_1_), channel_id=1, source_target_pairs={{4,0},{5,1},{6,2},{7,3},{8,12},{9,13},{10,14},{11,15},{20,16},{21,... | collective-permute-start | bytes 3145736 | tf_op jit(solution)/shard_map/ppermute | solution.py:176
  131.7 43.4 %all-to-all-start.3 = ((bf16[16,64,1024]{2,1,0:T(8,128)(2,1)}), bf16[16,64,1024]{2,1,0:T(8,128)(2,1)}, u32[]{:S(2)}, u32[]{:S(2)}) async-start(bf16[16,64,1024]{2,1,0:T(8,128)(2,1)} %shard_map.78), calls=%async_computation.3 | async-start | bytes 4194304 | tf_op jit(solution)/shard_map/all_to_all | solution.py:205
  139.6 72.6 %collective-permute-start.19 = (bf16[2,256,256]{2,1,0:T(8,128)(2,1)}, bf16[2,256,256]{2,1,0:T(8,128)(2,1)}, u32[]{:S(2)}, u32[]{:S(2)}) collective-permute-start(bf16[2,256,256]{2,1,0:T(8,128)(2,1)} %shard_map.74.rest_4_), channel_id=1, source_target_pairs={{0,12},{1,13},{2,14},{3,15},{12,0},{13,1},{14,2},{15,3},{4,8},{5,9... | collective-permute-start | bytes 786440 | tf_op jit(solution)/shard_map/ppermute | solution.py:176
  173.7 42.1 %collective-permute-start.22 = (bf16[2,256,256]{2,1,0:T(8,128)(2,1)}, bf16[2,256,256]{2,1,0:T(8,128)(2,1)S(1)}, u32[]{:S(2)}, u32[]{:S(2)}) collective-permute-start(bf16[2,256,256]{2,1,0:T(8,128)(2,1)} %shard_map.84), channel_id=1, source_target_pairs={{0,12},{1,13},{2,14},{3,15},{12,0},{13,1},{14,2},{15,3},{4,8},{5,9... | collective-permute-start | bytes 786440 | tf_op jit(solution)/shard_map/ppermute | solution.py:176
  175.0 29.3 %all-to-all-start.2 = ((bf16[16,64,1024]{2,1,0:T(8,128)(2,1)}), bf16[16,64,1024]{2,1,0:T(8,128)(2,1)S(1)}, u32[]{:S(2)}, u32[]{:S(2)}) async-start(bf16[16,64,1024]{2,1,0:T(8,128)(2,1)} %shard_map.75), calls=%async_computation.2 | async-start | bytes 4194304 | tf_op jit(solution)/shard_map/all_to_all | solution.py:205
  185.7 26.5 %collective-permute-start.18 = (bf16[2,256,256]{2,1,0:T(8,128)(2,1)}, bf16[2,256,256]{2,1,0:T(8,128)(2,1)S(1)}, u32[]{:S(2)}, u32[]{:S(2)}) collective-permute-start(bf16[2,256,256]{2,1,0:T(8,128)(2,1)} %shard_map.79), channel_id=1, source_target_pairs={{0,8},{1,9},{2,10},{3,11},{8,0},{9,1},{10,2},{11,3},{4,12},{5,13},... | collective-permute-start | bytes 786440 | tf_op jit(solution)/shard_map/ppermute | solution.py:176
  209.0 14.3 %collective-permute-start.21 = (bf16[2,256,256]{2,1,0:T(8,128)(2,1)S(1)}, bf16[2,256,256]{2,1,0:T(8,128)(2,1)S(1)}, u32[]{:S(2)}, u32[]{:S(2)}) collective-permute-start(bf16[2,256,256]{2,1,0:T(8,128)(2,1)S(1)} %copy-done.13), channel_id=1, source_target_pairs={{0,8},{1,9},{2,10},{3,11},{8,0},{9,1},{10,2},{11,3},{4,12},{5,13},... | collective-permute-start | bytes 786440 | tf_op jit(solution)/shard_map/ppermute | solution.py:176
  215.8 11.1 %copy-start = (bf16[2,1024,256]{2,1,0:T(8,128)(2,1)S(1)}, bf16[2,1024,256]{2,1,0:T(8,128)(2,1)}, u32[]{:S(2)}) copy-start(bf16[2,1024,256]{2,1,0:T(8,128)(2,1)} %shard_map.80) | copy-start | bytes 3145732
  (9 other events, 17.8 us)

commit v3 on v2

--- a/solution.py
+++ b/solution.py
@@ -34,8 +34,8 @@
     return value
 
 
-def potential_kernel(fields_ref, chol_ref, *rest):
-    out, spread = rest[-2:]
+def potential_kernel(slots, fields_ref, chol_ref, *rest):
+    outs, spread = rest[-1 - slots : -1], rest[-1]
     vectors, tile, width = chol_ref.shape
     walkers = fields_ref.shape[0]
 
@@ -53,26 +53,29 @@
     total = jnp.dot(
         spread[...], chol_ref[...].reshape(vectors * tile, width), preferred_element_type=jnp.float32
     )
-    out[...] = (total * 0.3).astype(jnp.bfloat16).reshape(walkers, tile, width)
+    value = (total * 0.3).astype(jnp.bfloat16).reshape(slots, walkers // slots, tile, width)
+    for i in range(slots):
+        outs[i][...] = value[i]
 
 
 def potential_rows(fields, chol_full, after):
     vectors, rows, width = chol_full.shape
-    walkers = fields.shape[0]
-    return pl.pallas_call(
-        potential_kernel,
+    slots, share = len(fields), fields[0].shape[0]
+    walkers = slots * share
+    return pl.pallas_call(
+        functools.partial(potential_kernel, slots),
         grid=(rows // TILE,),
         in_specs=[
             pl.BlockSpec((walkers, vectors), lambda b: (0, 0)),
             pl.BlockSpec((vectors, TILE, width), lambda b: (0, b, 0)),
         ]
         + [pl.BlockSpec(memory_space=pl.ANY)] * len(after),
-        out_specs=pl.BlockSpec((walkers, TILE, width), lambda b: (0, b, 0)),
-        out_shape=jax.ShapeDtypeStruct((walkers, rows, width), jnp.bfloat16),
+        out_specs=[pl.BlockSpec((share, TILE, width), lambda b: (0, b, 0))] * slots,
+        out_shape=[jax.ShapeDtypeStruct((share, rows, width), jnp.bfloat16)] * slots,
         scratch_shapes=[pltpu.VMEM((walkers * TILE, vectors * TILE), jnp.bfloat16)],
         compiler_params=pltpu.CompilerParams(vmem_limit_bytes=VMEM),
         cost_estimate=pl.CostEstimate(flops=60_000_000_000, bytes_accessed=1, transcendentals=0),
-    )(fields, chol_full, *after)
+    )(jnp.concatenate(fields, axis=0), chol_full, *after)
 
 
 def copy_kernel(source, *rest):
@@ -128,32 +131,38 @@
     )(scalars, pieces, *orbs, *after)
 
 
-def join_kernel(scalars, *refs):
-    own, beside, sent, cross, mirror, out = refs
-    rows = own.shape[1]
-
-    def put(value, k):
-        out[0, pl.ds(pl.multiple_of((scalars[1] ^ k) * rows, rows), rows), :] = value
-
-    put(own[0], 0)
-    put(jnp.where(scalars[0] == 0, beside[0], sent[0]), 1)
-    put(cross[0], 2)
-    put(mirror[0], 3)
-
-
-def join_rows(scalars, blocks):
-    walkers, rows, occupied = blocks[0].shape
-    return pl.pallas_call(
-        join_kernel,
+def join_kernel(parts, scalars, *refs):
+    out = refs[-1]
+    rows = refs[0].shape[1]
+    share = refs[0].shape[0]
+
+    for part in range(parts):
+        own, beside, sent, cross, mirror = refs[part * 5 : part * 5 + 5]
+        walkers = pl.ds(part * share, share)
+
+        def put(value, k):
+            out[walkers, pl.ds(pl.multiple_of((scalars[1] ^ k) * rows, rows), rows), :] = value
+
+        put(own[...], 0)
+        put(jnp.where(scalars[0] == 0, beside[...], sent[...]), 1)
+        put(cross[...], 2)
+        put(mirror[...], 3)
+
+
+def join_rows(scalars, parts):
+    walkers, rows, occupied = parts[0][0].shape
+    columns = 128 if occupied % 128 == 0 else occupied
+    return pl.pallas_call(
+        functools.partial(join_kernel, len(parts)),
         grid_spec=pltpu.PrefetchScalarGridSpec(
             num_scalar_prefetch=1,
-            grid=(walkers,),
-            in_specs=[pl.BlockSpec((1, rows, occupied), lambda w, s: (w, 0, 0))] * len(blocks),
-            out_specs=pl.BlockSpec((1, PLANES * rows, occupied), lambda w, s: (w, 0, 0)),
+            grid=(occupied // columns,),
+            in_specs=[pl.BlockSpec((walkers, rows, columns), lambda c, s: (0, 0, c))] * (5 * len(parts)),
+            out_specs=pl.BlockSpec((len(parts) * walkers, PLANES * rows, columns), lambda c, s: (0, 0, c)),
         ),
-        out_shape=jax.ShapeDtypeStruct((walkers, PLANES * rows, occupied), jnp.bfloat16),
-        compiler_params=pltpu.CompilerParams(vmem_limit_bytes=VMEM),
-    )(scalars, *blocks)
+        out_shape=jax.ShapeDtypeStruct((len(parts) * walkers, PLANES * rows, occupied), jnp.bfloat16),
+        compiler_params=pltpu.CompilerParams(vmem_limit_bytes=VMEM),
+    )(scalars, *(block for part in parts for block in part))
 
 
 def on_device(size, chol_full, chol_half, green, gauss, orbitals):
@@ -198,8 +207,9 @@
     rows, width = chol_full.shape[1:]
     groups = [[p * lanes + k for k in range(lanes)] for p in range(PLANES)]
 
-    def made_for(slot, after):
-        return potential_rows(lax.dynamic_index_in_dim(fields, plane ^ slot, 0, keepdims=False), chol_full, after)
+    def made_for(slots, after):
+        chosen = [lax.dynamic_index_in_dim(fields, plane ^ slot, 0, keepdims=False) for slot in slots]
+        return potential_rows(chosen, chol_full, after)
 
     def exchange(made):
         return lax.all_to_all(made, "chol", 0, 0, axis_index_groups=groups, tiled=True).reshape(lanes, owned, rows, width)
@@ -211,26 +221,25 @@
         return moved_rows(pieces, choices, scalars(rows_of), i * share, after)
 
     first, second = range(parts)
-    made = made_for(1, [halves[0][1], halves[0][2]])
+    (made,) = made_for((1,), [halves[0][1], halves[0][2]])
     halves.append(forward(some_walkers(orbitals, share, share, [made])))
     own, beside, facing, far, out_facing, out_far = zip(*halves)
     pieces = exchange(made)
     (sent,) = send([pieces], inward)
     next_to = [moved(pieces, [beside[i]], plane, i) for i in range(parts)]
-    pieces = exchange(made_for(3, [far[first], out_facing[first]]))
-    mirror = [moved(pieces, [out_far[i], facing[i]], plane, i) for i in range(parts)]
-    pieces = exchange(made_for(2, [facing[second], beside[second], out_far[first]]))
-    cross = [moved(pieces, [out_facing[i], far[i]], plane, i, [out_far[second]]) for i in range(parts)]
-    pieces = exchange(made_for(0, [far[second], out_facing[second], *next_to, mirror[first]]))
+    pieces = exchange(*made_for((2,), [far[first], out_facing[first]]))
+    made = made_for((3, 0), [facing[second], beside[second], out_far[first]])
+    cross = [moved(pieces, [out_facing[i], far[i]], plane, i, made[1:]) for i in range(parts)]
+    landed = [moved(sent, [own[i]], plane ^ 1, i, cross) for i in range(parts)]
+    pieces = exchange(made[0])
+    mirror = [moved(pieces, [out_far[i], facing[i]], plane, i, cross) for i in range(parts)]
     mirror = send(mirror, along([(0, 3), (3, 0), (1, 2), (2, 1)]))
     cross = send(cross, along([(0, 2), (2, 0), (1, 3), (3, 1)]))
     next_to = send(next_to, outward)
-    new = []
-    for i in range(parts):
-        home = moved(pieces, [own[i]], plane, i)
-        landed = moved(sent, [own[i]], plane ^ 1, i)
-        new.append(join_rows(scalars(plane), [home, next_to[i], landed, cross[i], mirror[i]]))
-    return (jnp.concatenate(new, axis=0), log_factor)
+    pieces = exchange(made[1])
+    home = [moved(pieces, [own[first]], plane, first, cross)]
+    home.append(moved(pieces, [own[second]], plane, second, mirror))
+    return (join_rows(scalars(plane), list(zip(home, next_to, landed, cross, mirror))), log_factor)
 
 
 def solution(mesh):

time: 231 us -> 219 us (0.948)
  the two profiles are of different devices: /device:TPU:0 before, /device:TPU:15 now
where the time goes in v3:
time: 219 us; the launch traced here: 217 us
  Pallas kernels  74.4 us (34%)
  starting transfers between devices  67.9 us (31%)
  waiting for transfers between devices  56.9 us (26%)
  matrix products  8.87 us (4%)
  local copies, waits for them, and re-layouts  6.58 us (3%)
    ppermute x17, starting transfers between devices, send(): return [lax.ppermute(a, 'chol', targets) for a in arrays]  38.1 us
    pallas_call x3, Pallas kernels, potential_rows(): pl.pallas_call(functools.partial(potential_kernel, slots), grid=(rows //...  33.2 us
    pallas_call x10, Pallas kernels, moved_rows(): pl.pallas_call(functools.partial(moved_kernel, choices), grid_spec=pltpu....  33.2 us
    ppermute x17, waiting for transfers between devices, send(): return [lax.ppermute(a, 'chol', targets) for a in arrays]  29.3 us
    all_to_all x4, starting transfers between devices, exchange(): lax.all_to_all(made, 'chol', 0, 0, axis_index_groups=groups, tiled=True)  24.4 us
    all_to_all x4, waiting for transfers between devices, exchange(): lax.all_to_all(made, 'chol', 0, 0, axis_index_groups=groups, tiled=True)  16.9 us
    ppermute x6, waiting for transfers between devices, butterfly_sum(): lax.ppermute(value, 'chol', [(i, i ^ k * step) for i in range(size)])  10.7 us
    dot_general x1, matrix products, on_device(): lax.dot_general(green.reshape(walkers, -1), chol_half.reshape(vectors, -1...  8.87 us
  transfers between devices with their start and end apart: 27, of which 10 were waited for; matrix products, arithmetic and copies ran while one was open for 6% of the time, Pallas kernels for 32%

profile of v3, /device:TPU:15, one launch (start us, length us, event | category | flops | bytes accessed | tf_op | source)
XLA Modules:
  0.0 217.5 jit_solution(6182828516455428458)
XLA Ops:
  4.3 3.2 %collective-permute-start.7 = (bf16[2,1024,256]{2,1,0:T(8,128)(2,1)}, bf16[2,1024,256]{2,1,0:T(8,128)(2,1)S(1)}, u32[]{:S(2)}, u32[]{:S(2)}) collective-permute-start(bf16[2,1024,256]{2,1,0:T(8,128)(2,1)} %shard_map.68.refs_0_), channel_id=1, source_target_pairs={{4,8},{5,9},{6,10},{7,11},{8,4},{9,5},{10,6},{11,7},{20,24},{21,25... | collective-permute-start | bytes 3145736 | tf_op jit(solution)/shard_map/ppermute | solution.py:185
  7.5 8.9 %fusion.3 = f32[64,128]{1,0:T(8,128)S(1)} fusion(bf16[128,64,256]{2,1,0:T(8,128)(2,1)} %param.6, bf16[64,64,256]{2,1,0:T(8,128)(2,1)S(1)} %copy-done.7), kind=kOutput, calls=%fused_computation.3 | convolution fusion | flops 268435456 | bytes 6324224 | tf_op jit(solution)/shard_map/dot_general | solution.py:197
  24.5 5.4 %collective-permute-done.3 = f32[64,128]{1,0:T(8,128)S(1)} collective-permute-done((f32[64,128]{1,0:T(8,128)S(1)}, f32[64,128]{1,0:T(8,128)S(1)}, u32[]{:S(2)}, u32[]{:S(2)}) %collective-permute-start.3) | collective-permute-done | bytes 32800 | tf_op jit(solution)/shard_map/ppermute | solution.py:27
  33.3 3.9 %collective-permute-start.10 = (bf16[2,1024,256]{2,1,0:T(8,128)(2,1)}, bf16[2,1024,256]{2,1,0:T(8,128)(2,1)}, u32[]{:S(2)}, u32[]{:S(2)}) collective-permute-start(bf16[2,1024,256]{2,1,0:T(8,128)(2,1)} %collective-permute-done.6.rest_0_.refs_0_), channel_id=1, source_target_pairs={{4,8},{5,9},{6,10},{7,11},{8,4},{9,5},{10,6},{11,7},{20,24},{21,25... | collective-permute-start | bytes 3145736 | tf_op jit(solution)/shard_map/ppermute | solution.py:185
  38.1 9.9 %shard_map.69.rest_0_ = bf16[16,64,1024]{2,1,0:T(8,128)(2,1)} custom-call(bf16[16,128]{1,0:T(8,128)(2,1)} %get-tuple-element.9.fields_ref, bf16[128,64,1024]{2,1,0:T(8,128)(2,1)} %chol_ref.5, bf16[2,1024,256]{2,1,0:T(8,128)(2,1)} %collective-permute-done.6.rest_0_.refs_0_, bf16[2,1024,256]{2,1,0:T(8,128)(2,1)} %copy-done.8), custom_call_target="tpu_custom_call" | custom-call | flops 60000002048 | bytes 1 | tf_op jit(solution)/shard_map/pallas_call | solution.py:65
  53.5 5.0 %collective-permute-start.12 = (bf16[2,1024,256]{2,1,0:T(8,128)(2,1)S(1)}, bf16[2,1024,256]{2,1,0:T(8,128)(2,1)S(1)}, u32[]{:S(2)}, u32[]{:S(2)}) collective-permute-start(bf16[2,1024,256]{2,1,0:T(8,128)(2,1)S(1)} %copy-done.9), channel_id=1, source_target_pairs={{4,0},{5,1},{6,2},{7,3},{8,12},{9,13},{10,14},{11,15},{20,16},{21,... | collective-permute-start | bytes 3145736 | tf_op jit(solution)/shard_map/ppermute | solution.py:185
  60.9 7.4 %all-to-all-start.2 = ((bf16[16,64,1024]{2,1,0:T(8,128)(2,1)}), bf16[16,64,1024]{2,1,0:T(8,128)(2,1)}, u32[]{:S(2)}, u32[]{:S(2)}) async-start(bf16[16,64,1024]{2,1,0:T(8,128)(2,1)} %shard_map.69.rest_0_), calls=%async_computation.2 | async-start | bytes 4194304 | tf_op jit(solution)/shard_map/all_to_all | solution.py:215
  68.3 2.3 %collective-permute-start.11 = (bf16[2,1024,256]{2,1,0:T(8,128)(2,1)}, bf16[2,1024,256]{2,1,0:T(8,128)(2,1)}, u32[]{:S(2)}, u32[]{:S(2)}) collective-permute-start(bf16[2,1024,256]{2,1,0:T(8,128)(2,1)} %collective-permute-done.10.rest_0_.refs_1_), channel_id=1, source_target_pairs={{4,0},{5,1},{6,2},{7,3},{8,12},{9,13},{10,14},{11,15},{20,16},{21,... | collective-permute-start | bytes 3145736 | tf_op jit(solution)/shard_map/ppermute | solution.py:185
  70.6 10.9 %collective-permute-done.8.rest_0_.refs_1_ = bf16[2,1024,256]{2,1,0:T(8,128)(2,1)} collective-permute-done((bf16[2,1024,256]{2,1,0:T(8,128)(2,1)}, bf16[2,1024,256]{2,1,0:T(8,128)(2,1)}, u32[]{:S(2)}, u32[]{:S(2)}) %collective-permute-start.8) | collective-permute-done | bytes 1048608 | tf_op jit(solution)/shard_map/ppermute | solution.py:185
  81.4 2.3 %collective-permute-start.14 = (bf16[2,1024,256]{2,1,0:T(8,128)(2,1)}, bf16[2,1024,256]{2,1,0:T(8,128)(2,1)}, u32[]{:S(2)}, u32[]{:S(2)}) collective-permute-start(bf16[2,1024,256]{2,1,0:T(8,128)(2,1)} %collective-permute-done.8.rest_0_.refs_1_), channel_id=1, source_target_pairs={{4,0},{5,1},{6,2},{7,3},{8,12},{9,13},{10,14},{11,15},{20,16},{21,... | collective-permute-start | bytes 3145736 | tf_op jit(solution)/shard_map/ppermute | solution.py:185
  83.7 3.5 %collective-permute-start.15 = (bf16[2,1024,256]{2,1,0:T(8,128)(2,1)}, bf16[2,1024,256]{2,1,0:T(8,128)(2,1)}, u32[]{:S(2)}, u32[]{:S(2)}) collective-permute-start(bf16[2,1024,256]{2,1,0:T(8,128)(2,1)} %collective-permute-done.9.rest_1_.refs_0_), channel_id=1, source_target_pairs={{4,8},{5,9},{6,10},{7,11},{8,4},{9,5},{10,6},{11,7},{20,24},{21,25... | collective-permute-start | bytes 3145736 | tf_op jit(solution)/shard_map/ppermute | solution.py:185
  88.2 10.0 %shard_map.72 = bf16[16,64,1024]{2,1,0:T(8,128)(2,1)} custom-call(bf16[16,128]{1,0:T(8,128)(2,1)} %get-tuple-element.8.fields_ref, bf16[128,64,1024]{2,1,0:T(8,128)(2,1)} %chol_ref.5, bf16[2,1024,256]{2,1,0:T(8,128)(2,1)} %collective-permute-done.10.rest_0_.refs_1_, bf16[2,1024,256]{2,1,0:T(8,128)(2,1)} %copy-done.10), custom_call_target="tpu_custom_call" | custom-call | flops 60000002048 | bytes 1 | tf_op jit(solution)/shard_map/pallas_call | solution.py:65
  98.2 6.5 %all-to-all-start.1 = ((bf16[16,64,1024]{2,1,0:T(8,128)(2,1)}), bf16[16,64,1024]{2,1,0:T(8,128)(2,1)S(1)}, u32[]{:S(2)}, u32[]{:S(2)}) async-start(bf16[16,64,1024]{2,1,0:T(8,128)(2,1)} %shard_map.72), calls=%async_computation.1 | async-start | bytes 4194304 | tf_op jit(solution)/shard_map/all_to_all | solution.py:215
  105.9 3.2 %shard_map.81 = bf16[2,256,256]{2,1,0:T(8,128)(2,1)} custom-call(s32[2]{0:T(128)} %pad_add_fusion.scalars, bf16[4,4,64,1024]{3,2,1,0:T(8,128)(2,1)} %bitcast.10.pieces, bf16[2,1024,256]{2,1,0:T(8,128)(2,1)} %collective-permute-done.9.rest_1_.refs_0_), custom_call_target="tpu_custom_call" | custom-call | flops 15000000512 | bytes 1 | tf_op jit(solution)/shard_map/pallas_call | solution.py:118
  109.1 6.0 %collective-permute-start.22 = (bf16[2,256,256]{2,1,0:T(8,128)(2,1)}, bf16[2,256,256]{2,1,0:T(8,128)(2,1)}, u32[]{:S(2)}, u32[]{:S(2)}) collective-permute-start(bf16[2,256,256]{2,1,0:T(8,128)(2,1)} %shard_map.81), channel_id=1, source_target_pairs={{4,0},{5,1},{6,2},{7,3},{8,12},{9,13},{10,14},{11,15},{20,16},{21,... | collective-permute-start | bytes 786440 | tf_op jit(solution)/shard_map/ppermute | solution.py:185
  115.1 3.2 %shard_map.76 = bf16[2,256,256]{2,1,0:T(8,128)(2,1)} custom-call(s32[2]{0:T(128)} %pad_add_fusion.scalars, bf16[4,4,64,1024]{3,2,1,0:T(8,128)(2,1)} %bitcast.10.pieces, bf16[2,1024,256]{2,1,0:T(8,128)(2,1)} %collective-permute-done.6.rest_0_.refs_0_), custom_call_target="tpu_custom_call" | custom-call | flops 15000000512 | bytes 1 | tf_op jit(solution)/shard_map/pallas_call | solution.py:118
  120.5 2.3 %collective-permute-start.20 = (bf16[2,1024,256]{2,1,0:T(8,128)(2,1)}, bf16[2,1024,256]{2,1,0:T(8,128)(2,1)}, u32[]{:S(2)}, u32[]{:S(2)}) collective-permute-start(bf16[2,1024,256]{2,1,0:T(8,128)(2,1)} %collective-permute-done.15.refs_1_), channel_id=1, source_target_pairs={{4,0},{5,1},{6,2},{7,3},{8,12},{9,13},{10,14},{11,15},{20,16},{21,... | collective-permute-start | bytes 3145736 | tf_op jit(solution)/shard_map/ppermute | solution.py:185
  122.8 13.4 %shard_map.71 = (bf16[16,64,1024]{2,1,0:T(8,128)(2,1)}, bf16[16,64,1024]{2,1,0:T(8,128)(2,1)}) custom-call(bf16[32,128]{1,0:T(8,128)(2,1)} %pad_maximum_fusion.fields_ref, bf16[128,64,1024]{2,1,0:T(8,128)(2,1)} %chol_ref.5, bf16[2,1024,256]{2,1,0:T(8,128)(2,1)} %collective-permute-done.8.rest_0_.refs_1_, ...), custom_call_target="tpu_custom_call" | custom-call | flops 60000002048 | bytes 1 | tf_op jit(solution)/shard_map/pallas_call | solution.py:65
  137.5 5.0 %all-to-all-start.3 = ((bf16[16,64,1024]{2,1,0:T(8,128)(2,1)}), bf16[16,64,1024]{2,1,0:T(8,128)(2,1)}, u32[]{:S(2)}, u32[]{:S(2)}) async-start(bf16[16,64,1024]{2,1,0:T(8,128)(2,1)} %get-tuple-element.5), calls=%async_computation.3 | async-start | bytes 4194304 | tf_op jit(solution)/shard_map/all_to_all | solution.py:215
  142.5 3.5 %shard_map.74.refs_2_.refs_3_ = bf16[2,256,256]{2,1,0:T(8,128)(2,1)} custom-call(s32[2]{0:T(128)} %pad_add_fusion.scalars, bf16[4,4,64,1024]{3,2,1,0:T(8,128)(2,1)} %bitcast.20, bf16[2,1024,256]{2,1,0:T(8,128)(2,1)} %collective-permute-done.14.refs_0_, bf16[2,1024,256]{2,1,0:T(8,128)(2,1)} %collective-permute-done.15.refs_1_, ...), custom_call_target="tpu_custom_call" | custom-call | flops 15000000512 | bytes 1 | tf_op jit(solution)/shard_map/pallas_call | solution.py:118
  146.0 3.5 %shard_map.73.refs_1_.refs_2_ = bf16[2,256,256]{2,1,0:T(8,128)(2,1)} custom-call(s32[2]{0:T(128)} %pad_add_fusion.scalars, bf16[4,4,64,1024]{3,2,1,0:T(8,128)(2,1)} %bitcast.21, bf16[2,1024,256]{2,1,0:T(8,128)(2,1)} %copy-done.10, bf16[2,1024,256]{2,1,0:T(8,128)(2,1)} %collective-permute-done.10.rest_0_.refs_1_, bf16[16,64,1024]{2,1,0:T(8,128)(2,1)} %get-tuple-element.4.refs_2_), custom_call_target="tpu_custom_call" | custom-call | flops 15000000512 | bytes 1 | tf_op jit(solution)/shard_map/pallas_call | solution.py:118
  149.5 16.9 %all-to-all-done.3 = bf16[16,64,1024]{2,1,0:T(8,128)(2,1)} async-done(((bf16[16,64,1024]{2,1,0:T(8,128)(2,1)}), bf16[16,64,1024]{2,1,0:T(8,128)(2,1)}, u32[]{:S(2)}, u32[]{:S(2)}) %all-to-all-start.3) | async-done | bytes 2097184 | tf_op jit(solution)/shard_map/all_to_all | solution.py:215
  166.4 5.5 %all-to-all-start = ((bf16[16,64,1024]{2,1,0:T(8,128)(2,1)}), bf16[16,64,1024]{2,1,0:T(8,128)(2,1)S(1)}, u32[]{:S(2)}, u32[]{:S(2)}) async-start(bf16[16,64,1024]{2,1,0:T(8,128)(2,1)} %get-tuple-element.4.refs_2_), calls=%async_computation | async-start | bytes 4194304 | tf_op jit(solution)/shard_map/all_to_all | solution.py:215
  171.9 3.6 %shard_map.78 = bf16[2,256,256]{2,1,0:T(8,128)(2,1)} custom-call(s32[2]{0:T(128)} %pad_add_fusion.scalars, bf16[4,4,64,1024]{3,2,1,0:T(8,128)(2,1)} %bitcast.12.pieces, bf16[2,1024,256]{2,1,0:T(8,128)(2,1)} %collective-permute-done.11.rest_2_.refs_0_, bf16[2,1024,256]{2,1,0:T(8,128)(2,1)} %copy-done.8, bf16[2,256,256]{2,1,0:T(8,128)(2,1)} %shard_map.73.refs_1_.refs_2_, ...), custom_call_target="tpu_custom_call" | custom-call | flops 15000000512 | bytes 1 | tf_op jit(solution)/shard_map/pallas_call | solution.py:118
  175.6 3.5 %shard_map.79 = bf16[2,256,256]{2,1,0:T(8,128)(2,1)} custom-call(s32[2]{0:T(128)} %pad_add_fusion.scalars, bf16[4,4,64,1024]{3,2,1,0:T(8,128)(2,1)} %bitcast.12.pieces, bf16[2,1024,256]{2,1,0:T(8,128)(2,1)} %collective-permute-done.20.refs_0_, bf16[2,1024,256]{2,1,0:T(8,128)(2,1)} %collective-permute-done.8.rest_0_.refs_1_, ...), custom_call_target="tpu_custom_call" | custom-call | flops 15000000512 | bytes 1 | tf_op jit(solution)/shard_map/pallas_call | solution.py:118
  179.1 3.2 %shard_map.82.refs_7_ = bf16[2,256,256]{2,1,0:T(8,128)(2,1)} custom-call(s32[2]{0:T(128)} %pad_add_fusion.1.scalars, bf16[4,4,64,1024]{3,2,1,0:T(8,128)(2,1)} %collective-permute-done.18.pieces, bf16[2,1024,256]{2,1,0:T(8,128)(2,1)} %shard_map.70.refs_0_, bf16[2,256,256]{2,1,0:T(8,128)(2,1)} %shard_map.73.refs_1_.refs_2_, ...), custom_call_target="tpu_custom_call" | custom-call | flops 15000000512 | bytes 1 | tf_op jit(solution)/shard_map/pallas_call | solution.py:118
  182.3 3.3 %shard_map.77.refs_2_ = bf16[2,256,256]{2,1,0:T(8,128)(2,1)} custom-call(s32[2]{0:T(128)} %pad_add_fusion.1.scalars, bf16[4,4,64,1024]{3,2,1,0:T(8,128)(2,1)} %collective-permute-done.18.pieces, bf16[2,1024,256]{2,1,0:T(8,128)(2,1)} %shard_map.68.refs_0_, bf16[2,256,256]{2,1,0:T(8,128)(2,1)} %shard_map.73.refs_1_.refs_2_, ...), custom_call_target="tpu_custom_call" | custom-call | flops 15000000512 | bytes 1 | tf_op jit(solution)/shard_map/pallas_call | solution.py:118
  187.1 11.0 %collective-permute-done.13.refs_1_.refs_3_ = bf16[2,256,256]{2,1,0:T(8,128)(2,1)S(1)} collective-permute-done((bf16[2,256,256]{2,1,0:T(8,128)(2,1)S(1)}, bf16[2,256,256]{2,1,0:T(8,128)(2,1)S(1)}, u32[]{:S(2)}, u32[]{:S(2)}) %collective-permute-start.13) | collective-permute-done | bytes 262176 | tf_op jit(solution)/shard_map/ppermute | solution.py:185
  199.5 3.2 %shard_map.75.refs_0_ = bf16[2,256,256]{2,1,0:T(8,128)(2,1)} custom-call(s32[2]{0:T(128)} %pad_add_fusion.scalars, bf16[4,4,64,1024]{3,2,1,0:T(8,128)(2,1)} %bitcast.18, bf16[2,1024,256]{2,1,0:T(8,128)(2,1)} %shard_map.68.refs_0_, bf16[2,256,256]{2,1,0:T(8,128)(2,1)} %copy-done.3, bf16[2,256,256]{2,1,0:T(8,128)(2,1)} %copy-done.2), custom_call_target="tpu_custom_call" | custom-call | flops 15000000512 | bytes 1 | tf_op jit(solution)/shard_map/pallas_call | solution.py:118
  204.4 5.6 %collective-permute-done.19.refs_1_.refs_4_ = bf16[2,256,256]{2,1,0:T(8,128)(2,1)S(1)} collective-permute-done((bf16[2,256,256]{2,1,0:T(8,128)(2,1)S(1)}, bf16[2,256,256]{2,1,0:T(8,128)(2,1)S(1)}, u32[]{:S(2)}, u32[]{:S(2)}) %collective-permute-start.19) | collective-permute-done | bytes 262176 | tf_op jit(solution)/shard_map/ppermute | solution.py:185
  210.7 3.2 %shard_map.80.refs_5_ = bf16[2,256,256]{2,1,0:T(8,128)(2,1)} custom-call(s32[2]{0:T(128)} %pad_add_fusion.scalars, bf16[4,4,64,1024]{3,2,1,0:T(8,128)(2,1)} %bitcast.19, bf16[2,1024,256]{2,1,0:T(8,128)(2,1)} %shard_map.70.refs_0_, bf16[2,256,256]{2,1,0:T(8,128)(2,1)} %copy-done.5, bf16[2,256,256]{2,1,0:T(8,128)(2,1)} %copy-done.4), custom_call_target="tpu_custom_call" | custom-call | flops 15000000512 | bytes 1 | tf_op jit(solution)/shard_map/pallas_call | solution.py:118
  213.9 3.5 %shard_map.83 = bf16[4,1024,256]{2,1,0:T(8,128)(2,1)} custom-call(s32[2]{0:T(128)} %pad_add_fusion.scalars, bf16[2,256,256]{2,1,0:T(8,128)(2,1)} %shard_map.75.refs_0_, bf16[2,256,256]{2,1,0:T(8,128)(2,1)} %collective-permute-done.17.refs_1_, bf16[2,256,256]{2,1,0:T(8,128)(2,1)} %shard_map.77.refs_2_, bf16[2,256,256]{2,1,0:T(8,128)(2,1)} %copy-done.3, ...), custom_call_target="tpu_custom_call" | custom-call | tf_op jit(solution)/shard_map/pallas_call | solution.py:155
  (73 shorter events, 35.1 us)
Async XLA Ops:
  0.6 6.9 %copy-start.7 = (bf16[64,64,256]{2,1,0:T(8,128)(2,1)S(1)}, bf16[64,64,256]{2,1,0:T(8,128)(2,1)}, u32[]{:S(2)}) copy-start(bf16[64,64,256]{2,1,0:T(8,128)(2,1)} %param.7) | copy-start | bytes 6291460
  2.8 29.7 %copy-start.6 = (f32[64,128]{1,0:T(8,128)S(1)}, f32[64,128]{1,0:T(8,128)}, u32[]{:S(2)}) copy-start(f32[64,128]{1,0:T(8,128)} %param.8) | copy-start | bytes 98308
  2.9 30.4 %collective-permute-start.6 = (bf16[2,1024,256]{2,1,0:T(8,128)(2,1)}, bf16[2,1024,256]{2,1,0:T(8,128)(2,1)}, u32[]{:S(2)}, u32[]{:S(2)}) collective-permute-start(bf16[2,1024,256]{2,1,0:T(8,128)(2,1)} %shard_map.68.refs_0_), channel_id=1, source_target_pairs={{0,4},{1,5},{2,6},{3,7},{12,8},{13,9},{14,10},{15,11},{16,20},{17,... | collective-permute-start | bytes 3145736 | tf_op jit(solution)/shard_map/ppermute | solution.py:185
  4.3 32.9 %collective-permute-start.7 = (bf16[2,1024,256]{2,1,0:T(8,128)(2,1)}, bf16[2,1024,256]{2,1,0:T(8,128)(2,1)S(1)}, u32[]{:S(2)}, u32[]{:S(2)}) collective-permute-start(bf16[2,1024,256]{2,1,0:T(8,128)(2,1)} %shard_map.68.refs_0_), channel_id=1, source_target_pairs={{4,8},{5,9},{6,10},{7,11},{8,4},{9,5},{10,6},{11,7},{20,24},{21,25... | collective-permute-start | bytes 3145736 | tf_op jit(solution)/shard_map/ppermute | solution.py:185
  16.4 2.7 %collective-permute-start = (f32[64,128]{1,0:T(8,128)S(1)}, f32[64,128]{1,0:T(8,128)S(1)}, u32[]{:S(2)}, u32[]{:S(2)}) collective-permute-start(f32[64,128]{1,0:T(8,128)S(1)} %fusion.3), channel_id=1, source_target_pairs={{0,1},{1,0},{2,3},{3,2},{4,5},{5,4},{6,7},{7,6},{8,9},{9,8},{10,11... | collective-permute-start | bytes 98312 | tf_op jit(solution)/shard_map/ppermute | solution.py:27
  17.4 3.2 %collective-permute-start.1 = (f32[64,128]{1,0:T(8,128)S(1)}, f32[64,128]{1,0:T(8,128)S(1)}, u32[]{:S(2)}, u32[]{:S(2)}) collective-permute-start(f32[64,128]{1,0:T(8,128)S(1)} %fusion.3), channel_id=1, source_target_pairs={{0,2},{1,3},{2,0},{3,1},{4,6},{5,7},{6,4},{7,5},{8,10},{9,11},{10,... | collective-permute-start | bytes 98312 | tf_op jit(solution)/shard_map/ppermute | solution.py:27
  17.6 4.1 %collective-permute-start.2 = (f32[64,128]{1,0:T(8,128)S(1)}, f32[64,128]{1,0:T(8,128)S(1)}, u32[]{:S(2)}, u32[]{:S(2)}) collective-permute-start(f32[64,128]{1,0:T(8,128)S(1)} %fusion.3), channel_id=1, source_target_pairs={{0,3},{1,2},{2,1},{3,0},{4,7},{5,6},{6,5},{7,4},{8,11},{9,10},{10,... | collective-permute-start | bytes 98312 | tf_op jit(solution)/shard_map/ppermute | solution.py:27
  21.7 8.2 %collective-permute-start.3 = (f32[64,128]{1,0:T(8,128)S(1)}, f32[64,128]{1,0:T(8,128)S(1)}, u32[]{:S(2)}, u32[]{:S(2)}) collective-permute-start(f32[64,128]{1,0:T(8,128)S(1)} %add_add_fusion), channel_id=1, source_target_pairs={{0,4},{1,5},{2,6},{3,7},{4,0},{5,1},{6,2},{7,3},{8,12},{9,13},{10,... | collective-permute-start | bytes 98312 | tf_op jit(solution)/shard_map/ppermute | solution.py:27
  22.0 9.2 %collective-permute-start.4 = (f32[64,128]{1,0:T(8,128)S(1)}, f32[64,128]{1,0:T(8,128)S(1)}, u32[]{:S(2)}, u32[]{:S(2)}) collective-permute-start(f32[64,128]{1,0:T(8,128)S(1)} %add_add_fusion), channel_id=1, source_target_pairs={{0,8},{1,9},{2,10},{3,11},{4,12},{5,13},{6,14},{7,15},{8,0},{9,1},... | collective-permute-start | bytes 98312 | tf_op jit(solution)/shard_map/ppermute | solution.py:27
  23.2 9.3 %collective-permute-start.5 = (f32[64,128]{1,0:T(8,128)S(1)}, f32[64,128]{1,0:T(8,128)S(1)}, u32[]{:S(2)}, u32[]{:S(2)}) collective-permute-start(f32[64,128]{1,0:T(8,128)S(1)} %add_add_fusion), channel_id=1, source_target_pairs={{0,12},{1,13},{2,14},{3,15},{4,8},{5,9},{6,10},{7,11},{8,4},{9,5},... | collective-permute-start | bytes 98312 | tf_op jit(solution)/shard_map/ppermute | solution.py:27
  33.3 35.0 %collective-permute-start.10 = (bf16[2,1024,256]{2,1,0:T(8,128)(2,1)}, bf16[2,1024,256]{2,1,0:T(8,128)(2,1)}, u32[]{:S(2)}, u32[]{:S(2)}) collective-permute-start(bf16[2,1024,256]{2,1,0:T(8,128)(2,1)} %collective-permute-done.6.rest_0_.refs_0_), channel_id=1, source_target_pairs={{4,8},{5,9},{6,10},{7,11},{8,4},{9,5},{10,6},{11,7},{20,24},{21,25... | collective-permute-start | bytes 3145736 | tf_op jit(solution)/shard_map/ppermute | solution.py:185
  48.0 5.4 %copy-start.9 = (bf16[2,1024,256]{2,1,0:T(8,128)(2,1)S(1)}, bf16[2,1024,256]{2,1,0:T(8,128)(2,1)}, u32[]{:S(2)}) copy-start(bf16[2,1024,256]{2,1,0:T(8,128)(2,1)} %copy-done.8) | copy-start | bytes 3145732
  50.2 31.2 %collective-permute-start.8 = (bf16[2,1024,256]{2,1,0:T(8,128)(2,1)}, bf16[2,1024,256]{2,1,0:T(8,128)(2,1)}, u32[]{:S(2)}, u32[]{:S(2)}) collective-permute-start(bf16[2,1024,256]{2,1,0:T(8,128)(2,1)} %shard_map.70.refs_0_), channel_id=1, source_target_pairs={{4,8},{5,9},{6,10},{7,11},{8,4},{9,5},{10,6},{11,7},{20,24},{21,25... | collective-permute-start | bytes 3145736 | tf_op jit(solution)/shard_map/ppermute | solution.py:185
  52.2 31.5 %collective-permute-start.9 = (bf16[2,1024,256]{2,1,0:T(8,128)(2,1)}, bf16[2,1024,256]{2,1,0:T(8,128)(2,1)}, u32[]{:S(2)}, u32[]{:S(2)}) collective-permute-start(bf16[2,1024,256]{2,1,0:T(8,128)(2,1)} %shard_map.70.refs_0_), channel_id=1, source_target_pairs={{0,4},{1,5},{2,6},{3,7},{12,8},{13,9},{14,10},{15,11},{16,20},{17,... | collective-permute-start | bytes 3145736 | tf_op jit(solution)/shard_map/ppermute | solution.py:185
  53.5 33.7 %collective-permute-start.12 = (bf16[2,1024,256]{2,1,0:T(8,128)(2,1)S(1)}, bf16[2,1024,256]{2,1,0:T(8,128)(2,1)S(1)}, u32[]{:S(2)}, u32[]{:S(2)}) collective-permute-start(bf16[2,1024,256]{2,1,0:T(8,128)(2,1)S(1)} %copy-done.9), channel_id=1, source_target_pairs={{4,0},{5,1},{6,2},{7,3},{8,12},{9,13},{10,14},{11,15},{20,16},{21,... | collective-permute-start | bytes 3145736 | tf_op jit(solution)/shard_map/ppermute | solution.py:185
  60.9 37.3 %all-to-all-start.2 = ((bf16[16,64,1024]{2,1,0:T(8,128)(2,1)}), bf16[16,64,1024]{2,1,0:T(8,128)(2,1)}, u32[]{:S(2)}, u32[]{:S(2)}) async-start(bf16[16,64,1024]{2,1,0:T(8,128)(2,1)} %shard_map.69.rest_0_), calls=%async_computation.2 | async-start | bytes 4194304 | tf_op jit(solution)/shard_map/all_to_all | solution.py:215
  68.3 50.0 %collective-permute-start.11 = (bf16[2,1024,256]{2,1,0:T(8,128)(2,1)}, bf16[2,1024,256]{2,1,0:T(8,128)(2,1)}, u32[]{:S(2)}, u32[]{:S(2)}) collective-permute-start(bf16[2,1024,256]{2,1,0:T(8,128)(2,1)} %collective-permute-done.10.rest_0_.refs_1_), channel_id=1, source_target_pairs={{4,0},{5,1},{6,2},{7,3},{8,12},{9,13},{10,14},{11,15},{20,16},{21,... | collective-permute-start | bytes 3145736 | tf_op jit(solution)/shard_map/ppermute | solution.py:185
  81.4 61.1 %collective-permute-start.14 = (bf16[2,1024,256]{2,1,0:T(8,128)(2,1)}, bf16[2,1024,256]{2,1,0:T(8,128)(2,1)}, u32[]{:S(2)}, u32[]{:S(2)}) collective-permute-start(bf16[2,1024,256]{2,1,0:T(8,128)(2,1)} %collective-permute-done.8.rest_0_.refs_1_), channel_id=1, source_target_pairs={{4,0},{5,1},{6,2},{7,3},{8,12},{9,13},{10,14},{11,15},{20,16},{21,... | collective-permute-start | bytes 3145736 | tf_op jit(solution)/shard_map/ppermute | solution.py:185
  83.7 36.8 %collective-permute-start.15 = (bf16[2,1024,256]{2,1,0:T(8,128)(2,1)}, bf16[2,1024,256]{2,1,0:T(8,128)(2,1)}, u32[]{:S(2)}, u32[]{:S(2)}) collective-permute-start(bf16[2,1024,256]{2,1,0:T(8,128)(2,1)} %collective-permute-done.9.rest_1_.refs_0_), channel_id=1, source_target_pairs={{4,8},{5,9},{6,10},{7,11},{8,4},{9,5},{10,6},{11,7},{20,24},{21,25... | collective-permute-start | bytes 3145736 | tf_op jit(solution)/shard_map/ppermute | solution.py:185
  98.2 38.0 %all-to-all-start.1 = ((bf16[16,64,1024]{2,1,0:T(8,128)(2,1)}), bf16[16,64,1024]{2,1,0:T(8,128)(2,1)S(1)}, u32[]{:S(2)}, u32[]{:S(2)}) async-start(bf16[16,64,1024]{2,1,0:T(8,128)(2,1)} %shard_map.72), calls=%async_computation.1 | async-start | bytes 4194304 | tf_op jit(solution)/shard_map/all_to_all | solution.py:215
  104.6 74.4 %collective-permute-start.18 = (bf16[4,4,64,1024]{3,2,1,0:T(8,128)(2,1)}, bf16[4,4,64,1024]{3,2,1,0:T(8,128)(2,1)}, u32[]{:S(2)}, u32[]{:S(2)}) collective-permute-start(bf16[4,4,64,1024]{3,2,1,0:T(8,128)(2,1)} %bitcast.10.pieces), channel_id=1, source_target_pairs={{0,4},{1,5},{2,6},{3,7},{12,8},{13,9},{14,10},{15,11},{16,20},{17,... | collective-permute-start | bytes 6291464 | tf_op jit(solution)/shard_map/ppermute | solution.py:185
  109.1 104.8 %collective-permute-start.22 = (bf16[2,256,256]{2,1,0:T(8,128)(2,1)}, bf16[2,256,256]{2,1,0:T(8,128)(2,1)}, u32[]{:S(2)}, u32[]{:S(2)}) collective-permute-start(bf16[2,256,256]{2,1,0:T(8,128)(2,1)} %shard_map.81), channel_id=1, source_target_pairs={{4,0},{5,1},{6,2},{7,3},{8,12},{9,13},{10,14},{11,15},{20,16},{21,... | collective-permute-start | bytes 786440 | tf_op jit(solution)/shard_map/ppermute | solution.py:185
  118.3 95.6 %collective-permute-start.17 = (bf16[2,256,256]{2,1,0:T(8,128)(2,1)}, bf16[2,256,256]{2,1,0:T(8,128)(2,1)}, u32[]{:S(2)}, u32[]{:S(2)}) collective-permute-start(bf16[2,256,256]{2,1,0:T(8,128)(2,1)} %shard_map.76), channel_id=1, source_target_pairs={{4,0},{5,1},{6,2},{7,3},{8,12},{9,13},{10,14},{11,15},{20,16},{21,... | collective-permute-start | bytes 786440 | tf_op jit(solution)/shard_map/ppermute | solution.py:185
  120.5 55.0 %collective-permute-start.20 = (bf16[2,1024,256]{2,1,0:T(8,128)(2,1)}, bf16[2,1024,256]{2,1,0:T(8,128)(2,1)}, u32[]{:S(2)}, u32[]{:S(2)}) collective-permute-start(bf16[2,1024,256]{2,1,0:T(8,128)(2,1)} %collective-permute-done.15.refs_1_), channel_id=1, source_target_pairs={{4,0},{5,1},{6,2},{7,3},{8,12},{9,13},{10,14},{11,15},{20,16},{21,... | collective-permute-start | bytes 3145736 | tf_op jit(solution)/shard_map/ppermute | solution.py:185
  137.5 28.9 %all-to-all-start.3 = ((bf16[16,64,1024]{2,1,0:T(8,128)(2,1)}), bf16[16,64,1024]{2,1,0:T(8,128)(2,1)}, u32[]{:S(2)}, u32[]{:S(2)}) async-start(bf16[16,64,1024]{2,1,0:T(8,128)(2,1)} %get-tuple-element.5), calls=%async_computation.3 | async-start | bytes 4194304 | tf_op jit(solution)/shard_map/all_to_all | solution.py:215
  146.0 39.6 %collective-permute-start.16 = (bf16[2,256,256]{2,1,0:T(8,128)(2,1)}, bf16[2,256,256]{2,1,0:T(8,128)(2,1)S(1)}, u32[]{:S(2)}, u32[]{:S(2)}) collective-permute-start(bf16[2,256,256]{2,1,0:T(8,128)(2,1)} %shard_map.74.refs_2_.refs_3_), channel_id=1, source_target_pairs={{0,8},{1,9},{2,10},{3,11},{8,0},{9,1},{10,2},{11,3},{4,12},{5,13},... | collective-permute-start | bytes 786440 | tf_op jit(solution)/shard_map/ppermute | solution.py:185
  166.4 31.7 %all-to-all-start = ((bf16[16,64,1024]{2,1,0:T(8,128)(2,1)}), bf16[16,64,1024]{2,1,0:T(8,128)(2,1)S(1)}, u32[]{:S(2)}, u32[]{:S(2)}) async-start(bf16[16,64,1024]{2,1,0:T(8,128)(2,1)} %get-tuple-element.4.refs_2_), calls=%async_computation | async-start | bytes 4194304 | tf_op jit(solution)/shard_map/all_to_all | solution.py:215
  175.5 22.6 %collective-permute-start.13 = (bf16[2,256,256]{2,1,0:T(8,128)(2,1)S(1)}, bf16[2,256,256]{2,1,0:T(8,128)(2,1)S(1)}, u32[]{:S(2)}, u32[]{:S(2)}) collective-permute-start(bf16[2,256,256]{2,1,0:T(8,128)(2,1)S(1)} %copy-done.12), channel_id=1, source_target_pairs={{0,8},{1,9},{2,10},{3,11},{8,0},{9,1},{10,2},{11,3},{4,12},{5,13},... | collective-permute-start | bytes 786440 | tf_op jit(solution)/shard_map/ppermute | solution.py:185
  179.1 25.4 %collective-permute-start.21 = (bf16[2,256,256]{2,1,0:T(8,128)(2,1)}, bf16[2,256,256]{2,1,0:T(8,128)(2,1)S(1)}, u32[]{:S(2)}, u32[]{:S(2)}) collective-permute-start(bf16[2,256,256]{2,1,0:T(8,128)(2,1)} %shard_map.79), channel_id=1, source_target_pairs={{0,12},{1,13},{2,14},{3,15},{12,0},{13,1},{14,2},{15,3},{4,8},{5,9... | collective-permute-start | bytes 786440 | tf_op jit(solution)/shard_map/ppermute | solution.py:185
  185.5 12.5 %copy-start.2 = (bf16[2,256,256]{2,1,0:T(8,128)(2,1)}, bf16[2,256,256]{2,1,0:T(8,128)(2,1)S(1)}, u32[]{:S(2)}) copy-start(bf16[2,256,256]{2,1,0:T(8,128)(2,1)S(1)} %collective-permute-done.16.refs_2_.refs_8_) | copy-start | bytes 786436
  185.6 24.5 %collective-permute-start.19 = (bf16[2,256,256]{2,1,0:T(8,128)(2,1)S(1)}, bf16[2,256,256]{2,1,0:T(8,128)(2,1)S(1)}, u32[]{:S(2)}, u32[]{:S(2)}) collective-permute-start(bf16[2,256,256]{2,1,0:T(8,128)(2,1)S(1)} %copy-done.11), channel_id=1, source_target_pairs={{0,12},{1,13},{2,14},{3,15},{12,0},{13,1},{14,2},{15,3},{4,8},{5,9... | collective-permute-start | bytes 786440 | tf_op jit(solution)/shard_map/ppermute | solution.py:185
  204.4 5.6 %copy-start.4 = (bf16[2,256,256]{2,1,0:T(8,128)(2,1)}, bf16[2,256,256]{2,1,0:T(8,128)(2,1)S(1)}, u32[]{:S(2)}) copy-start(bf16[2,256,256]{2,1,0:T(8,128)(2,1)S(1)} %collective-permute-done.21.refs_2_.refs_9_) | copy-start | bytes 786436
  (8 other events, 13.0 us)

commit v4 on v3

--- a/solution.py
+++ b/solution.py
@@ -237,8 +237,7 @@
     cross = send(cross, along([(0, 2), (2, 0), (1, 3), (3, 1)]))
     next_to = send(next_to, outward)
     pieces = exchange(made[1])
-    home = [moved(pieces, [own[first]], plane, first, cross)]
-    home.append(moved(pieces, [own[second]], plane, second, mirror))
+    home = [moved(pieces, [own[i]], plane, i, [*cross, mirror[first]]) for i in range(parts)]
     return (join_rows(scalars(plane), list(zip(home, next_to, landed, cross, mirror))), log_factor)
 
 

time: 219 us -> 209 us (0.954)
  waiting for transfers between devices: 56.9 us -> 47.4 us
  local copies, waits for them, and re-layouts: 6.58 us -> 4.29 us
    ppermute x17, waiting for transfers between devices: 29.3 us -> 16.2 us  [send(): return [lax.ppermute(a, 'chol', targets) for a in arrays]]
    all_to_all x4, waiting for transfers between devices: 16.9 us -> 20.4 us  [exchange(): lax.all_to_all(made, 'chol', 0, 0, axis_index_groups=groups, tiled=True)]
    unnamed x26 -> x20, local copies, waits for them, and re-layouts: 5.38 us -> 3.09 us
  transfers between devices with their start and end apart: 27 -> 27, of which waited for: 10 -> 9; matrix products, arithmetic and copies ran while one was open for 6% -> 6% of each run, Pallas kernels for 32% -> 33%
where the time goes in v4:
time: 209 us; the launch traced here: 206 us
  Pallas kernels  74 us (35%)
  starting transfers between devices  68.8 us (33%)
  waiting for transfers between devices  47.4 us (23%)
  matrix products  8.87 us (4%)
  local copies, waits for them, and re-layouts  4.29 us (2%)
    ppermute x17, starting transfers between devices, send(): return [lax.ppermute(a, 'chol', targets) for a in arrays]  39 us
    pallas_call x3, Pallas kernels, potential_rows(): pl.pallas_call(functools.partial(potential_kernel, slots), grid=(rows //...  33.2 us
    pallas_call x10, Pallas kernels, moved_rows(): pl.pallas_call(functools.partial(moved_kernel, choices), grid_spec=pltpu....  32.9 us
    all_to_all x4, starting transfers between devices, exchange(): lax.all_to_all(made, 'chol', 0, 0, axis_index_groups=groups, tiled=True)  24.4 us
    all_to_all x4, waiting for transfers between devices, exchange(): lax.all_to_all(made, 'chol', 0, 0, axis_index_groups=groups, tiled=True)  20.4 us
    ppermute x17, waiting for transfers between devices, send(): return [lax.ppermute(a, 'chol', targets) for a in arrays]  16.2 us
    ppermute x6, waiting for transfers between devices, butterfly_sum(): lax.ppermute(value, 'chol', [(i, i ^ k * step) for i in range(size)])  10.7 us
    dot_general x1, matrix products, on_device(): lax.dot_general(green.reshape(walkers, -1), chol_half.reshape(vectors, -1...  8.87 us
  transfers between devices with their start and end apart: 27, of which 9 were waited for; matrix products, arithmetic and copies ran while one was open for 6% of the time, Pallas kernels for 33%

profile of v4, /device:TPU:15, one launch (start us, length us, event | category | flops | bytes accessed | tf_op | source)
XLA Modules:
  0.0 206.1 jit_solution(12431421851497024486)
XLA Ops:
  4.3 3.2 %collective-permute-start.7 = (bf16[2,1024,256]{2,1,0:T(8,128)(2,1)}, bf16[2,1024,256]{2,1,0:T(8,128)(2,1)S(1)}, u32[]{:S(2)}, u32[]{:S(2)}) collective-permute-start(bf16[2,1024,256]{2,1,0:T(8,128)(2,1)} %shard_map.68.refs_0_), channel_id=1, source_target_pairs={{4,8},{5,9},{6,10},{7,11},{8,4},{9,5},{10,6},{11,7},{20,24},{21,25... | collective-permute-start | bytes 3145736 | tf_op jit(solution)/shard_map/ppermute | solution.py:185
  7.5 8.9 %fusion.3 = f32[64,128]{1,0:T(8,128)S(1)} fusion(bf16[128,64,256]{2,1,0:T(8,128)(2,1)} %param.6, bf16[64,64,256]{2,1,0:T(8,128)(2,1)S(1)} %copy-done.7), kind=kOutput, calls=%fused_computation.3 | convolution fusion | flops 268435456 | bytes 6324224 | tf_op jit(solution)/shard_map/dot_general | solution.py:197
  24.5 5.4 %collective-permute-done.3 = f32[64,128]{1,0:T(8,128)S(1)} collective-permute-done((f32[64,128]{1,0:T(8,128)S(1)}, f32[64,128]{1,0:T(8,128)S(1)}, u32[]{:S(2)}, u32[]{:S(2)}) %collective-permute-start.3) | collective-permute-done | bytes 32800 | tf_op jit(solution)/shard_map/ppermute | solution.py:27
  33.3 3.9 %collective-permute-start.10 = (bf16[2,1024,256]{2,1,0:T(8,128)(2,1)}, bf16[2,1024,256]{2,1,0:T(8,128)(2,1)}, u32[]{:S(2)}, u32[]{:S(2)}) collective-permute-start(bf16[2,1024,256]{2,1,0:T(8,128)(2,1)} %collective-permute-done.6.rest_0_.refs_0_), channel_id=1, source_target_pairs={{4,8},{5,9},{6,10},{7,11},{8,4},{9,5},{10,6},{11,7},{20,24},{21,25... | collective-permute-start | bytes 3145736 | tf_op jit(solution)/shard_map/ppermute | solution.py:185
  38.2 9.9 %shard_map.69.rest_0_ = bf16[16,64,1024]{2,1,0:T(8,128)(2,1)} custom-call(bf16[16,128]{1,0:T(8,128)(2,1)} %get-tuple-element.9.fields_ref, bf16[128,64,1024]{2,1,0:T(8,128)(2,1)} %chol_ref.5, bf16[2,1024,256]{2,1,0:T(8,128)(2,1)} %collective-permute-done.6.rest_0_.refs_0_, bf16[2,1024,256]{2,1,0:T(8,128)(2,1)} %copy-done.8), custom_call_target="tpu_custom_call" | custom-call | flops 60000002048 | bytes 1 | tf_op jit(solution)/shard_map/pallas_call | solution.py:65
  53.5 5.9 %collective-permute-start.12 = (bf16[2,1024,256]{2,1,0:T(8,128)(2,1)S(1)}, bf16[2,1024,256]{2,1,0:T(8,128)(2,1)}, u32[]{:S(2)}, u32[]{:S(2)}) collective-permute-start(bf16[2,1024,256]{2,1,0:T(8,128)(2,1)S(1)} %copy-done.9), channel_id=1, source_target_pairs={{4,0},{5,1},{6,2},{7,3},{8,12},{9,13},{10,14},{11,15},{20,16},{21,... | collective-permute-start | bytes 3145736 | tf_op jit(solution)/shard_map/ppermute | solution.py:185
  61.8 6.5 %all-to-all-start.3 = ((bf16[16,64,1024]{2,1,0:T(8,128)(2,1)}), bf16[16,64,1024]{2,1,0:T(8,128)(2,1)S(1)}, u32[]{:S(2)}, u32[]{:S(2)}) async-start(bf16[16,64,1024]{2,1,0:T(8,128)(2,1)} %shard_map.69.rest_0_), calls=%async_computation.3 | async-start | bytes 4194304 | tf_op jit(solution)/shard_map/all_to_all | solution.py:215
  68.4 2.3 %collective-permute-start.11 = (bf16[2,1024,256]{2,1,0:T(8,128)(2,1)}, bf16[2,1024,256]{2,1,0:T(8,128)(2,1)}, u32[]{:S(2)}, u32[]{:S(2)}) collective-permute-start(bf16[2,1024,256]{2,1,0:T(8,128)(2,1)} %collective-permute-done.10.rest_0_.refs_1_), channel_id=1, source_target_pairs={{4,0},{5,1},{6,2},{7,3},{8,12},{9,13},{10,14},{11,15},{20,16},{21,... | collective-permute-start | bytes 3145736 | tf_op jit(solution)/shard_map/ppermute | solution.py:185
  70.7 10.8 %collective-permute-done.8.rest_0_.refs_1_ = bf16[2,1024,256]{2,1,0:T(8,128)(2,1)} collective-permute-done((bf16[2,1024,256]{2,1,0:T(8,128)(2,1)}, bf16[2,1024,256]{2,1,0:T(8,128)(2,1)}, u32[]{:S(2)}, u32[]{:S(2)}) %collective-permute-start.8) | collective-permute-done | bytes 1048608 | tf_op jit(solution)/shard_map/ppermute | solution.py:185
  81.4 2.3 %collective-permute-start.14 = (bf16[2,1024,256]{2,1,0:T(8,128)(2,1)}, bf16[2,1024,256]{2,1,0:T(8,128)(2,1)}, u32[]{:S(2)}, u32[]{:S(2)}) collective-permute-start(bf16[2,1024,256]{2,1,0:T(8,128)(2,1)} %collective-permute-done.8.rest_0_.refs_1_), channel_id=1, source_target_pairs={{4,0},{5,1},{6,2},{7,3},{8,12},{9,13},{10,14},{11,15},{20,16},{21,... | collective-permute-start | bytes 3145736 | tf_op jit(solution)/shard_map/ppermute | solution.py:185
  83.7 3.5 %collective-permute-start.15 = (bf16[2,1024,256]{2,1,0:T(8,128)(2,1)}, bf16[2,1024,256]{2,1,0:T(8,128)(2,1)}, u32[]{:S(2)}, u32[]{:S(2)}) collective-permute-start(bf16[2,1024,256]{2,1,0:T(8,128)(2,1)} %collective-permute-done.9.rest_1_.refs_0_), channel_id=1, source_target_pairs={{4,8},{5,9},{6,10},{7,11},{8,4},{9,5},{10,6},{11,7},{20,24},{21,25... | collective-permute-start | bytes 3145736 | tf_op jit(solution)/shard_map/ppermute | solution.py:185
  87.2 10.0 %shard_map.72 = bf16[16,64,1024]{2,1,0:T(8,128)(2,1)} custom-call(bf16[16,128]{1,0:T(8,128)(2,1)} %get-tuple-element.8.fields_ref, bf16[128,64,1024]{2,1,0:T(8,128)(2,1)} %chol_ref.5, bf16[2,1024,256]{2,1,0:T(8,128)(2,1)} %collective-permute-done.10.rest_0_.refs_1_, bf16[2,1024,256]{2,1,0:T(8,128)(2,1)} %collective-permute-done.12.rest_1_.refs_0_), custom_call_target="tpu_custom_call" | custom-call | flops 60000002048 | bytes 1 | tf_op jit(solution)/shard_map/pallas_call | solution.py:65
  97.2 7.3 %all-to-all-start.1 = ((bf16[16,64,1024]{2,1,0:T(8,128)(2,1)}), bf16[16,64,1024]{2,1,0:T(8,128)(2,1)}, u32[]{:S(2)}, u32[]{:S(2)}) async-start(bf16[16,64,1024]{2,1,0:T(8,128)(2,1)} %shard_map.72), calls=%async_computation.1 | async-start | bytes 4194304 | tf_op jit(solution)/shard_map/all_to_all | solution.py:215
  105.8 3.2 %shard_map.80 = bf16[2,256,256]{2,1,0:T(8,128)(2,1)} custom-call(s32[2]{0:T(128)} %pad_add_fusion.scalars, bf16[4,4,64,1024]{3,2,1,0:T(8,128)(2,1)} %bitcast.19, bf16[2,1024,256]{2,1,0:T(8,128)(2,1)} %collective-permute-done.9.rest_1_.refs_0_), custom_call_target="tpu_custom_call" | custom-call | flops 15000000512 | bytes 1 | tf_op jit(solution)/shard_map/pallas_call | solution.py:118
  109.0 6.0 %collective-permute-start.20 = (bf16[2,256,256]{2,1,0:T(8,128)(2,1)}, bf16[2,256,256]{2,1,0:T(8,128)(2,1)}, u32[]{:S(2)}, u32[]{:S(2)}) collective-permute-start(bf16[2,256,256]{2,1,0:T(8,128)(2,1)} %shard_map.80), channel_id=1, source_target_pairs={{4,0},{5,1},{6,2},{7,3},{8,12},{9,13},{10,14},{11,15},{20,16},{21,... | collective-permute-start | bytes 786440 | tf_op jit(solution)/shard_map/ppermute | solution.py:185
  115.0 3.2 %shard_map.77 = bf16[2,256,256]{2,1,0:T(8,128)(2,1)} custom-call(s32[2]{0:T(128)} %pad_add_fusion.scalars, bf16[4,4,64,1024]{3,2,1,0:T(8,128)(2,1)} %bitcast.20, bf16[2,1024,256]{2,1,0:T(8,128)(2,1)} %collective-permute-done.6.rest_0_.refs_0_), custom_call_target="tpu_custom_call" | custom-call | flops 15000000512 | bytes 1 | tf_op jit(solution)/shard_map/pallas_call | solution.py:118
  120.1 2.4 %collective-permute-start.21 = (bf16[2,1024,256]{2,1,0:T(8,128)(2,1)}, bf16[2,1024,256]{2,1,0:T(8,128)(2,1)}, u32[]{:S(2)}, u32[]{:S(2)}) collective-permute-start(bf16[2,1024,256]{2,1,0:T(8,128)(2,1)} %collective-permute-done.15.refs_1_), channel_id=1, source_target_pairs={{4,0},{5,1},{6,2},{7,3},{8,12},{9,13},{10,14},{11,15},{20,16},{21,... | collective-permute-start | bytes 3145736 | tf_op jit(solution)/shard_map/ppermute | solution.py:185
  122.6 13.3 %shard_map.71 = (bf16[16,64,1024]{2,1,0:T(8,128)(2,1)}, bf16[16,64,1024]{2,1,0:T(8,128)(2,1)}) custom-call(bf16[32,128]{1,0:T(8,128)(2,1)} %pad_maximum_fusion.fields_ref, bf16[128,64,1024]{2,1,0:T(8,128)(2,1)} %chol_ref.5, bf16[2,1024,256]{2,1,0:T(8,128)(2,1)} %collective-permute-done.8.rest_0_.refs_1_, ...), custom_call_target="tpu_custom_call" | custom-call | flops 60000002048 | bytes 1 | tf_op jit(solution)/shard_map/pallas_call | solution.py:65
  135.9 5.0 %all-to-all-start.2 = ((bf16[16,64,1024]{2,1,0:T(8,128)(2,1)}), bf16[16,64,1024]{2,1,0:T(8,128)(2,1)}, u32[]{:S(2)}, u32[]{:S(2)}) async-start(bf16[16,64,1024]{2,1,0:T(8,128)(2,1)} %get-tuple-element.5), calls=%async_computation.2 | async-start | bytes 4194304 | tf_op jit(solution)/shard_map/all_to_all | solution.py:215
  140.9 3.5 %shard_map.74.refs_3_.refs_2_ = bf16[2,256,256]{2,1,0:T(8,128)(2,1)} custom-call(s32[2]{0:T(128)} %pad_add_fusion.scalars, bf16[4,4,64,1024]{3,2,1,0:T(8,128)(2,1)} %bitcast.9.pieces, bf16[2,1024,256]{2,1,0:T(8,128)(2,1)} %collective-permute-done.14.refs_0_, bf16[2,1024,256]{2,1,0:T(8,128)(2,1)} %collective-permute-done.15.refs_1_, ...), custom_call_target="tpu_custom_call" | custom-call | flops 15000000512 | bytes 1 | tf_op jit(solution)/shard_map/pallas_call | solution.py:118
  144.4 3.5 %shard_map.73.refs_2_.refs_1_ = bf16[2,256,256]{2,1,0:T(8,128)(2,1)} custom-call(s32[2]{0:T(128)} %pad_add_fusion.scalars, bf16[4,4,64,1024]{3,2,1,0:T(8,128)(2,1)} %bitcast.9.pieces, bf16[2,1024,256]{2,1,0:T(8,128)(2,1)} %collective-permute-done.12.rest_1_.refs_0_, bf16[2,1024,256]{2,1,0:T(8,128)(2,1)} %collective-permute-done.10.rest_0_.refs_1_, ...), custom_call_target="tpu_custom_call" | custom-call | flops 15000000512 | bytes 1 | tf_op jit(solution)/shard_map/pallas_call | solution.py:118
  147.9 5.5 %collective-permute-done.19.pieces = bf16[4,4,64,1024]{3,2,1,0:T(8,128)(2,1)} collective-permute-done((bf16[4,4,64,1024]{3,2,1,0:T(8,128)(2,1)S(1)}, bf16[4,4,64,1024]{3,2,1,0:T(8,128)(2,1)}, u32[]{:S(2)}, u32[]{:S(2)}) %collective-permute-start.19) | collective-permute-done | bytes 2097184 | tf_op jit(solution)/shard_map/ppermute | solution.py:185
  153.4 3.2 %shard_map.81.refs_7_ = bf16[2,256,256]{2,1,0:T(8,128)(2,1)} custom-call(s32[2]{0:T(128)} %pad_add_fusion.1.scalars, bf16[4,4,64,1024]{3,2,1,0:T(8,128)(2,1)} %collective-permute-done.19.pieces, bf16[2,1024,256]{2,1,0:T(8,128)(2,1)} %shard_map.70.refs_0_, bf16[2,256,256]{2,1,0:T(8,128)(2,1)} %shard_map.73.refs_2_.refs_1_, ...), custom_call_target="tpu_custom_call" | custom-call | flops 15000000512 | bytes 1 | tf_op jit(solution)/shard_map/pallas_call | solution.py:118
  156.5 3.2 %shard_map.78.refs_2_ = bf16[2,256,256]{2,1,0:T(8,128)(2,1)} custom-call(s32[2]{0:T(128)} %pad_add_fusion.1.scalars, bf16[4,4,64,1024]{3,2,1,0:T(8,128)(2,1)} %collective-permute-done.19.pieces, bf16[2,1024,256]{2,1,0:T(8,128)(2,1)} %shard_map.68.refs_0_, bf16[2,256,256]{2,1,0:T(8,128)(2,1)} %shard_map.73.refs_2_.refs_1_, ...), custom_call_target="tpu_custom_call" | custom-call | flops 15000000512 | bytes 1 | tf_op jit(solution)/shard_map/pallas_call | solution.py:118
  159.7 5.1 %all-to-all-done.2 = bf16[16,64,1024]{2,1,0:T(8,128)(2,1)} async-done(((bf16[16,64,1024]{2,1,0:T(8,128)(2,1)}), bf16[16,64,1024]{2,1,0:T(8,128)(2,1)}, u32[]{:S(2)}, u32[]{:S(2)}) %all-to-all-start.2) | async-done | bytes 2097184 | tf_op jit(solution)/shard_map/all_to_all | solution.py:215
  164.8 5.5 %all-to-all-start = ((bf16[16,64,1024]{2,1,0:T(8,128)(2,1)}), bf16[16,64,1024]{2,1,0:T(8,128)(2,1)S(1)}, u32[]{:S(2)}, u32[]{:S(2)}) async-start(bf16[16,64,1024]{2,1,0:T(8,128)(2,1)} %get-tuple-element.4.refs_2_), calls=%async_computation | async-start | bytes 4194304 | tf_op jit(solution)/shard_map/all_to_all | solution.py:215
  170.3 3.5 %shard_map.75 = bf16[2,256,256]{2,1,0:T(8,128)(2,1)} custom-call(s32[2]{0:T(128)} %pad_add_fusion.scalars, bf16[4,4,64,1024]{3,2,1,0:T(8,128)(2,1)} %bitcast.10.pieces, bf16[2,1024,256]{2,1,0:T(8,128)(2,1)} %collective-permute-done.11.rest_2_.refs_0_, bf16[2,1024,256]{2,1,0:T(8,128)(2,1)} %copy-done.8, bf16[2,256,256]{2,1,0:T(8,128)(2,1)} %shard_map.73.refs_2_.refs_1_, ...), custom_call_target="tpu_custom_call" | custom-call | flops 15000000512 | bytes 1 | tf_op jit(solution)/shard_map/pallas_call | solution.py:118
  173.8 3.5 %shard_map.82 = bf16[2,256,256]{2,1,0:T(8,128)(2,1)} custom-call(s32[2]{0:T(128)} %pad_add_fusion.scalars, bf16[4,4,64,1024]{3,2,1,0:T(8,128)(2,1)} %bitcast.10.pieces, bf16[2,1024,256]{2,1,0:T(8,128)(2,1)} %collective-permute-done.21.refs_0_, bf16[2,1024,256]{2,1,0:T(8,128)(2,1)} %collective-permute-done.8.rest_0_.refs_1_, ...), custom_call_target="tpu_custom_call" | custom-call | flops 15000000512 | bytes 1 | tf_op jit(solution)/shard_map/pallas_call | solution.py:118
  178.8 15.3 %all-to-all-done = bf16[16,64,1024]{2,1,0:T(8,128)(2,1)S(1)} async-done(((bf16[16,64,1024]{2,1,0:T(8,128)(2,1)}), bf16[16,64,1024]{2,1,0:T(8,128)(2,1)S(1)}, u32[]{:S(2)}, u32[]{:S(2)}) %all-to-all-start) | async-done | bytes 2097184 | tf_op jit(solution)/shard_map/all_to_all | solution.py:215
  195.5 3.2 %shard_map.79.refs_5_ = bf16[2,256,256]{2,1,0:T(8,128)(2,1)} custom-call(s32[2]{0:T(128)} %pad_add_fusion.scalars, bf16[4,4,64,1024]{3,2,1,0:T(8,128)(2,1)} %bitcast.21, bf16[2,1024,256]{2,1,0:T(8,128)(2,1)} %shard_map.70.refs_0_, bf16[2,256,256]{2,1,0:T(8,128)(2,1)} %copy-done.3, bf16[2,256,256]{2,1,0:T(8,128)(2,1)} %copy-done.2, bf16[2,256,256]{2,1,0:T(8,128)(2,1)} %copy-done.4), custom_call_target="tpu_custom_call" | custom-call | flops 15000000512 | bytes 1 | tf_op jit(solution)/shard_map/pallas_call | solution.py:118
  198.7 3.2 %shard_map.76.refs_0_ = bf16[2,256,256]{2,1,0:T(8,128)(2,1)} custom-call(s32[2]{0:T(128)} %pad_add_fusion.scalars, bf16[4,4,64,1024]{3,2,1,0:T(8,128)(2,1)} %bitcast.22, bf16[2,1024,256]{2,1,0:T(8,128)(2,1)} %shard_map.68.refs_0_, bf16[2,256,256]{2,1,0:T(8,128)(2,1)} %copy-done.3, bf16[2,256,256]{2,1,0:T(8,128)(2,1)} %copy-done.2, bf16[2,256,256]{2,1,0:T(8,128)(2,1)} %copy-done.4), custom_call_target="tpu_custom_call" | custom-call | flops 15000000512 | bytes 1 | tf_op jit(solution)/shard_map/pallas_call | solution.py:118
  202.6 3.5 %shard_map.83 = bf16[4,1024,256]{2,1,0:T(8,128)(2,1)} custom-call(s32[2]{0:T(128)} %pad_add_fusion.scalars, bf16[2,256,256]{2,1,0:T(8,128)(2,1)} %shard_map.76.refs_0_, bf16[2,256,256]{2,1,0:T(8,128)(2,1)} %collective-permute-done.18.refs_1_, bf16[2,256,256]{2,1,0:T(8,128)(2,1)} %shard_map.78.refs_2_, bf16[2,256,256]{2,1,0:T(8,128)(2,1)} %copy-done.3, ...), custom_call_target="tpu_custom_call" | custom-call | tf_op jit(solution)/shard_map/pallas_call | solution.py:155
  (67 shorter events, 30.7 us)
Async XLA Ops:
  0.6 6.9 %copy-start.7 = (bf16[64,64,256]{2,1,0:T(8,128)(2,1)S(1)}, bf16[64,64,256]{2,1,0:T(8,128)(2,1)}, u32[]{:S(2)}) copy-start(bf16[64,64,256]{2,1,0:T(8,128)(2,1)} %param.7) | copy-start | bytes 6291460
  2.9 29.7 %copy-start.6 = (f32[64,128]{1,0:T(8,128)S(1)}, f32[64,128]{1,0:T(8,128)}, u32[]{:S(2)}) copy-start(f32[64,128]{1,0:T(8,128)} %param.8) | copy-start | bytes 98308
  2.9 30.4 %collective-permute-start.6 = (bf16[2,1024,256]{2,1,0:T(8,128)(2,1)}, bf16[2,1024,256]{2,1,0:T(8,128)(2,1)}, u32[]{:S(2)}, u32[]{:S(2)}) collective-permute-start(bf16[2,1024,256]{2,1,0:T(8,128)(2,1)} %shard_map.68.refs_0_), channel_id=1, source_target_pairs={{0,4},{1,5},{2,6},{3,7},{12,8},{13,9},{14,10},{15,11},{16,20},{17,... | collective-permute-start | bytes 3145736 | tf_op jit(solution)/shard_map/ppermute | solution.py:185
  4.3 32.9 %collective-permute-start.7 = (bf16[2,1024,256]{2,1,0:T(8,128)(2,1)}, bf16[2,1024,256]{2,1,0:T(8,128)(2,1)S(1)}, u32[]{:S(2)}, u32[]{:S(2)}) collective-permute-start(bf16[2,1024,256]{2,1,0:T(8,128)(2,1)} %shard_map.68.refs_0_), channel_id=1, source_target_pairs={{4,8},{5,9},{6,10},{7,11},{8,4},{9,5},{10,6},{11,7},{20,24},{21,25... | collective-permute-start | bytes 3145736 | tf_op jit(solution)/shard_map/ppermute | solution.py:185
  16.4 2.7 %collective-permute-start = (f32[64,128]{1,0:T(8,128)S(1)}, f32[64,128]{1,0:T(8,128)S(1)}, u32[]{:S(2)}, u32[]{:S(2)}) collective-permute-start(f32[64,128]{1,0:T(8,128)S(1)} %fusion.3), channel_id=1, source_target_pairs={{0,1},{1,0},{2,3},{3,2},{4,5},{5,4},{6,7},{7,6},{8,9},{9,8},{10,11... | collective-permute-start | bytes 98312 | tf_op jit(solution)/shard_map/ppermute | solution.py:27
  17.4 3.2 %collective-permute-start.1 = (f32[64,128]{1,0:T(8,128)S(1)}, f32[64,128]{1,0:T(8,128)S(1)}, u32[]{:S(2)}, u32[]{:S(2)}) collective-permute-start(f32[64,128]{1,0:T(8,128)S(1)} %fusion.3), channel_id=1, source_target_pairs={{0,2},{1,3},{2,0},{3,1},{4,6},{5,7},{6,4},{7,5},{8,10},{9,11},{10,... | collective-permute-start | bytes 98312 | tf_op jit(solution)/shard_map/ppermute | solution.py:27
  17.6 4.1 %collective-permute-start.2 = (f32[64,128]{1,0:T(8,128)S(1)}, f32[64,128]{1,0:T(8,128)S(1)}, u32[]{:S(2)}, u32[]{:S(2)}) collective-permute-start(f32[64,128]{1,0:T(8,128)S(1)} %fusion.3), channel_id=1, source_target_pairs={{0,3},{1,2},{2,1},{3,0},{4,7},{5,6},{6,5},{7,4},{8,11},{9,10},{10,... | collective-permute-start | bytes 98312 | tf_op jit(solution)/shard_map/ppermute | solution.py:27
  21.7 8.2 %collective-permute-start.3 = (f32[64,128]{1,0:T(8,128)S(1)}, f32[64,128]{1,0:T(8,128)S(1)}, u32[]{:S(2)}, u32[]{:S(2)}) collective-permute-start(f32[64,128]{1,0:T(8,128)S(1)} %add_add_fusion), channel_id=1, source_target_pairs={{0,4},{1,5},{2,6},{3,7},{4,0},{5,1},{6,2},{7,3},{8,12},{9,13},{10,... | collective-permute-start | bytes 98312 | tf_op jit(solution)/shard_map/ppermute | solution.py:27
  22.0 9.2 %collective-permute-start.4 = (f32[64,128]{1,0:T(8,128)S(1)}, f32[64,128]{1,0:T(8,128)S(1)}, u32[]{:S(2)}, u32[]{:S(2)}) collective-permute-start(f32[64,128]{1,0:T(8,128)S(1)} %add_add_fusion), channel_id=1, source_target_pairs={{0,8},{1,9},{2,10},{3,11},{4,12},{5,13},{6,14},{7,15},{8,0},{9,1},... | collective-permute-start | bytes 98312 | tf_op jit(solution)/shard_map/ppermute | solution.py:27
  23.2 9.3 %collective-permute-start.5 = (f32[64,128]{1,0:T(8,128)S(1)}, f32[64,128]{1,0:T(8,128)S(1)}, u32[]{:S(2)}, u32[]{:S(2)}) collective-permute-start(f32[64,128]{1,0:T(8,128)S(1)} %add_add_fusion), channel_id=1, source_target_pairs={{0,12},{1,13},{2,14},{3,15},{4,8},{5,9},{6,10},{7,11},{8,4},{9,5},... | collective-permute-start | bytes 98312 | tf_op jit(solution)/shard_map/ppermute | solution.py:27
  33.3 35.1 %collective-permute-start.10 = (bf16[2,1024,256]{2,1,0:T(8,128)(2,1)}, bf16[2,1024,256]{2,1,0:T(8,128)(2,1)}, u32[]{:S(2)}, u32[]{:S(2)}) collective-permute-start(bf16[2,1024,256]{2,1,0:T(8,128)(2,1)} %collective-permute-done.6.rest_0_.refs_0_), channel_id=1, source_target_pairs={{4,8},{5,9},{6,10},{7,11},{8,4},{9,5},{10,6},{11,7},{20,24},{21,25... | collective-permute-start | bytes 3145736 | tf_op jit(solution)/shard_map/ppermute | solution.py:185
  50.3 31.2 %collective-permute-start.8 = (bf16[2,1024,256]{2,1,0:T(8,128)(2,1)}, bf16[2,1024,256]{2,1,0:T(8,128)(2,1)}, u32[]{:S(2)}, u32[]{:S(2)}) collective-permute-start(bf16[2,1024,256]{2,1,0:T(8,128)(2,1)} %shard_map.70.refs_0_), channel_id=1, source_target_pairs={{4,8},{5,9},{6,10},{7,11},{8,4},{9,5},{10,6},{11,7},{20,24},{21,25... | collective-permute-start | bytes 3145736 | tf_op jit(solution)/shard_map/ppermute | solution.py:185
  52.2 31.5 %collective-permute-start.9 = (bf16[2,1024,256]{2,1,0:T(8,128)(2,1)}, bf16[2,1024,256]{2,1,0:T(8,128)(2,1)}, u32[]{:S(2)}, u32[]{:S(2)}) collective-permute-start(bf16[2,1024,256]{2,1,0:T(8,128)(2,1)} %shard_map.70.refs_0_), channel_id=1, source_target_pairs={{0,4},{1,5},{2,6},{3,7},{12,8},{13,9},{14,10},{15,11},{16,20},{17,... | collective-permute-start | bytes 3145736 | tf_op jit(solution)/shard_map/ppermute | solution.py:185
  53.5 33.7 %collective-permute-start.12 = (bf16[2,1024,256]{2,1,0:T(8,128)(2,1)S(1)}, bf16[2,1024,256]{2,1,0:T(8,128)(2,1)}, u32[]{:S(2)}, u32[]{:S(2)}) collective-permute-start(bf16[2,1024,256]{2,1,0:T(8,128)(2,1)S(1)} %copy-done.9), channel_id=1, source_target_pairs={{4,0},{5,1},{6,2},{7,3},{8,12},{9,13},{10,14},{11,15},{20,16},{21,... | collective-permute-start | bytes 3145736 | tf_op jit(solution)/shard_map/ppermute | solution.py:185
  61.8 35.4 %all-to-all-start.3 = ((bf16[16,64,1024]{2,1,0:T(8,128)(2,1)}), bf16[16,64,1024]{2,1,0:T(8,128)(2,1)S(1)}, u32[]{:S(2)}, u32[]{:S(2)}) async-start(bf16[16,64,1024]{2,1,0:T(8,128)(2,1)} %shard_map.69.rest_0_), calls=%async_computation.3 | async-start | bytes 4194304 | tf_op jit(solution)/shard_map/all_to_all | solution.py:215
  68.4 49.8 %collective-permute-start.11 = (bf16[2,1024,256]{2,1,0:T(8,128)(2,1)}, bf16[2,1024,256]{2,1,0:T(8,128)(2,1)}, u32[]{:S(2)}, u32[]{:S(2)}) collective-permute-start(bf16[2,1024,256]{2,1,0:T(8,128)(2,1)} %collective-permute-done.10.rest_0_.refs_1_), channel_id=1, source_target_pairs={{4,0},{5,1},{6,2},{7,3},{8,12},{9,13},{10,14},{11,15},{20,16},{21,... | collective-permute-start | bytes 3145736 | tf_op jit(solution)/shard_map/ppermute | solution.py:185
  81.4 59.5 %collective-permute-start.14 = (bf16[2,1024,256]{2,1,0:T(8,128)(2,1)}, bf16[2,1024,256]{2,1,0:T(8,128)(2,1)}, u32[]{:S(2)}, u32[]{:S(2)}) collective-permute-start(bf16[2,1024,256]{2,1,0:T(8,128)(2,1)} %collective-permute-done.8.rest_0_.refs_1_), channel_id=1, source_target_pairs={{4,0},{5,1},{6,2},{7,3},{8,12},{9,13},{10,14},{11,15},{20,16},{21,... | collective-permute-start | bytes 3145736 | tf_op jit(solution)/shard_map/ppermute | solution.py:185
  83.7 36.4 %collective-permute-start.15 = (bf16[2,1024,256]{2,1,0:T(8,128)(2,1)}, bf16[2,1024,256]{2,1,0:T(8,128)(2,1)}, u32[]{:S(2)}, u32[]{:S(2)}) collective-permute-start(bf16[2,1024,256]{2,1,0:T(8,128)(2,1)} %collective-permute-done.9.rest_1_.refs_0_), channel_id=1, source_target_pairs={{4,8},{5,9},{6,10},{7,11},{8,4},{9,5},{10,6},{11,7},{20,24},{21,25... | collective-permute-start | bytes 3145736 | tf_op jit(solution)/shard_map/ppermute | solution.py:185
  97.2 7.3 %copy-start = (bf16[16,64,1024]{2,1,0:T(8,128)(2,1)}, bf16[16,64,1024]{2,1,0:T(8,128)(2,1)S(1)}, u32[]{:S(2)}) copy-start(bf16[16,64,1024]{2,1,0:T(8,128)(2,1)S(1)} %all-to-all-done.3) | copy-start | bytes 6291460
  97.2 38.7 %all-to-all-start.1 = ((bf16[16,64,1024]{2,1,0:T(8,128)(2,1)}), bf16[16,64,1024]{2,1,0:T(8,128)(2,1)}, u32[]{:S(2)}, u32[]{:S(2)}) async-start(bf16[16,64,1024]{2,1,0:T(8,128)(2,1)} %shard_map.72), calls=%async_computation.1 | async-start | bytes 4194304 | tf_op jit(solution)/shard_map/all_to_all | solution.py:215
  104.5 48.8 %collective-permute-start.19 = (bf16[4,4,64,1024]{3,2,1,0:T(8,128)(2,1)S(1)}, bf16[4,4,64,1024]{3,2,1,0:T(8,128)(2,1)}, u32[]{:S(2)}, u32[]{:S(2)}) collective-permute-start(bf16[4,4,64,1024]{3,2,1,0:T(8,128)(2,1)S(1)} %bitcast.18), channel_id=1, source_target_pairs={{0,4},{1,5},{2,6},{3,7},{12,8},{13,9},{14,10},{15,11},{16,20},{17,... | collective-permute-start | bytes 6291464 | tf_op jit(solution)/shard_map/ppermute | solution.py:185
  109.0 92.9 %collective-permute-start.20 = (bf16[2,256,256]{2,1,0:T(8,128)(2,1)}, bf16[2,256,256]{2,1,0:T(8,128)(2,1)}, u32[]{:S(2)}, u32[]{:S(2)}) collective-permute-start(bf16[2,256,256]{2,1,0:T(8,128)(2,1)} %shard_map.80), channel_id=1, source_target_pairs={{4,0},{5,1},{6,2},{7,3},{8,12},{9,13},{10,14},{11,15},{20,16},{21,... | collective-permute-start | bytes 786440 | tf_op jit(solution)/shard_map/ppermute | solution.py:185
  118.2 83.7 %collective-permute-start.18 = (bf16[2,256,256]{2,1,0:T(8,128)(2,1)}, bf16[2,256,256]{2,1,0:T(8,128)(2,1)}, u32[]{:S(2)}, u32[]{:S(2)}) collective-permute-start(bf16[2,256,256]{2,1,0:T(8,128)(2,1)} %shard_map.77), channel_id=1, source_target_pairs={{4,0},{5,1},{6,2},{7,3},{8,12},{9,13},{10,14},{11,15},{20,16},{21,... | collective-permute-start | bytes 786440 | tf_op jit(solution)/shard_map/ppermute | solution.py:185
  120.1 53.7 %collective-permute-start.21 = (bf16[2,1024,256]{2,1,0:T(8,128)(2,1)}, bf16[2,1024,256]{2,1,0:T(8,128)(2,1)}, u32[]{:S(2)}, u32[]{:S(2)}) collective-permute-start(bf16[2,1024,256]{2,1,0:T(8,128)(2,1)} %collective-permute-done.15.refs_1_), channel_id=1, source_target_pairs={{4,0},{5,1},{6,2},{7,3},{8,12},{9,13},{10,14},{11,15},{20,16},{21,... | collective-permute-start | bytes 3145736 | tf_op jit(solution)/shard_map/ppermute | solution.py:185
  135.9 28.9 %all-to-all-start.2 = ((bf16[16,64,1024]{2,1,0:T(8,128)(2,1)}), bf16[16,64,1024]{2,1,0:T(8,128)(2,1)}, u32[]{:S(2)}, u32[]{:S(2)}) async-start(bf16[16,64,1024]{2,1,0:T(8,128)(2,1)} %get-tuple-element.5), calls=%async_computation.2 | async-start | bytes 4194304 | tf_op jit(solution)/shard_map/all_to_all | solution.py:215
  144.4 32.9 %collective-permute-start.16 = (bf16[2,256,256]{2,1,0:T(8,128)(2,1)}, bf16[2,256,256]{2,1,0:T(8,128)(2,1)S(1)}, u32[]{:S(2)}, u32[]{:S(2)}) collective-permute-start(bf16[2,256,256]{2,1,0:T(8,128)(2,1)} %shard_map.74.refs_3_.refs_2_), channel_id=1, source_target_pairs={{0,8},{1,9},{2,10},{3,11},{8,0},{9,1},{10,2},{11,3},{4,12},{5,13},... | collective-permute-start | bytes 786440 | tf_op jit(solution)/shard_map/ppermute | solution.py:185
  153.4 25.5 %collective-permute-start.13 = (bf16[2,256,256]{2,1,0:T(8,128)(2,1)}, bf16[2,256,256]{2,1,0:T(8,128)(2,1)S(1)}, u32[]{:S(2)}, u32[]{:S(2)}) collective-permute-start(bf16[2,256,256]{2,1,0:T(8,128)(2,1)} %shard_map.73.refs_2_.refs_1_), channel_id=1, source_target_pairs={{0,8},{1,9},{2,10},{3,11},{8,0},{9,1},{10,2},{11,3},{4,12},{5,13},... | collective-permute-start | bytes 786440 | tf_op jit(solution)/shard_map/ppermute | solution.py:185
  164.8 29.3 %all-to-all-start = ((bf16[16,64,1024]{2,1,0:T(8,128)(2,1)}), bf16[16,64,1024]{2,1,0:T(8,128)(2,1)S(1)}, u32[]{:S(2)}, u32[]{:S(2)}) async-start(bf16[16,64,1024]{2,1,0:T(8,128)(2,1)} %get-tuple-element.4.refs_2_), calls=%async_computation | async-start | bytes 4194304 | tf_op jit(solution)/shard_map/all_to_all | solution.py:215
  173.8 20.3 %collective-permute-start.17 = (bf16[2,256,256]{2,1,0:T(8,128)(2,1)}, bf16[2,256,256]{2,1,0:T(8,128)(2,1)S(1)}, u32[]{:S(2)}, u32[]{:S(2)}) collective-permute-start(bf16[2,256,256]{2,1,0:T(8,128)(2,1)} %shard_map.75), channel_id=1, source_target_pairs={{0,12},{1,13},{2,14},{3,15},{12,0},{13,1},{14,2},{15,3},{4,8},{5,9... | collective-permute-start | bytes 786440 | tf_op jit(solution)/shard_map/ppermute | solution.py:185
  177.3 16.8 %copy-start.2 = (bf16[2,256,256]{2,1,0:T(8,128)(2,1)}, bf16[2,256,256]{2,1,0:T(8,128)(2,1)S(1)}, u32[]{:S(2)}) copy-start(bf16[2,256,256]{2,1,0:T(8,128)(2,1)S(1)} %collective-permute-done.16.refs_2_.refs_8_) | copy-start | bytes 786436
  177.3 24.5 %collective-permute-start.22 = (bf16[2,256,256]{2,1,0:T(8,128)(2,1)}, bf16[2,256,256]{2,1,0:T(8,128)(2,1)S(1)}, u32[]{:S(2)}, u32[]{:S(2)}) collective-permute-start(bf16[2,256,256]{2,1,0:T(8,128)(2,1)} %shard_map.82), channel_id=1, source_target_pairs={{0,12},{1,13},{2,14},{3,15},{12,0},{13,1},{14,2},{15,3},{4,8},{5,9... | collective-permute-start | bytes 786440 | tf_op jit(solution)/shard_map/ppermute | solution.py:185
  178.8 15.3 %copy-start.3 = (bf16[2,256,256]{2,1,0:T(8,128)(2,1)}, bf16[2,256,256]{2,1,0:T(8,128)(2,1)S(1)}, u32[]{:S(2)}) copy-start(bf16[2,256,256]{2,1,0:T(8,128)(2,1)S(1)} %collective-permute-done.13.refs_1_.refs_3_) | copy-start | bytes 786436
  (5 other events, 9.8 us)
